TPU v7x, 128 devices: a whole 4x4x4 slice. The times are simulated.
128 devices in a mesh: rep: 16 (over z, y_lo, core), dom: 8 (over y_hi, x).
Axes of the slice: x: 4, y: 4 (y_hi: 2, y_lo: 2; y = y_hi * 2 + y_lo), z: 4, core: 2. Of those that a mesh axis runs over, the one named last changes fastest.
Arguments:
- positions: float32 [16, 3, 524288], P('rep', None, 'dom'), may hold values from -6 to 6
- velocities: float32 [16, 3, 524288], P('rep', None, 'dom'), may hold values from -6 to 6
- charges: float32 [524288], P('dom'), may hold values from -5 to 5
- inv_mass: float32 [524288], P('dom'), may hold values from 0.05 to 1
- path_weight: float32 [524288], P('dom'), may hold values from -0.0078125 to 0.0078125
- halo_index: int32 [2, 131072], P(None, 'dom'), may hold values from 0 to 65535, as said below
- tile_pairs: int32 [4096, 2], P('dom'), may hold values from 0 to 767, as said below
- partner: int32 [16], P('rep'), may hold values from 0 to 15, as said below
- bias_center: float32 [16], P('rep'), may hold values from -1.5 to 1.5
- bias_spring: float32 [16], P('rep'), may hold values from 0.5 to 5
Outputs:
- new_positions: float32 [16, 3, 524288], P('rep', None, 'dom')
- new_velocities: float32 [16, 3, 524288], P('rep', None, 'dom')
- bias_energy: float32 [16], P('rep')
Inputs may be any that keep to these rules, and one draw needn't show every extreme that they name: partner[partner[w]] = w, and partner[w] differs from w by at most one. `halo_index`: within one domain's block the 32768 indices of both rows are different atoms of that domain. `tile_pairs`: entries name tiles of a domain's extended list (512 own tiles, then 128 from the domain below, then 128 from the domain above); the 2 entries of one row differ.
All inputs are finite; a program needn't handle non-finite values.
Results may differ from a plain program's by a relative error of at most 0.0001.
Values sent between devices are 32-bit elements; how exact they have to be, the bound alone decides.
A program may use at most 128 MiB of HBM per device.

v0:
```python
import math

import jax
import jax.numpy as jnp
from jax import lax
from jax.sharding import PartitionSpec as P

TILE = 128
STEPS = 2


time_step = 0.1


def passed_along(shard, axis, by):
    count = lax.axis_size(axis)
    return lax.ppermute(shard, axis, [(i, (i + by) % count) for i in range(count)])


def shifted(shard, axis, by):
    count = lax.axis_size(axis)
    pairs = [(i, i + by) for i in range(count) if 0 <= i + by < count]
    return lax.ppermute(shard, axis, pairs)


def tile_forces(extended, pairs):
    tile_count = pairs.shape[0]
    neighbours = pairs.shape[1]
    group_size = math.gcd(tile_count, 16)
    tiles_major = extended.reshape(4, extended.shape[1] // TILE, TILE).transpose(1, 0, 2)
    nearby_all = jnp.take(tiles_major, pairs.reshape(-1), axis=0)
    nearby_all = nearby_all.reshape(tile_count, neighbours, 4, TILE).transpose(0, 2, 1, 3)
    nearby_all = nearby_all.reshape(tile_count // group_size, group_size, 4, neighbours * TILE)
    own_tiles = tiles_major[:tile_count].reshape(tile_count // group_size, group_size, 4, TILE)

    def one_block(block_item):
        own_block, nearby = block_item
        offset = own_block[:, :3, :, None] - nearby[:, :3, None, :]
        spread = jnp.sum(offset * offset, axis=1) + 1.0
        weight = own_block[:, 3, :, None] * nearby[:, 3, None, :] / (spread * spread)
        return jnp.sum(offset * weight[:, None], axis=-1)

    result = lax.map(one_block, (own_tiles, nearby_all))
    return result.reshape(tile_count, 3, TILE).transpose(1, 0, 2).reshape(3, tile_count * TILE)


def ghost_layer(atom_state, halo_index):
    send_down = atom_state[:, halo_index[0]]
    send_up = atom_state[:, halo_index[1]]
    from_lower = passed_along(send_up, "dom", 1)
    from_upper = passed_along(send_down, "dom", -1)
    return jnp.concatenate([from_lower, from_upper], axis=1)


def path_value(position, path_weight):
    return lax.psum(jnp.sum(path_weight * position[2]), "dom")


def choose_state(own_value, from_below, from_above, partner_now, window):
    return jnp.where(
        partner_now == window - 1,
        from_below,
        jnp.where(partner_now == window + 1, from_above, own_value),
    )


def body(
    positions,
    velocities,
    charges,
    inv_mass,
    path_weight,
    halo_index,
    tile_pairs,
    partner,
    bias_center,
    bias_spring,
):
    position = positions[0]
    velocity = velocities[0]
    partner_now = partner[0]
    window = lax.axis_index("rep")
    carried = None
    from_below = shifted((position, velocity), "rep", 1)
    from_above = shifted((position, velocity), "rep", -1)
    position = choose_state(position, from_below[0], from_above[0], partner_now, window)
    velocity = choose_state(velocity, from_below[1], from_above[1], partner_now, window)
    center = bias_center[0]
    spring = bias_spring[0]
    for step_index in range(STEPS):
        atom_state = jnp.concatenate([position, charges[None]], axis=0)
        ghosts = ghost_layer(atom_state, halo_index)
        extended = jnp.concatenate([atom_state, ghosts], axis=1)
        forces = tile_forces(extended, tile_pairs)
        progress = path_value(position, path_weight)
        forces = forces.at[2].add(-spring * (progress - center) * path_weight)
        velocity = velocity + time_step * inv_mass * forces
        position = position + time_step * velocity
    progress = path_value(position, path_weight)
    energy = 0.5 * spring * (progress - center) ** 2
    return (position[None], velocity[None], energy[None])


def solution(mesh):
    in_specs = (
        P("rep", None, "dom"),
        P("rep", None, "dom"),
        P("dom"),
        P("dom"),
        P("dom"),
        P(None, "dom"),
        P("dom", None),
        P("rep"),
        P("rep"),
        P("rep"),
    )
    out_specs = (P("rep", None, "dom"), P("rep", None, "dom"), P("rep"))
    return jax.shard_map(body, mesh=mesh, in_specs=in_specs, out_specs=out_specs, check_vma=False)
```

profile of v0, /device:TPU:96, one launch (start us, length us, event | category | flops | bytes accessed | tf_op | source)
XLA Modules:
  0.0 828.2 jit_solution(18405915107891485313)
XLA Ops:
  4.5 4.5 collective-permute-start.1
  21.1 6.9 collective-permute-done
  28.0 4.6 collective-permute-done.1
  33.9 16.1 %copy.93 = f32[4,65536]{0,1:T(8,128)} copy(f32[4,65536]{1,0:T(4,128)S(1)} %pad_maximum_fusion.3) | data formatting | bytes 2097152 | tf_op jit(solution)/shard_map/concatenate | solution.py:91
  50.0 65.0 %gather_fusion = f32[16384,4]{1,0:T(8,128)} fusion(f32[4,65536]{0,1:T(8,128)} %copy.93, s32[16384]{0:T(1024)S(1)} %broadcast_clamp_fusion.1), kind=kCustom, calls=%fused_computation.2 | custom fusion | bytes 589824 | tf_op jit(solution)/shard_map/gather | solution.py:49
  115.1 5.4 copy.94
  122.1 65.0 %gather_fusion.1 = f32[16384,4]{1,0:T(8,128)} fusion(f32[4,65536]{0,1:T(8,128)} %copy.93, s32[16384]{0:T(1024)S(1)} %broadcast_clamp_fusion), kind=kCustom, calls=%fused_computation.3 | custom fusion | bytes 589824 | tf_op jit(solution)/shard_map/gather | solution.py:48
  187.1 5.5 copy.96
  197.8 21.5 %psum.21 = f32[]{:T(128)} all-reduce(f32[]{:T(128)} %multiply_reduce_fusion.2), channel_id=1, replica_groups=mesh['rep'=16,'dom'=8] {'dom'}, use_global_device_ids=true, to_apply=%region_5.7 | all-reduce | flops 1 | bytes 8 | tf_op jit(solution)/shard_map/psum | solution.py:56
  222.3 7.9 gather_fusion.4
  230.2 5.5 broadcast_select_fusion.1
  243.1 163.1 %while.22 = (s32[]{:T(128)}, f32[32,16,3,128]{3,1,0,2:T(8,128)}, f32[32,16,4,128]{3,2,1,0:T(4,128)S(1)}, f32[32,16,4,256]{3,1,0,2:T(8,128)}, s32[]{:T(128)}) while((s32[]{:T(128)}, f32[32,16,3,128]{3,1,0,2:T(8,128)}, f32[32,16,4,128]{3,2,1,0:T(4,128)S(1)}, f32[32,16,4,256]{3,1,0,2:T(8,128)}, s32[]{:T(128)}) %tuple.64), condition=%wide.region_3.5_spmd, body=%wide.region_0.4_spmd.sunk | while | flops 11003906 | bytes 9241157 | solution.py:43
  408.9 4.6 scatter-add.6
  419.5 16.4 %copy.102 = f32[4,65536]{0,1:T(8,128)} copy(f32[4,65536]{1,0:T(4,128)} %pad_maximum_fusion.2) | data formatting | bytes 2097152 | tf_op jit(solution)/shard_map/concatenate | solution.py:91
  435.9 65.0 %gather_fusion.2 = f32[16384,4]{1,0:T(8,128)} fusion(f32[4,65536]{0,1:T(8,128)} %copy.102, s32[16384]{0:T(1024)S(1)} %broadcast_clamp_fusion.1), kind=kCustom, calls=%fused_computation.4 | custom fusion | bytes 589824 | tf_op jit(solution)/shard_map/gather | solution.py:49
  500.9 65.0 %gather_fusion.3 = f32[16384,4]{1,0:T(8,128)} fusion(f32[4,65536]{0,1:T(8,128)} %copy.102, s32[16384]{0:T(1024)S(1)} %broadcast_clamp_fusion), kind=kCustom, calls=%fused_computation.5 | custom fusion | bytes 589824 | tf_op jit(solution)/shard_map/gather | solution.py:48
  565.9 5.4 copy.103
  571.7 5.9 copy.105
  577.6 5.4 collective-permute-start.7
  583.9 20.3 %psum.22 = f32[]{:T(128)} all-reduce(f32[]{:T(128)} %multiply_reduce_fusion.1), channel_id=1, replica_groups=mesh['rep'=16,'dom'=8] {'dom'}, use_global_device_ids=true, to_apply=%region_11.13 | all-reduce | flops 1 | bytes 8 | tf_op jit(solution)/shard_map/psum | solution.py:56
  606.8 7.9 gather_fusion.5
  627.4 163.1 %while.23 = (s32[]{:T(128)}, f32[32,16,3,128]{3,1,0,2:T(8,128)}, f32[32,16,4,128]{3,2,1,0:T(4,128)S(1)}, f32[32,16,4,256]{3,1,0,2:T(8,128)}, s32[]{:T(128)}) while((s32[]{:T(128)}, f32[32,16,3,128]{3,1,0,2:T(8,128)}, f32[32,16,4,128]{3,2,1,0:T(4,128)S(1)}, f32[32,16,4,256]{3,1,0,2:T(8,128)}, s32[]{:T(128)}) %tuple.63), condition=%wide.region_9.11_spmd, body=%wide.region_6.10_spmd.sunk | while | flops 11003906 | bytes 9241157 | solution.py:43
  793.2 4.6 scatter-add.9
  805.3 21.1 %psum.23 = f32[]{:T(128)} all-reduce(f32[]{:T(128)} %multiply_reduce_fusion), channel_id=1, replica_groups=mesh['rep'=16,'dom'=8] {'dom'}, use_global_device_ids=true, to_apply=%region_13.15 | all-reduce | flops 1 | bytes 8 | tf_op jit(solution)/shard_map/psum | solution.py:56
  (912 shorter events, 387.8 us)
Async XLA Ops:
  0.6 8.4 %copy-start.9 = (f32[1,3,65536]{2,0,1:T(1,128)S(1)}, f32[1,3,65536]{2,0,1:T(1,128)}, u32[]{:S(2)}) copy-start(f32[1,3,65536]{2,0,1:T(1,128)} %param.21) | copy-start | bytes 2359300
  0.6 16.4 %copy-start.12 = (s32[2,16384]{1,0:T(2,128)S(1)}, s32[2,16384]{1,0:T(2,128)}, u32[]{:S(2)}) copy-start(s32[2,16384]{1,0:T(2,128)} %param.25) | copy-start | bytes 393220
  0.7 17.2 %copy-start.10 = (f32[65536]{0:T(1024)S(1)}, f32[65536]{0:T(1024)}, u32[]{:S(2)}) copy-start(f32[65536]{0:T(1024)} %param.23) | copy-start | bytes 786436
  0.7 17.9 %copy-start.13 = (s32[512,2]{0,1:T(2,128)S(1)}, s32[512,2]{0,1:T(2,128)}, u32[]{:S(2)}) copy-start(s32[512,2]{0,1:T(2,128)} %param.26) | copy-start | bytes 12292
  2.4 30.2 %copy-start.8 = (f32[1,3,65536]{2,0,1:T(1,128)S(1)}, f32[1,3,65536]{2,0,1:T(1,128)}, u32[]{:S(2)}) copy-start(f32[1,3,65536]{2,0,1:T(1,128)} %param.20) | copy-start | bytes 2359300
  2.5 25.6 %collective-permute-start = (f32[3,65536]{1,0:T(4,128)S(1)}, f32[3,65536]{1,0:T(4,128)S(1)}, u32[]{:S(2)}, u32[]{:S(2)}) collective-permute-start(f32[3,65536]{1,0:T(4,128)S(1)} %bitcast.151), channel_id=1, source_target_pairs={{0,8},{8,16},{16,24},{24,32},{32,40},{40,48},{48,56},{56,64},{64,7... | collective-permute-start | bytes 2359304 | tf_op jit(solution)/shard_map/ppermute | solution.py:23
  4.5 28.1 %collective-permute-start.1 = (f32[3,65536]{1,0:T(4,128)S(1)}, f32[3,65536]{1,0:T(4,128)}, u32[]{:S(2)}, u32[]{:S(2)}) collective-permute-start(f32[3,65536]{1,0:T(4,128)S(1)} %bitcast.152), channel_id=1, source_target_pairs={{8,0},{16,8},{24,16},{32,24},{40,32},{48,40},{56,48},{64,56},{72,6... | collective-permute-start | bytes 2359304 | tf_op jit(solution)/shard_map/ppermute | solution.py:23
  10.6 402.8 %collective-permute-start.2 = (f32[3,65536]{1,0:T(4,128)}, f32[3,65536]{1,0:T(4,128)}, u32[]{:S(2)}, u32[]{:S(2)}) collective-permute-start(f32[3,65536]{1,0:T(4,128)} %bitcast.101), channel_id=1, source_target_pairs={{0,8},{8,16},{16,24},{24,32},{32,40},{40,48},{48,56},{56,64},{64,7... | collective-permute-start | bytes 2359304 | tf_op jit(solution)/shard_map/ppermute | solution.py:23
  12.5 401.9 %collective-permute-start.3 = (f32[3,65536]{1,0:T(4,128)}, f32[3,65536]{1,0:T(4,128)}, u32[]{:S(2)}, u32[]{:S(2)}) collective-permute-start(f32[3,65536]{1,0:T(4,128)} %bitcast.101), channel_id=1, source_target_pairs={{8,0},{16,8},{24,16},{32,24},{40,32},{48,40},{56,48},{64,56},{72,6... | collective-permute-start | bytes 2359304 | tf_op jit(solution)/shard_map/ppermute | solution.py:23
  18.9 14.5 %copy-start.7 = (f32[65536]{0:T(1024)S(1)}, f32[65536]{0:T(1024)}, u32[]{:S(2)}) copy-start(f32[65536]{0:T(1024)} %param.22) | copy-start | bytes 786436
  120.5 99.5 %collective-permute-start.4 = (f32[4,16384]{1,0:T(4,128)S(1)}, f32[4,16384]{1,0:T(4,128)S(1)}, u32[]{:S(2)}, u32[]{:S(2)}) collective-permute-start(f32[4,16384]{1,0:T(4,128)S(1)} %copy.94), channel_id=1, source_target_pairs={{0,1},{1,2},{2,3},{3,4},{4,5},{5,6},{6,7},{7,0},{8,9},{9,10},{10,1... | collective-permute-start | bytes 786440 | tf_op jit(solution)/shard_map/ppermute | solution.py:17
  187.1 10.0 %copy-start.4 = (f32[65536]{0:T(1024)S(1)}, f32[65536]{0:T(1024)}, u32[]{:S(2)}) copy-start(f32[65536]{0:T(1024)} %param.24) | copy-start | bytes 786436
  192.6 28.1 %collective-permute-start.5 = (f32[4,16384]{1,0:T(4,128)S(1)}, f32[4,16384]{1,0:T(4,128)}, u32[]{:S(2)}, u32[]{:S(2)}) collective-permute-start(f32[4,16384]{1,0:T(4,128)S(1)} %copy.96), channel_id=1, source_target_pairs={{0,7},{1,0},{2,1},{3,2},{4,3},{5,4},{6,5},{7,6},{8,15},{9,8},{10,9... | collective-permute-start | bytes 786440 | tf_op jit(solution)/shard_map/ppermute | solution.py:17
  220.0 0.7 copy-start.11
  222.3 7.9 copy-start.1
  238.1 5.0 slice-start.1
  413.5 1.0 copy-start.6
  418.1 164.9 %copy-start.2 = (f32[3,65536]{1,0:T(4,128)}, f32[3,65536]{1,0:T(4,128)S(1)}, u32[]{:S(2)}) copy-start(f32[3,65536]{1,0:T(4,128)S(1)} %get-tuple-element.124) | copy-start | bytes 2359300
  571.4 33.4 %collective-permute-start.6 = (f32[4,16384]{1,0:T(4,128)S(1)}, f32[4,16384]{1,0:T(4,128)}, u32[]{:S(2)}, u32[]{:S(2)}) collective-permute-start(f32[4,16384]{1,0:T(4,128)S(1)} %copy.103), channel_id=1, source_target_pairs={{0,1},{1,2},{2,3},{3,4},{4,5},{5,6},{6,7},{7,0},{8,9},{9,10},{10,1... | collective-permute-start | bytes 786440 | tf_op jit(solution)/shard_map/ppermute | solution.py:17
  577.6 27.2 %collective-permute-start.7 = (f32[4,16384]{1,0:T(4,128)}, f32[4,16384]{1,0:T(4,128)}, u32[]{:S(2)}, u32[]{:S(2)}) collective-permute-start(f32[4,16384]{1,0:T(4,128)} %copy.105), channel_id=1, source_target_pairs={{0,7},{1,0},{2,1},{3,2},{4,3},{5,4},{6,5},{7,6},{8,15},{9,8},{10,9... | collective-permute-start | bytes 786440 | tf_op jit(solution)/shard_map/ppermute | solution.py:17
  606.8 7.9 copy-start
  614.7 1.6 copy-start.3
  622.4 5.0 slice-start
  797.8 1.0 copy-start.5
where the time goes:
time: 834 us; the launch traced here: 828 us
  local copies, waits for them, and re-layouts  469 us (56%)
  other arithmetic  249 us (30%)
  blocking collectives  62.9 us (8%)
  starting transfers between devices  24.5 us (3%)
  waiting for transfers between devices  11.5 us (1%)
    gather x4, local copies, waits for them, and re-layouts, ghost_layer(): send_down = atom_state[:, halo_index[0]]  141 us
    gather x4, local copies, waits for them, and re-layouts, ghost_layer(): send_up = atom_state[:, halo_index[1]]  141 us
    reduce_sum x64, other arithmetic, one_block(): return jnp.sum(offset * weight[:, None], axis=-1)  119 us
    reduce_sum x64, other arithmetic, one_block(): spread = jnp.sum(offset * offset, axis=1) + 1.0  74.2 us
    psum x3, blocking collectives, path_value(): return lax.psum(jnp.sum(path_weight * position[2]), 'dom')  62.9 us
    squeeze x64, local copies, waits for them, and re-layouts, tile_forces(): result = lax.map(one_block, (own_tiles, nearby_all))  54.1 us
    dynamic_update_slice x64, local copies, waits for them, and re-layouts, tile_forces(): result = lax.map(one_block, (own_tiles, nearby_all))  39.7 us
    concatenate x2, local copies, waits for them, and re-layouts, body(): atom_state = jnp.concatenate([position, charges[None]], axis=0)  32.5 us
  transfers between devices with their start and end apart: 8, of which 2 were waited for; matrix products, arithmetic and copies ran while one was open for 43% of the time, Pallas kernels for 0%

commit v1 on v0

v1 whole, which is shorter than its diff:
```python
import jax
import jax.numpy as jnp
from jax import lax
from jax.experimental import pallas as pl
from jax.experimental.pallas import tpu as pltpu
from jax.sharding import PartitionSpec as P

LANES = 128
STEPS = 2
TILES = 512
GHOST_ROWS = 256
GROUPS = 16
GROUP_ROWS = 32
CELLS = 32
TILES_AT_ONCE = 8
time_step = 0.1
f32 = jnp.float32
bf16 = jnp.bfloat16
VMEM = pl.BlockSpec(memory_space=pltpu.VMEM)
SMEM = pl.BlockSpec(memory_space=pltpu.SMEM)


def params():
    return pltpu.CompilerParams(vmem_limit_bytes=58 * 1024 * 1024)


def plan_halo(halo_index):
    index = halo_index.reshape(-1)
    count = index.shape[0]
    slot = lax.iota(jnp.int32, count)
    key = ((index >> 12) << 27) | (slot << 12) | (index & 4095)
    (key,) = lax.sort((key,), num_keys=1, is_stable=False)
    group = key >> 27
    source = (group << 12) | (key & 4095)
    back = (((key >> 12) & (count - 1)) << 15) | slot
    (back,) = lax.sort((back,), num_keys=1, is_stable=False)
    place = back & (count - 1)
    block_group = (index >> 12).reshape(CELLS, count // CELLS)
    counts = jnp.sum(
        (block_group[None] == lax.iota(jnp.int32, GROUPS)[:, None, None]).astype(jnp.int32), axis=2
    ).reshape(-1)
    cells = GROUPS * CELLS
    before = (lax.iota(jnp.int32, cells)[:, None] > lax.iota(jnp.int32, cells)[None, :]).astype(jnp.int32)
    starts = jnp.sum(before * counts[None, :], axis=1)
    first_row = jnp.minimum(starts >> 7, GHOST_ROWS - 1)
    last_row = jnp.maximum(starts + counts - 1, starts) >> 7
    last_row = jnp.minimum(last_row, GHOST_ROWS - 1)
    ranges = group.reshape(GHOST_ROWS // 8, 1024)
    return (
        source.reshape(GHOST_ROWS, LANES),
        place.reshape(GHOST_ROWS, LANES),
        jnp.stack([ranges[:, 0], ranges[:, -1]]),
        jnp.stack([first_row, last_row]),
    )


def gather_stages(comps, read_row, source, place, span, cell_rows, listed, out):
    def list_block(v, carry):
        base = pl.multiple_of(v * 8, 8)
        src = source[pl.ds(base, 8), :]
        lane = src & 127
        row = src >> 7

        def one_group(group, accs):
            first = pl.multiple_of(group * GROUP_ROWS, GROUP_ROWS)
            accs = list(accs)
            for u in range(GROUP_ROWS):
                here = row == first + u
                for c in range(comps):
                    line = jnp.broadcast_to(read_row(c, first + u), (8, LANES))
                    accs[c] = jnp.where(here, jnp.take_along_axis(line, lane, axis=1), accs[c])
            return tuple(accs)

        zero = jnp.zeros((8, LANES), f32)
        accs = lax.fori_loop(span[0, v], span[1, v] + 1, one_group, (zero,) * comps)
        for c in range(comps):
            listed[c, pl.ds(base, 8), :] = accs[c]
        return carry

    lax.fori_loop(0, GHOST_ROWS // 8, list_block, 0)

    def slot_block(t, carry):
        base = pl.multiple_of(t * 8, 8)
        at = place[pl.ds(base, 8), :]
        lane = at & 127
        row = at >> 7

        def visit(r, accs):
            here = row == r
            return tuple(
                jnp.where(
                    here,
                    jnp.take_along_axis(jnp.broadcast_to(listed[c, pl.ds(r, 1), :], (8, LANES)), lane, axis=1),
                    accs[c],
                )
                for c in range(comps)
            )

        accs = (jnp.zeros((8, LANES), f32),) * comps
        widest = 0
        for g in range(GROUPS):
            first = cell_rows[0, g * CELLS + t]
            last = cell_rows[1, g * CELLS + t]
            accs = visit(first, accs)
            accs = visit(last, accs)
            widest = jnp.maximum(widest, last - first)
        for c in range(comps):
            out[c, pl.ds(base, 8), :] = accs[c]

        @pl.when(widest > 1)
        def _():
            def rest(g, accs):
                return lax.fori_loop(cell_rows[0, g * CELLS + t], cell_rows[1, g * CELLS + t] + 1, visit, accs)

            more = lax.fori_loop(0, GROUPS, rest, tuple(out[c, pl.ds(base, 8), :] for c in range(comps)))
            for c in range(comps):
                out[c, pl.ds(base, 8), :] = more[c]

        return carry

    lax.fori_loop(0, GHOST_ROWS // 8, slot_block, 0)


def first_gather_kernel(position, charges, path_weight, source, place, span, cell_rows, ghosts, partial, listed):
    def read_row(c, r):
        if c == 3:
            return charges[pl.ds(r, 1), :]
        return position[c, pl.ds(r, 1), :]

    partial[...] = jnp.sum((path_weight[...] * position[2]).reshape(64, 8, LANES), axis=0)
    gather_stages(4, read_row, source, place, span, cell_rows, listed, ghosts)


def first_gather(position, charges, path_weight, plan):
    return pl.pallas_call(
        first_gather_kernel,
        out_shape=(
            jax.ShapeDtypeStruct((4, GHOST_ROWS, LANES), f32),
            jax.ShapeDtypeStruct((8, LANES), f32),
        ),
        in_specs=[VMEM] * 5 + [SMEM] * 2,
        out_specs=(VMEM, VMEM),
        scratch_shapes=[pltpu.VMEM((4, GHOST_ROWS, LANES), f32)],
        compiler_params=params(),
        name="first_gather",
    )(position, charges, path_weight, *plan)


def parts3(value):
    high = value.astype(bf16).astype(f32)
    rest = value - high
    middle = rest.astype(bf16).astype(f32)
    return high, middle, rest - middle


def force_kernel(pairs, position, charges, lower, upper, lower_q, upper_q, force, rows_j, rows_i, rows_a, feat_j, feat_i, feat_a, sums):
    zero8 = jnp.zeros((8, LANES), f32)
    one8 = jnp.ones((8, LANES), f32)
    for f in (13, 14, 15):
        rows_j[pl.ds(f, 8, stride=16), :] = zero8
    rows_j[pl.ds(12, 8, stride=16), :] = one8
    for f in (12, 13, 14, 15):
        rows_a[pl.ds(f, 8, stride=16), :] = zero8
    rows_i[...] = jnp.zeros_like(rows_i)
    for f in (9, 10, 11):
        rows_i[pl.ds(f, 8, stride=48), :] = one8

    def build(first_tile, x, y, z, q, own):
        norm = x * x + y * y + z * z
        split = [parts3(value) for value in (x, y, z)]
        for c in range(3):
            for s in range(3):
                rows_j[pl.ds(3 * s + c, 8, stride=16), :] = split[c][s]
        for s, value in enumerate(parts3(norm)):
            rows_j[pl.ds(9 + s, 8, stride=16), :] = value
        for k, value in enumerate((q, q * x, q * y, q * z)):
            for s, piece in enumerate(parts3(value)):
                rows_a[pl.ds(4 * s + k, 8, stride=16), :] = piece
        for n in range(8):
            feat_j[first_tile + n] = rows_j[16 * n : 16 * n + 16, :].astype(bf16)
            feat_a[first_tile + n] = rows_a[16 * n : 16 * n + 16, :].astype(bf16)
        if own:
            for c in range(3):
                for s in range(3):
                    value = -2.0 * split[c][s]
                    for j in range(3 - s):
                        rows_i[pl.ds(16 * s + 3 * j + c, 8, stride=48), :] = value
            for s, value in enumerate(parts3(norm + 1.0)):
                rows_i[pl.ds(16 * s + 12, 8, stride=48), :] = value
            for n in range(8):
                feat_i[first_tile + n] = rows_i[48 * n : 48 * n + 48, :].astype(bf16)

    def own_block(b, carry):
        base = pl.multiple_of(b * 8, 8)
        here = pl.ds(base, 8)
        build(base, position[0, here, :], position[1, here, :], position[2, here, :], charges[here, :], True)
        return carry

    lax.fori_loop(0, TILES // 8, own_block, 0)

    def ghost_block(values, charge, offset):
        def block(b, carry):
            base = pl.multiple_of(b * 8, 8)
            here = pl.ds(base, 8)
            build(offset + base, values[0, here, :], values[1, here, :], values[2, here, :], charge[here, :], False)
            return carry

        return block

    lax.fori_loop(0, 16, ghost_block(lower, lower_q, TILES), 0)
    lax.fori_loop(0, 16, ghost_block(upper, upper_q, TILES + 128), 0)

    def contract(a, b, left, right):
        return lax.dot_general(a, b, (((left,), (right,)), ((), ())), preferred_element_type=f32)

    def tiles(n, carry):
        found = []
        for u in range(TILES_AT_ONCE):
            tile = n * TILES_AT_ONCE + u
            one, two = pairs[2 * tile], pairs[2 * tile + 1]
            near = jnp.concatenate([feat_j[one], feat_j[two]], axis=1)
            spread = contract(jnp.concatenate([near] * 3, axis=0), feat_i[tile], 0, 0)
            found.append((tile, one, two, spread))
        done = []
        for tile, one, two, spread in found:
            weight = pl.reciprocal(spread * spread, approx=True)
            high = weight.astype(bf16)
            low = (weight - high.astype(f32)).astype(bf16)
            near = jnp.concatenate([feat_a[one], feat_a[two]], axis=1)
            done.append(
                (
                    tile,
                    contract(
                        jnp.concatenate([near, near], axis=1), jnp.concatenate([high, low], axis=0), 1, 0
                    ),
                )
            )
        for tile, value in done:
            sums[pl.ds(pl.multiple_of(tile * 16, 16), 16), :] = value
        return carry

    lax.fori_loop(0, TILES // TILES_AT_ONCE, tiles, 0)

    def combine(b, carry):
        base = pl.multiple_of(b * 8, 8)
        here = pl.ds(base, 8)
        total = []
        for k in range(4):
            value = sums[pl.ds(base * 16 + k, 8, stride=16), :]
            value = value + sums[pl.ds(base * 16 + 4 + k, 8, stride=16), :]
            value = value + sums[pl.ds(base * 16 + 8 + k, 8, stride=16), :]
            total.append(value)
        q = charges[here, :]
        for c in range(3):
            force[c, here, :] = q * (position[c, here, :] * total[0] - total[c + 1])
        return carry

    lax.fori_loop(0, TILES // 8, combine, 0)


def pair_forces(pairs, position, charges, lower, upper, lower_q, upper_q):
    return pl.pallas_call(
        force_kernel,
        out_shape=jax.ShapeDtypeStruct((3, TILES, LANES), f32),
        in_specs=[SMEM] + [VMEM] * 6,
        out_specs=VMEM,
        scratch_shapes=[
            pltpu.VMEM((8 * 16, LANES), f32),
            pltpu.VMEM((8 * 48, LANES), f32),
            pltpu.VMEM((8 * 16, LANES), f32),
            pltpu.VMEM((TILES + 256, 16, LANES), bf16),
            pltpu.VMEM((TILES, 48, LANES), bf16),
            pltpu.VMEM((TILES + 256, 16, LANES), bf16),
            pltpu.VMEM((TILES * 16, LANES), f32),
        ],
        compiler_params=params(),
        name="pair_forces",
    )(pairs, position, charges, lower, upper, lower_q, upper_q)


def advance(scalars, position, velocity, force, inv_mass, path_weight, new_position, new_velocity):
    weight = path_weight[...]
    rate = time_step * inv_mass[...]
    pull = scalars[0] * (scalars[1] - scalars[2])
    for c in range(3):
        total = force[c]
        if c == 2:
            total = total - pull * weight
        moved = velocity[c] + rate * total
        new_velocity[c] = moved
        new_position[c] = position[c] + time_step * moved
    return jnp.sum((weight * new_position[2]).reshape(64, 8, LANES), axis=0)


def middle_kernel(
    scalars, position, velocity, force, inv_mass, path_weight, source, place, span, cell_rows,
    new_position, new_velocity, ghosts, partial, listed,
):
    partial[...] = advance(scalars, position, velocity, force, inv_mass, path_weight, new_position, new_velocity)

    def read_row(c, r):
        return new_position[c, pl.ds(r, 1), :]

    gather_stages(3, read_row, source, place, span, cell_rows, listed, ghosts)


def last_kernel(scalars, position, velocity, force, inv_mass, path_weight, new_position, new_velocity, partial):
    partial[...] = advance(scalars, position, velocity, force, inv_mass, path_weight, new_position, new_velocity)


def middle_update(scalars, position, velocity, force, inv_mass, path_weight, plan):
    whole = jax.ShapeDtypeStruct((3, TILES, LANES), f32)
    return pl.pallas_call(
        middle_kernel,
        out_shape=(
            whole,
            whole,
            jax.ShapeDtypeStruct((3, GHOST_ROWS, LANES), f32),
            jax.ShapeDtypeStruct((8, LANES), f32),
        ),
        in_specs=[SMEM] + [VMEM] * 7 + [SMEM] * 2,
        out_specs=(VMEM,) * 4,
        scratch_shapes=[pltpu.VMEM((3, GHOST_ROWS, LANES), f32)],
        compiler_params=params(),
        name="middle_update",
    )(scalars, position, velocity, force, inv_mass, path_weight, *plan)


def last_update(scalars, position, velocity, force, inv_mass, path_weight):
    whole = jax.ShapeDtypeStruct((3, TILES, LANES), f32)
    return pl.pallas_call(
        last_kernel,
        out_shape=(whole, whole, jax.ShapeDtypeStruct((8, LANES), f32)),
        in_specs=[SMEM] + [VMEM] * 5,
        out_specs=(VMEM,) * 3,
        compiler_params=params(),
        name="last_update",
    )(scalars, position, velocity, force, inv_mass, path_weight)


def passed_along(shard, axis, by):
    count = lax.axis_size(axis)
    return lax.ppermute(shard, axis, [(i, (i + by) % count) for i in range(count)])


def shifted(shard, axis, by):
    count = lax.axis_size(axis)
    pairs = [(i, i + by) for i in range(count) if 0 <= i + by < count]
    return lax.ppermute(shard, axis, pairs)


def body(positions, velocities, charges, inv_mass, path_weight, halo_index, tile_pairs, partner, bias_center, bias_spring):
    position = positions[0].reshape(3, TILES, LANES)
    velocity = velocities[0].reshape(3, TILES, LANES)
    charges = charges.reshape(TILES, LANES)
    inv_mass = inv_mass.reshape(TILES, LANES)
    path_weight = path_weight.reshape(TILES, LANES)
    pairs = tile_pairs.reshape(-1)
    partner_now = partner[0]
    window = lax.axis_index("rep")

    def choose(own, below, above):
        return jnp.where(partner_now == window - 1, below, jnp.where(partner_now == window + 1, above, own))

    position_below = shifted(position, "rep", 1)
    position_above = shifted(position, "rep", -1)
    velocity_below = shifted(velocity, "rep", 1)
    velocity_above = shifted(velocity, "rep", -1)
    plan = plan_halo(halo_index)
    position = choose(position, position_below, position_above)
    velocity = choose(velocity, velocity_below, velocity_above)
    center = bias_center[0]
    spring = bias_spring[0]

    half = GHOST_ROWS // 2
    ghosts, partial = first_gather(position, charges, path_weight, plan)
    lower = passed_along(ghosts[:, half:], "dom", 1)
    upper = passed_along(ghosts[:, :half], "dom", -1)
    lower_q, upper_q = lower[3], upper[3]
    for step_index in range(STEPS):
        progress = lax.psum(jnp.sum(partial), "dom")
        force = pair_forces(pairs, position, charges, lower, upper, lower_q, upper_q)
        scalars = jnp.stack([spring, progress, center])
        if step_index < STEPS - 1:
            position, velocity, ghosts, partial = middle_update(
                scalars, position, velocity, force, inv_mass, path_weight, plan
            )
            lower = passed_along(ghosts[:, half:], "dom", 1)
            upper = passed_along(ghosts[:, :half], "dom", -1)
        else:
            position, velocity, partial = last_update(scalars, position, velocity, force, inv_mass, path_weight)
    progress = lax.psum(jnp.sum(partial), "dom")
    energy = 0.5 * spring * (progress - center) ** 2
    atoms = TILES * LANES
    return position.reshape(1, 3, atoms), velocity.reshape(1, 3, atoms), energy[None]


def solution(mesh):
    in_specs = (
        P("rep", None, "dom"),
        P("rep", None, "dom"),
        P("dom"),
        P("dom"),
        P("dom"),
        P(None, "dom"),
        P("dom", None),
        P("rep"),
        P("rep"),
        P("rep"),
    )
    out_specs = (P("rep", None, "dom"), P("rep", None, "dom"), P("rep"))
    return jax.shard_map(body, mesh=mesh, in_specs=in_specs, out_specs=out_specs, check_vma=False)
```

time: 834 us -> 248 us (0.30)
  local copies, waits for them, and re-layouts: 469 us -> 5.73 us
  other arithmetic: 249 us -> 25.7 us
  Pallas kernels: 0 us -> 121 us
  waiting for transfers between devices: 11.5 us -> 0.02 us
    gather x10 -> x0, local copies, waits for them, and re-layouts: 298 us -> none  [the longest x4 141 us: ghost_layer(): send_down = atom_state[:, halo_index[0]]]
    reduce_sum x131 -> x5, other arithmetic: 196 us -> 3.01 us  [the longest x3 2.49 us: body(): progress = lax.psum(jnp.sum(partial), 'dom')]
    pallas_call x0 -> x5, Pallas kernels: none -> 121 us  [the longest x2 82.4 us: pair_forces(): pl.pallas_call(force_kernel, out_shape=jax.ShapeDtypeStruct((3, TILES, LA...]
    squeeze x64 -> x2, local copies, waits for them, and re-layouts: 54.1 us -> 1.32 us  [body(): lower_q, upper_q = (lower[3], upper[3])]
    dynamic_update_slice x64 -> x0, local copies, waits for them, and re-layouts: 39.7 us -> none  [tile_forces(): result = lax.map(one_block, (own_tiles, nearby_all))]
    concatenate x2 -> x0, local copies, waits for them, and re-layouts: 32.5 us -> none  [body(): atom_state = jnp.concatenate([position, charges[None]], axis=0)]
    div x64 -> x0, other arithmetic: 28.8 us -> none  [one_block(): own_block[:, 3, :, None] * nearby[:, 3, None, :] / (spread * spread)]
    sort x0 -> x2, other arithmetic: none -> 14.6 us  [the longest x1 7.31 us: plan_halo(): key, = lax.sort((key,), num_keys=1, is_stable=False)]
  transfers between devices with their start and end apart: 8 -> 8, of which waited for: 2 -> 0; matrix products, arithmetic and copies ran while one was open for 43% -> 11% of each run, Pallas kernels for 0% -> 7%
where the time goes in v1:
time: 248 us
  Pallas kernels  121 us (49%)
  blocking collectives  66.4 us (27%)
  other arithmetic  25.7 us (10%)
  starting transfers between devices  24.3 us (10%)
  local copies, waits for them, and re-layouts  5.73 us (2%)
  between operations  4.55 us (2%)
    pallas_call x2, Pallas kernels, pair_forces(): pl.pallas_call(force_kernel, out_shape=jax.ShapeDtypeStruct((3, TILES, LA...  82.4 us
    psum x3, blocking collectives, body(): progress = lax.psum(jnp.sum(partial), 'dom')  66.4 us
    pallas_call x1, Pallas kernels, first_gather(): pl.pallas_call(first_gather_kernel, out_shape=(jax.ShapeDtypeStruct((4, G...  18.4 us
    pallas_call x1, Pallas kernels, middle_update(): pl.pallas_call(middle_kernel, out_shape=(whole, whole, jax.ShapeDtypeStru...  17 us
    ppermute x4, starting transfers between devices, shifted(): return lax.ppermute(shard, axis, pairs)  12.9 us
    ppermute x4, starting transfers between devices, passed_along(): lax.ppermute(shard, axis, [(i, (i + by) % count) for i in range(count)])  11.4 us
    sort x1, other arithmetic, plan_halo(): key, = lax.sort((key,), num_keys=1, is_stable=False)  7.31 us
    sort x1, other arithmetic, plan_halo(): back, = lax.sort((back,), num_keys=1, is_stable=False)  7.31 us
  transfers between devices with their start and end apart: 8, of which 0 were waited for; matrix products, arithmetic and copies ran while one was open for 11% of the time, Pallas kernels for 7%

profile of v1, /device:TPU:96, one launch (start us, length us, event | category | flops | bytes accessed | tf_op | source)
XLA Modules:
  0.0 247.6 jit_solution(14796498913722597833)
XLA Ops:
  0.6 1.9 collective-permute-start
  2.6 4.5 %collective-permute-start.1 = (f32[3,512,128]{2,1,0:T(8,128)}, f32[3,512,128]{2,1,0:T(8,128)}, u32[]{:S(2)}, u32[]{:S(2)}) collective-permute-start(f32[3,512,128]{2,1,0:T(8,128)} %bitcast.42), channel_id=1, source_target_pairs={{8,0},{16,8},{24,16},{32,24},{40,32},{48,40},{56,48},{64,56},{72,6... | collective-permute-start | bytes 2359304 | tf_op jit(solution)/shard_map/ppermute | solution.py:349
  7.1 1.9 collective-permute-start.2
  9.0 4.5 %collective-permute-start.3 = (f32[3,512,128]{2,1,0:T(8,128)}, f32[3,512,128]{2,1,0:T(8,128)S(1)}, u32[]{:S(2)}, u32[]{:S(2)}) collective-permute-start(f32[3,512,128]{2,1,0:T(8,128)} %bitcast.45), channel_id=1, source_target_pairs={{8,0},{16,8},{24,16},{32,24},{40,32},{48,40},{56,48},{64,56},{72,6... | collective-permute-start | bytes 2359304 | tf_op jit(solution)/shard_map/ppermute | solution.py:349
  13.6 1.0 broadcast_shift-right-arithmetic_fusion.1
  15.4 7.3 %sort.14 = s32[32768]{0:T(1024)S(1)} sort(s32[32768]{0:T(1024)S(1)} %or_or_fusion), dimensions={0}, to_apply=%region_0.0 | sort | flops 491520 | bytes 262144 | tf_op jit(solution)/shard_map/sort | solution.py:32
  25.5 7.3 %sort.15 = s32[32768]{0:T(1024)S(1)} sort(s32[32768]{0:T(1024)S(1)} %get-tuple-element.43), dimensions={0}, to_apply=%region_1.0 | sort | flops 491520 | bytes 262144 | tf_op jit(solution)/shard_map/sort | solution.py:36
  35.8 1.0 select_select_fusion.1.position
  36.8 18.4 %first_gather.1 = (f32[4,256,128]{2,1,0:T(8,128)}, f32[8,128]{1,0:T(8,128)}) custom-call(f32[3,512,128]{2,1,0:T(8,128)} %select_select_fusion.1.position, f32[512,128]{1,0:T(8,128)} %bitcast.33, f32[512,128]{1,0:T(8,128)} %bitcast.36, s32[256,128]{1,0:T(8,128)} %get-tuple-element.44.source, s32[256,128]{1,0:T(8,128)} %and_bitcast_fusion.place, ...), custom_call_target="tpu_custom_call" | custom-call | tf_op jit(solution)/shard_map/first_gather/pallas_call | solution.py:135
  55.1 1.1 fusion
  56.3 5.7 %collective-permute-start.5 = (f32[4,128,128]{2,1,0:T(8,128)S(1)}, f32[4,128,128]{2,1,0:T(8,128)S(1)}, u32[]{:S(2)}, u32[]{:S(2)}) collective-permute-start(f32[4,128,128]{2,1,0:T(8,128)S(1)} %get-tuple-element.35), channel_id=1, source_target_pairs={{0,7},{1,0},{2,1},{3,2},{4,3},{5,4},{6,5},{7,6},{8,15},{9,8},{10,9... | collective-permute-start | bytes 786440 | tf_op jit(solution)/shard_map/ppermute | solution.py:343
  62.0 1.0 select_select_fusion.velocity
  63.6 25.2 %psum.21 = f32[1]{0:T(128)} all-reduce(f32[1]{0:T(128)} %bitcast.7), channel_id=1, replica_groups=mesh['rep'=16,'dom'=8] {'dom'}, use_global_device_ids=true, to_apply=%region_5.6 | all-reduce | flops 1 | bytes 8 | tf_op jit(solution)/shard_map/psum | solution.py:381
  88.8 1.3 maximum_maximum_fusion.scalars
  91.5 41.2 %pair_forces.2.force = f32[3,512,128]{2,1,0:T(8,128)} custom-call(s32[1024]{0:T(1024)} %reshape.95.pairs, f32[3,512,128]{2,1,0:T(8,128)} %select_select_fusion.1.position, f32[512,128]{1,0:T(8,128)} %bitcast.34, f32[4,128,128]{2,1,0:T(8,128)} %copy-done.3, f32[4,128,128]{2,1,0:T(8,128)} %copy-done.2, f32[128,128]{1,0:T(8,128)} %slice_bitcast_fusion.1.lower_q, ...), custom_call_target="tpu_custom_call" | custom-call | tf_op jit(solution)/shard_map/pair_forces/pallas_call | solution.py:262
  132.7 17.0 %middle_update.1 = (f32[3,512,128]{2,1,0:T(8,128)}, f32[3,512,128]{2,1,0:T(8,128)}, f32[3,256,128]{2,1,0:T(8,128)}, f32[8,128]{1,0:T(8,128)}) custom-call(f32[3]{0:T(128)} %maximum_maximum_fusion.scalars, f32[3,512,128]{2,1,0:T(8,128)} %select_select_fusion.1.position, f32[3,512,128]{2,1,0:T(8,128)} %select_select_fusion.velocity, ...), custom_call_target="tpu_custom_call" | custom-call | tf_op jit(solution)/shard_map/middle_update/pallas_call | solution.py:313
  149.7 1.1 fusion.1
  150.8 5.6 %collective-permute-start.7 = (f32[3,128,128]{2,1,0:T(8,128)S(1)}, f32[3,128,128]{2,1,0:T(8,128)S(1)}, u32[]{:S(2)}, u32[]{:S(2)}) collective-permute-start(f32[3,128,128]{2,1,0:T(8,128)S(1)} %get-tuple-element.37), channel_id=1, source_target_pairs={{0,7},{1,0},{2,1},{3,2},{4,3},{5,4},{6,5},{7,6},{8,15},{9,8},{10,9... | collective-permute-start | bytes 589832 | tf_op jit(solution)/shard_map/ppermute | solution.py:343
  157.0 19.7 %psum.22 = f32[1]{0:T(128)} all-reduce(f32[1]{0:T(128)} %bitcast.12), channel_id=1, replica_groups=mesh['rep'=16,'dom'=8] {'dom'}, use_global_device_ids=true, to_apply=%region_7.8 | all-reduce | flops 1 | bytes 8 | tf_op jit(solution)/shard_map/psum | solution.py:381
  176.8 1.2 maximum_maximum_fusion.1.scalars
  178.8 41.2 %pair_forces.3.force = f32[3,512,128]{2,1,0:T(8,128)} custom-call(s32[1024]{0:T(1024)} %reshape.95.pairs, f32[3,512,128]{2,1,0:T(8,128)} %get-tuple-element.15.position, f32[512,128]{1,0:T(8,128)} %bitcast.35, f32[3,128,128]{2,1,0:T(8,128)} %copy-done.4, f32[3,128,128]{2,1,0:T(8,128)} %copy-done.5, f32[128,128]{1,0:T(8,128)} %slice_bitcast_fusion.1.lower_q, ...), custom_call_target="tpu_custom_call" | custom-call | tf_op jit(solution)/shard_map/pair_forces/pallas_call | solution.py:262
  220.0 3.1 %last_update.1 = (f32[3,512,128]{2,1,0:T(8,128)}, f32[3,512,128]{2,1,0:T(8,128)}, f32[8,128]{1,0:T(8,128)}) custom-call(f32[3]{0:T(128)} %maximum_maximum_fusion.1.scalars, f32[3,512,128]{2,1,0:T(8,128)} %get-tuple-element.15.position, f32[3,512,128]{2,1,0:T(8,128)} %get-tuple-element.16.velocity, f32[3,512,128]{2,1,0:T(8,128)} %pair_forces.3.force, ...), custom_call_target="tpu_custom_call" | custom-call | tf_op jit(solution)/shard_map/last_update/pallas_call | solution.py:331
  223.1 1.3 reduce_sum.52
  224.4 21.4 %psum.23 = f32[]{:T(128)} all-reduce(f32[]{:T(128)} %reduce_sum.52), channel_id=1, replica_groups=mesh['rep'=16,'dom'=8] {'dom'}, use_global_device_ids=true, to_apply=%region_9.10 | all-reduce | flops 1 | bytes 8 | tf_op jit(solution)/shard_map/psum | solution.py:392
  (49 shorter events, 7.9 us)
Async XLA Ops:
  0.6 35.1 %collective-permute-start = (f32[3,512,128]{2,1,0:T(8,128)}, f32[3,512,128]{2,1,0:T(8,128)S(1)}, u32[]{:S(2)}, u32[]{:S(2)}) collective-permute-start(f32[3,512,128]{2,1,0:T(8,128)} %bitcast.41), channel_id=1, source_target_pairs={{0,8},{8,16},{16,24},{24,32},{32,40},{40,48},{48,56},{56,64},{64,7... | collective-permute-start | bytes 2359304 | tf_op jit(solution)/shard_map/ppermute | solution.py:349
  2.6 33.2 %collective-permute-start.1 = (f32[3,512,128]{2,1,0:T(8,128)}, f32[3,512,128]{2,1,0:T(8,128)}, u32[]{:S(2)}, u32[]{:S(2)}) collective-permute-start(f32[3,512,128]{2,1,0:T(8,128)} %bitcast.42), channel_id=1, source_target_pairs={{8,0},{16,8},{24,16},{32,24},{40,32},{48,40},{56,48},{64,56},{72,6... | collective-permute-start | bytes 2359304 | tf_op jit(solution)/shard_map/ppermute | solution.py:349
  7.1 54.8 %collective-permute-start.2 = (f32[3,512,128]{2,1,0:T(8,128)}, f32[3,512,128]{2,1,0:T(8,128)S(1)}, u32[]{:S(2)}, u32[]{:S(2)}) collective-permute-start(f32[3,512,128]{2,1,0:T(8,128)} %bitcast.44), channel_id=1, source_target_pairs={{0,8},{8,16},{16,24},{24,32},{32,40},{40,48},{48,56},{56,64},{64,7... | collective-permute-start | bytes 2359304 | tf_op jit(solution)/shard_map/ppermute | solution.py:349
  9.0 52.9 %collective-permute-start.3 = (f32[3,512,128]{2,1,0:T(8,128)}, f32[3,512,128]{2,1,0:T(8,128)S(1)}, u32[]{:S(2)}, u32[]{:S(2)}) collective-permute-start(f32[3,512,128]{2,1,0:T(8,128)} %bitcast.45), channel_id=1, source_target_pairs={{8,0},{16,8},{24,16},{32,24},{40,32},{48,40},{56,48},{64,56},{72,6... | collective-permute-start | bytes 2359304 | tf_op jit(solution)/shard_map/ppermute | solution.py:349
  15.4 17.5 %copy-start.6 = (s32[512,2]{0,1:T(2,128)S(1)}, s32[512,2]{0,1:T(2,128)}, u32[]{:S(2)}) copy-start(s32[512,2]{0,1:T(2,128)} %param.16) | copy-start | bytes 12292
  23.4 12.4 %copy-start = (f32[1,3,65536]{2,0,1:T(1,128)S(1)}, f32[1,3,65536]{2,0,1:T(1,128)}, u32[]{:S(2)}) copy-start(f32[1,3,65536]{2,0,1:T(1,128)} %param.10) | copy-start | bytes 2359300
  55.1 6.8 %copy-start.1 = (f32[1,3,65536]{2,0,1:T(1,128)S(1)}, f32[1,3,65536]{2,0,1:T(1,128)}, u32[]{:S(2)}) copy-start(f32[1,3,65536]{2,0,1:T(1,128)} %param.11) | copy-start | bytes 2359300
  56.3 33.8 %collective-permute-start.5 = (f32[4,128,128]{2,1,0:T(8,128)S(1)}, f32[4,128,128]{2,1,0:T(8,128)S(1)}, u32[]{:S(2)}, u32[]{:S(2)}) collective-permute-start(f32[4,128,128]{2,1,0:T(8,128)S(1)} %get-tuple-element.35), channel_id=1, source_target_pairs={{0,7},{1,0},{2,1},{3,2},{4,3},{5,4},{6,5},{7,6},{8,15},{9,8},{10,9... | collective-permute-start | bytes 786440 | tf_op jit(solution)/shard_map/ppermute | solution.py:343
  62.0 1.0 copy-start.7
  62.0 28.8 %collective-permute-start.4 = (f32[4,128,128]{2,1,0:T(8,128)S(1)}, f32[4,128,128]{2,1,0:T(8,128)S(1)}, u32[]{:S(2)}, u32[]{:S(2)}) collective-permute-start(f32[4,128,128]{2,1,0:T(8,128)S(1)} %get-tuple-element.36), channel_id=1, source_target_pairs={{0,1},{1,2},{2,3},{3,4},{4,5},{5,6},{6,7},{7,0},{8,9},{9,10},{10,1... | collective-permute-start | bytes 786440 | tf_op jit(solution)/shard_map/ppermute | solution.py:343
  90.1 1.3 copy-start.2
  90.7 0.7 copy-start.3
  149.7 6.8 %copy-start.8 = (f32[8,128]{1,0:T(8,128)S(1)}, f32[8,128]{1,0:T(8,128)}, u32[]{:S(2)}) copy-start(f32[8,128]{1,0:T(8,128)} %get-tuple-element.14) | copy-start | bytes 12292
  150.7 27.3 %collective-permute-start.6 = (f32[3,128,128]{2,1,0:T(8,128)S(1)}, f32[3,128,128]{2,1,0:T(8,128)S(1)}, u32[]{:S(2)}, u32[]{:S(2)}) collective-permute-start(f32[3,128,128]{2,1,0:T(8,128)S(1)} %get-tuple-element.38), channel_id=1, source_target_pairs={{0,1},{1,2},{2,3},{3,4},{4,5},{5,6},{6,7},{7,0},{8,9},{9,10},{10,1... | collective-permute-start | bytes 589832 | tf_op jit(solution)/shard_map/ppermute | solution.py:343
  150.8 27.2 %collective-permute-start.7 = (f32[3,128,128]{2,1,0:T(8,128)S(1)}, f32[3,128,128]{2,1,0:T(8,128)S(1)}, u32[]{:S(2)}, u32[]{:S(2)}) collective-permute-start(f32[3,128,128]{2,1,0:T(8,128)S(1)} %get-tuple-element.37), channel_id=1, source_target_pairs={{0,7},{1,0},{2,1},{3,2},{4,3},{5,4},{6,5},{7,6},{8,15},{9,8},{10,9... | collective-permute-start | bytes 589832 | tf_op jit(solution)/shard_map/ppermute | solution.py:343
  178.0 0.7 copy-start.4
  178.0 0.7 copy-start.5

commit v2 on v1

--- a/solution.py
+++ b/solution.py
@@ -12,7 +12,7 @@
 GROUPS = 16
 GROUP_ROWS = 32
 CELLS = 32
-TILES_AT_ONCE = 8
+TILES_AT_ONCE = 16
 time_step = 0.1
 f32 = jnp.float32
 bf16 = jnp.bfloat16
@@ -153,7 +153,7 @@
     return high, middle, rest - middle
 
 
-def force_kernel(pairs, position, charges, lower, upper, lower_q, upper_q, force, rows_j, rows_i, rows_a, feat_j, feat_i, feat_a, sums):
+def force_kernel(pairs, position, charges, lower, upper, lower_q, upper_q, force, rows_j, rows_i, rows_a, feat_j, feat_i, feat_a, sums, spread_a, spread_b):
     zero8 = jnp.zeros((8, LANES), f32)
     one8 = jnp.ones((8, LANES), f32)
     for f in (13, 14, 15):
@@ -213,33 +213,38 @@
     def contract(a, b, left, right):
         return lax.dot_general(a, b, (((left,), (right,)), ((), ())), preferred_element_type=f32)
 
-    def tiles(n, carry):
-        found = []
-        for u in range(TILES_AT_ONCE):
-            tile = n * TILES_AT_ONCE + u
-            one, two = pairs[2 * tile], pairs[2 * tile + 1]
-            near = jnp.concatenate([feat_j[one], feat_j[two]], axis=1)
-            spread = contract(jnp.concatenate([near] * 3, axis=0), feat_i[tile], 0, 0)
-            found.append((tile, one, two, spread))
-        done = []
-        for tile, one, two, spread in found:
-            weight = pl.reciprocal(spread * spread, approx=True)
-            high = weight.astype(bf16)
-            low = (weight - high.astype(f32)).astype(bf16)
-            near = jnp.concatenate([feat_a[one], feat_a[two]], axis=1)
-            done.append(
-                (
-                    tile,
-                    contract(
-                        jnp.concatenate([near, near], axis=1), jnp.concatenate([high, low], axis=0), 1, 0
-                    ),
-                )
-            )
-        for tile, value in done:
-            sums[pl.ds(pl.multiple_of(tile * 16, 16), 16), :] = value
+    def listed(tile):
+        tile = jnp.minimum(tile, TILES - 1)
+        return tile, pairs[2 * tile], pairs[2 * tile + 1]
+
+    def spread_of(tile):
+        tile, one, two = listed(tile)
+        near = jnp.concatenate([feat_j[one], feat_j[two]], axis=1)
+        return contract(jnp.concatenate([near] * 3, axis=0), feat_i[tile], 0, 0)
+
+    def force_of(tile, spread):
+        tile, one, two = listed(tile)
+        weight = pl.reciprocal(spread * spread, approx=True)
+        high = weight.astype(bf16)
+        low = (weight - high.astype(f32)).astype(bf16)
+        near = jnp.concatenate([feat_a[one], feat_a[two]], axis=1)
+        return contract(jnp.concatenate([near, near], axis=1), jnp.concatenate([high, low], axis=0), 1, 0)
+
+    many = TILES_AT_ONCE
+    for u in range(many):
+        spread_a[u] = spread_of(u)
+
+    def tiles(m, carry):
+        for now, later, n in ((spread_a, spread_b, 2 * m), (spread_b, spread_a, 2 * m + 1)):
+            done = []
+            for u in range(many):
+                later[u] = spread_of((n + 1) * many + u)
+                done.append(force_of(n * many + u, now[u]))
+            for u in range(many):
+                sums[pl.ds(pl.multiple_of((n * many + u) * 16, 16), 16), :] = done[u]
         return carry
 
-    lax.fori_loop(0, TILES // TILES_AT_ONCE, tiles, 0)
+    lax.fori_loop(0, TILES // many // 2, tiles, 0)
 
     def combine(b, carry):
         base = pl.multiple_of(b * 8, 8)
@@ -272,16 +277,18 @@
             pltpu.VMEM((TILES, 48, LANES), bf16),
             pltpu.VMEM((TILES + 256, 16, LANES), bf16),
             pltpu.VMEM((TILES * 16, LANES), f32),
+            pltpu.VMEM((TILES_AT_ONCE, 2 * LANES, LANES), f32),
+            pltpu.VMEM((TILES_AT_ONCE, 2 * LANES, LANES), f32),
         ],
         compiler_params=params(),
         name="pair_forces",
     )(pairs, position, charges, lower, upper, lower_q, upper_q)
 
 
-def advance(scalars, position, velocity, force, inv_mass, path_weight, new_position, new_velocity):
+def advance(scalars, parts, position, velocity, force, inv_mass, path_weight, new_position, new_velocity):
     weight = path_weight[...]
     rate = time_step * inv_mass[...]
-    pull = scalars[0] * (scalars[1] - scalars[2])
+    pull = scalars[0] * (jnp.sum(parts[...]) - scalars[1])
     for c in range(3):
         total = force[c]
         if c == 2:
@@ -293,10 +300,10 @@
 
 
 def middle_kernel(
-    scalars, position, velocity, force, inv_mass, path_weight, source, place, span, cell_rows,
+    scalars, parts, position, velocity, force, inv_mass, path_weight, source, place, span, cell_rows,
     new_position, new_velocity, ghosts, partial, listed,
 ):
-    partial[...] = advance(scalars, position, velocity, force, inv_mass, path_weight, new_position, new_velocity)
+    partial[...] = advance(scalars, parts, position, velocity, force, inv_mass, path_weight, new_position, new_velocity)
 
     def read_row(c, r):
         return new_position[c, pl.ds(r, 1), :]
@@ -304,11 +311,11 @@
     gather_stages(3, read_row, source, place, span, cell_rows, listed, ghosts)
 
 
-def last_kernel(scalars, position, velocity, force, inv_mass, path_weight, new_position, new_velocity, partial):
-    partial[...] = advance(scalars, position, velocity, force, inv_mass, path_weight, new_position, new_velocity)
-
-
-def middle_update(scalars, position, velocity, force, inv_mass, path_weight, plan):
+def last_kernel(scalars, parts, position, velocity, force, inv_mass, path_weight, new_position, new_velocity, partial):
+    partial[...] = advance(scalars, parts, position, velocity, force, inv_mass, path_weight, new_position, new_velocity)
+
+
+def middle_update(scalars, parts, position, velocity, force, inv_mass, path_weight, plan):
     whole = jax.ShapeDtypeStruct((3, TILES, LANES), f32)
     return pl.pallas_call(
         middle_kernel,
@@ -318,29 +325,105 @@
             jax.ShapeDtypeStruct((3, GHOST_ROWS, LANES), f32),
             jax.ShapeDtypeStruct((8, LANES), f32),
         ),
-        in_specs=[SMEM] + [VMEM] * 7 + [SMEM] * 2,
+        in_specs=[SMEM] + [VMEM] * 8 + [SMEM] * 2,
         out_specs=(VMEM,) * 4,
         scratch_shapes=[pltpu.VMEM((3, GHOST_ROWS, LANES), f32)],
         compiler_params=params(),
         name="middle_update",
-    )(scalars, position, velocity, force, inv_mass, path_weight, *plan)
-
-
-def last_update(scalars, position, velocity, force, inv_mass, path_weight):
+    )(scalars, parts, position, velocity, force, inv_mass, path_weight, *plan)
+
+
+def last_update(scalars, parts, position, velocity, force, inv_mass, path_weight):
     whole = jax.ShapeDtypeStruct((3, TILES, LANES), f32)
     return pl.pallas_call(
         last_kernel,
         out_shape=(whole, whole, jax.ShapeDtypeStruct((8, LANES), f32)),
-        in_specs=[SMEM] + [VMEM] * 5,
+        in_specs=[SMEM] + [VMEM] * 6,
         out_specs=(VMEM,) * 3,
         compiler_params=params(),
         name="last_update",
-    )(scalars, position, velocity, force, inv_mass, path_weight)
-
-
-def passed_along(shard, axis, by):
-    count = lax.axis_size(axis)
-    return lax.ppermute(shard, axis, [(i, (i + by) % count) for i in range(count)])
+    )(scalars, parts, position, velocity, force, inv_mass, path_weight)
+
+
+def exchange_kernel(count, half, ghosts, partial, lower, upper, parts, sent, got, local):
+    me = lax.axis_index("dom")
+    barrier = pltpu.get_barrier_semaphore()
+    for k in range(1, count):
+        pl.semaphore_signal(
+            barrier, inc=1, device_id={"dom": lax.rem(me + k, count)}, device_id_type=pl.DeviceIdType.MESH
+        )
+    pl.semaphore_wait(barrier, count - 1)
+    copies = []
+
+    def send(source, target, k, n):
+        copy = pltpu.make_async_remote_copy(
+            src_ref=source,
+            dst_ref=target,
+            send_sem=sent.at[n],
+            recv_sem=got.at[n],
+            device_id={"dom": lax.rem(me + k, count)},
+            device_id_type=pl.DeviceIdType.MESH,
+        )
+        copy.start()
+        copies.append(copy)
+
+    if half:
+        send(ghosts.at[:, pl.ds(half, half)], lower, 1, 0)
+        send(ghosts.at[:, pl.ds(0, half)], upper, count - 1, count)
+    for k in range(1, count):
+        send(partial, parts.at[me], k, k)
+    own = pltpu.make_async_copy(partial, parts.at[me], local)
+    own.start()
+    own.wait()
+    for copy in copies:
+        copy.wait()
+
+
+def exchange(ghosts, partial, number):
+    count = lax.axis_size("dom")
+    comps, rows = ghosts.shape[:2]
+    side = jax.ShapeDtypeStruct((comps, rows // 2, LANES), f32)
+
+    def kernel(*refs):
+        exchange_kernel(count, rows // 2, *refs)
+
+    return pl.pallas_call(
+        kernel,
+        out_shape=(side, side, jax.ShapeDtypeStruct((count, 8, LANES), f32)),
+        in_specs=[VMEM] * 2,
+        out_specs=(VMEM,) * 3,
+        scratch_shapes=[
+            pltpu.SemaphoreType.DMA((count + 1,)),
+            pltpu.SemaphoreType.DMA((count + 1,)),
+            pltpu.SemaphoreType.DMA,
+        ],
+        compiler_params=pltpu.CompilerParams(collective_id=number, has_side_effects=True),
+        name="exchange",
+    )(ghosts, partial)
+
+
+def share_energy(partial, scalars, number):
+    count = lax.axis_size("dom")
+
+    def kernel(partial, scalars, energy, parts, sent, got, local):
+        exchange_kernel(count, 0, None, partial, None, None, parts, sent, got, local)
+        off = jnp.sum(parts[...]) - scalars[1]
+        energy[...] = jnp.full((8, LANES), 0.5 * scalars[0] * off * off, f32)
+
+    return pl.pallas_call(
+        kernel,
+        out_shape=jax.ShapeDtypeStruct((8, LANES), f32),
+        in_specs=[VMEM, SMEM],
+        out_specs=VMEM,
+        scratch_shapes=[
+            pltpu.VMEM((count, 8, LANES), f32),
+            pltpu.SemaphoreType.DMA((count,)),
+            pltpu.SemaphoreType.DMA((count,)),
+            pltpu.SemaphoreType.DMA,
+        ],
+        compiler_params=pltpu.CompilerParams(collective_id=number, has_side_effects=True),
+        name="share_energy",
+    )(partial, scalars)
 
 
 def shifted(shard, axis, by):
@@ -372,27 +455,22 @@
     center = bias_center[0]
     spring = bias_spring[0]
 
-    half = GHOST_ROWS // 2
+    scalars = jnp.stack([spring, center])
     ghosts, partial = first_gather(position, charges, path_weight, plan)
-    lower = passed_along(ghosts[:, half:], "dom", 1)
-    upper = passed_along(ghosts[:, :half], "dom", -1)
-    lower_q, upper_q = lower[3], upper[3]
     for step_index in range(STEPS):
-        progress = lax.psum(jnp.sum(partial), "dom")
+        lower, upper, parts = exchange(ghosts, partial, step_index)
+        if step_index == 0:
+            lower_q, upper_q = lower[3], upper[3]
         force = pair_forces(pairs, position, charges, lower, upper, lower_q, upper_q)
-        scalars = jnp.stack([spring, progress, center])
         if step_index < STEPS - 1:
             position, velocity, ghosts, partial = middle_update(
-                scalars, position, velocity, force, inv_mass, path_weight, plan
+                scalars, parts, position, velocity, force, inv_mass, path_weight, plan
             )
-            lower = passed_along(ghosts[:, half:], "dom", 1)
-            upper = passed_along(ghosts[:, :half], "dom", -1)
         else:
-            position, velocity, partial = last_update(scalars, position, velocity, force, inv_mass, path_weight)
-    progress = lax.psum(jnp.sum(partial), "dom")
-    energy = 0.5 * spring * (progress - center) ** 2
+            position, velocity, partial = last_update(scalars, parts, position, velocity, force, inv_mass, path_weight)
+    energy = share_energy(partial, scalars, STEPS)[0, :1]
     atoms = TILES * LANES
-    return position.reshape(1, 3, atoms), velocity.reshape(1, 3, atoms), energy[None]
+    return position.reshape(1, 3, atoms), velocity.reshape(1, 3, atoms), energy
 
 
 def solution(mesh):

time: 248 us -> 180 us (0.73)
  blocking collectives: 66.4 us -> 0 us
  Pallas kernels: 121 us -> 138 us
  starting transfers between devices: 24.3 us -> 11.2 us
  other arithmetic: 25.7 us -> 21.3 us
    psum x3 -> x0, blocking collectives: 66.4 us -> none  [body(): progress = lax.psum(jnp.sum(partial), 'dom')]
    pallas_call x0 -> x3, Pallas kernels: none -> 36.8 us  [the longest x2 27.5 us: exchange(): pl.pallas_call(kernel, out_shape=(side, side, jax.ShapeDtypeStruct((count...]
    pallas_call x2, Pallas kernels: 82.4 us -> 62.6 us  [pair_forces(): pl.pallas_call(force_kernel, out_shape=jax.ShapeDtypeStruct((3, TILES, LA...]
    ppermute x4 -> x0, starting transfers between devices: 11.4 us -> none  [passed_along(): lax.ppermute(shard, axis, [(i, (i + by) % count) for i in range(count)])]
    reduce_sum x3 -> x0, other arithmetic: 2.49 us -> none  [body(): progress = lax.psum(jnp.sum(partial), 'dom')]
  transfers between devices with their start and end apart: 8 -> 4, of which waited for: 0 -> 0; matrix products, arithmetic and copies ran while one was open for 11% -> 13% of each run, Pallas kernels for 7% -> 37%
where the time goes in v2:
time: 180 us; the launch traced here: 178 us
  Pallas kernels  138 us (77%)
  other arithmetic  21.3 us (12%)
  starting transfers between devices  11.2 us (6%)
  local copies, waits for them, and re-layouts  4.13 us (2%)
  between operations  2.76 us (2%)
    pallas_call x2, Pallas kernels, pair_forces(): pl.pallas_call(force_kernel, out_shape=jax.ShapeDtypeStruct((3, TILES, LA...  62.6 us
    pallas_call x2, Pallas kernels, exchange(): pl.pallas_call(kernel, out_shape=(side, side, jax.ShapeDtypeStruct((count...  27.5 us
    pallas_call x1, Pallas kernels, first_gather(): pl.pallas_call(first_gather_kernel, out_shape=(jax.ShapeDtypeStruct((4, G...  18.8 us
    pallas_call x1, Pallas kernels, middle_update(): pl.pallas_call(middle_kernel, out_shape=(whole, whole, jax.ShapeDtypeStru...  17.2 us
    ppermute x4, starting transfers between devices, shifted(): return lax.ppermute(shard, axis, pairs)  11.2 us
    pallas_call x1, Pallas kernels, share_energy(): pl.pallas_call(kernel, out_shape=jax.ShapeDtypeStruct((8, LANES), f32), i...  9.3 us
    sort x1, other arithmetic, plan_halo(): key, = lax.sort((key,), num_keys=1, is_stable=False)  7.31 us
    sort x1, other arithmetic, plan_halo(): back, = lax.sort((back,), num_keys=1, is_stable=False)  7.31 us
  transfers between devices with their start and end apart: 4, of which 0 were waited for; matrix products, arithmetic and copies ran while one was open for 13% of the time, Pallas kernels for 37%

profile of v2, /device:TPU:96, one launch (start us, length us, event | category | flops | bytes accessed | tf_op | source)
XLA Modules:
  0.0 177.8 jit_solution(397668046820569824)
XLA Ops:
  0.6 2.8 %collective-permute-start.1 = (f32[3,512,128]{2,1,0:T(8,128)}, f32[3,512,128]{2,1,0:T(8,128)S(1)}, u32[]{:S(2)}, u32[]{:S(2)}) collective-permute-start(f32[3,512,128]{2,1,0:T(8,128)} %bitcast.36), channel_id=1, source_target_pairs={{8,0},{16,8},{24,16},{32,24},{40,32},{48,40},{56,48},{64,56},{72,6... | collective-permute-start | bytes 2359304 | tf_op jit(solution)/shard_map/ppermute | solution.py:432
  3.4 1.9 %collective-permute-start = (f32[3,512,128]{2,1,0:T(8,128)}, f32[3,512,128]{2,1,0:T(8,128)}, u32[]{:S(2)}, u32[]{:S(2)}) collective-permute-start(f32[3,512,128]{2,1,0:T(8,128)} %bitcast.37), channel_id=1, source_target_pairs={{0,8},{8,16},{16,24},{24,32},{32,40},{40,48},{48,56},{56,64},{64,7... | collective-permute-start | bytes 2359304 | tf_op jit(solution)/shard_map/ppermute | solution.py:432
  5.3 4.5 %collective-permute-start.3 = (f32[3,512,128]{2,1,0:T(8,128)}, f32[3,512,128]{2,1,0:T(8,128)S(1)}, u32[]{:S(2)}, u32[]{:S(2)}) collective-permute-start(f32[3,512,128]{2,1,0:T(8,128)} %bitcast.39), channel_id=1, source_target_pairs={{8,0},{16,8},{24,16},{32,24},{40,32},{48,40},{56,48},{64,56},{72,6... | collective-permute-start | bytes 2359304 | tf_op jit(solution)/shard_map/ppermute | solution.py:432
  9.9 1.9 %collective-permute-start.2 = (f32[3,512,128]{2,1,0:T(8,128)}, f32[3,512,128]{2,1,0:T(8,128)S(1)}, u32[]{:S(2)}, u32[]{:S(2)}) collective-permute-start(f32[3,512,128]{2,1,0:T(8,128)} %bitcast.40), channel_id=1, source_target_pairs={{0,8},{8,16},{16,24},{24,32},{32,40},{40,48},{48,56},{56,64},{64,7... | collective-permute-start | bytes 2359304 | tf_op jit(solution)/shard_map/ppermute | solution.py:432
  11.8 1.0 broadcast_shift-right-arithmetic_fusion.1
  15.0 7.3 %sort.14 = s32[32768]{0:T(1024)S(1)} sort(s32[32768]{0:T(1024)S(1)} %or_or_fusion), dimensions={0}, to_apply=%region_0.0 | sort | flops 491520 | bytes 262144 | tf_op jit(solution)/shard_map/sort | solution.py:32
  22.4 0.7 broadcast_shift-right-arithmetic_fusion
  23.3 0.6 pad_add_fusion.1.span
  23.9 0.6 pad_add_fusion.cell_rows
  25.9 0.8 reshape.93.pairs
  26.6 7.3 %sort.15 = s32[32768]{0:T(1024)S(1)} sort(s32[32768]{0:T(1024)S(1)} %get-tuple-element.51), dimensions={0}, to_apply=%region_1.0 | sort | flops 491520 | bytes 262144 | tf_op jit(solution)/shard_map/sort | solution.py:36
  34.0 0.7 and_bitcast_fusion.place
  34.6 1.0 select_select_fusion.1.position
  35.6 18.8 %first_gather.1 = (f32[4,256,128]{2,1,0:T(8,128)}, f32[8,128]{1,0:T(8,128)}) custom-call(f32[3,512,128]{2,1,0:T(8,128)} %select_select_fusion.1.position, f32[512,128]{1,0:T(8,128)} %bitcast.28, f32[512,128]{1,0:T(8,128)} %bitcast.31, s32[256,128]{1,0:T(8,128)} %get-tuple-element.52.source, s32[256,128]{1,0:T(8,128)} %and_bitcast_fusion.place, ...), custom_call_target="tpu_custom_call" | custom-call | tf_op jit(solution)/shard_map/first_gather/pallas_call | solution.py:135
  54.4 15.2 %exchange.2 = (f32[4,128,128]{2,1,0:T(8,128)}, f32[4,128,128]{2,1,0:T(8,128)}, f32[8,8,128]{2,1,0:T(8,128)}) custom-call(f32[4,256,128]{2,1,0:T(8,128)} %get-tuple-element.18.refs_0_, f32[8,128]{1,0:T(8,128)} %get-tuple-element.19.refs_1_), custom_call_target="tpu_custom_call" | custom-call | tf_op jit(solution)/shard_map/exchange/pallas_call | solution.py:390
  69.7 1.5 slice_bitcast_fusion
  71.2 31.3 %pair_forces.2.force = f32[3,512,128]{2,1,0:T(8,128)} custom-call(s32[1024]{0:T(1024)} %reshape.93.pairs, f32[3,512,128]{2,1,0:T(8,128)} %select_select_fusion.1.position, f32[512,128]{1,0:T(8,128)} %bitcast.29, f32[4,128,128]{2,1,0:T(8,128)} %get-tuple-element.21.lower, f32[4,128,128]{2,1,0:T(8,128)} %get-tuple-element.22.upper, ...), custom_call_target="tpu_custom_call" | custom-call | tf_op jit(solution)/shard_map/pair_forces/pallas_call | solution.py:267
  102.5 1.0 select_select_fusion.velocity
  103.5 17.2 %middle_update.1 = (f32[3,512,128]{2,1,0:T(8,128)}, f32[3,512,128]{2,1,0:T(8,128)}, f32[3,256,128]{2,1,0:T(8,128)}, f32[8,128]{1,0:T(8,128)}) custom-call(f32[2]{0:T(128)} %pad_maximum_fusion.scalars, f32[8,8,128]{2,1,0:T(8,128)} %get-tuple-element.20.parts, f32[3,512,128]{2,1,0:T(8,128)} %select_select_fusion.1.position, ...), custom_call_target="tpu_custom_call" | custom-call | tf_op jit(solution)/shard_map/middle_update/pallas_call | solution.py:320
  120.7 12.2 %exchange.3 = (f32[3,128,128]{2,1,0:T(8,128)}, f32[3,128,128]{2,1,0:T(8,128)}, f32[8,8,128]{2,1,0:T(8,128)}) custom-call(f32[3,256,128]{2,1,0:T(8,128)} %get-tuple-element.23.refs_0_, f32[8,128]{1,0:T(8,128)} %get-tuple-element.24.refs_1_), custom_call_target="tpu_custom_call" | custom-call | tf_op jit(solution)/shard_map/exchange/pallas_call | solution.py:390
  132.9 31.3 %pair_forces.3.force = f32[3,512,128]{2,1,0:T(8,128)} custom-call(s32[1024]{0:T(1024)} %reshape.93.pairs, f32[3,512,128]{2,1,0:T(8,128)} %get-tuple-element.26.position, f32[512,128]{1,0:T(8,128)} %bitcast.30, f32[3,128,128]{2,1,0:T(8,128)} %get-tuple-element.28.lower, f32[3,128,128]{2,1,0:T(8,128)} %get-tuple-element.29.upper, ...), custom_call_target="tpu_custom_call" | custom-call | tf_op jit(solution)/shard_map/pair_forces/pallas_call | solution.py:267
  164.2 3.1 %last_update.1 = (f32[3,512,128]{2,1,0:T(8,128)}, f32[3,512,128]{2,1,0:T(8,128)}, f32[8,128]{1,0:T(8,128)}) custom-call(f32[2]{0:T(128)} %pad_maximum_fusion.scalars, f32[8,8,128]{2,1,0:T(8,128)} %get-tuple-element.25.parts, f32[3,512,128]{2,1,0:T(8,128)} %get-tuple-element.26.position, f32[3,512,128]{2,1,0:T(8,128)} %get-tuple-element.27.velocity, ...), custom_call_target="tpu_custom_call" | custom-call | tf_op jit(solution)/shard_map/last_update/pallas_call | solution.py:338
  167.3 9.3 %share_energy.1 = f32[8,128]{1,0:T(8,128)} custom-call(f32[8,128]{1,0:T(8,128)} %get-tuple-element.32.partial, f32[2]{0:T(128)} %pad_maximum_fusion.scalars), custom_call_target="tpu_custom_call" | custom-call | tf_op jit(solution)/shard_map/share_energy/pallas_call | solution.py:413
  176.6 1.2 slice.19
  (23 shorter events, 1.8 us)
Async XLA Ops:
  0.6 34.0 %collective-permute-start.1 = (f32[3,512,128]{2,1,0:T(8,128)}, f32[3,512,128]{2,1,0:T(8,128)S(1)}, u32[]{:S(2)}, u32[]{:S(2)}) collective-permute-start(f32[3,512,128]{2,1,0:T(8,128)} %bitcast.36), channel_id=1, source_target_pairs={{8,0},{16,8},{24,16},{32,24},{40,32},{48,40},{56,48},{64,56},{72,6... | collective-permute-start | bytes 2359304 | tf_op jit(solution)/shard_map/ppermute | solution.py:432
  3.4 31.2 %collective-permute-start = (f32[3,512,128]{2,1,0:T(8,128)}, f32[3,512,128]{2,1,0:T(8,128)}, u32[]{:S(2)}, u32[]{:S(2)}) collective-permute-start(f32[3,512,128]{2,1,0:T(8,128)} %bitcast.37), channel_id=1, source_target_pairs={{0,8},{8,16},{16,24},{24,32},{32,40},{40,48},{48,56},{56,64},{64,7... | collective-permute-start | bytes 2359304 | tf_op jit(solution)/shard_map/ppermute | solution.py:432
  5.3 97.2 %collective-permute-start.3 = (f32[3,512,128]{2,1,0:T(8,128)}, f32[3,512,128]{2,1,0:T(8,128)S(1)}, u32[]{:S(2)}, u32[]{:S(2)}) collective-permute-start(f32[3,512,128]{2,1,0:T(8,128)} %bitcast.39), channel_id=1, source_target_pairs={{8,0},{16,8},{24,16},{32,24},{40,32},{48,40},{56,48},{64,56},{72,6... | collective-permute-start | bytes 2359304 | tf_op jit(solution)/shard_map/ppermute | solution.py:432
  9.9 92.7 %collective-permute-start.2 = (f32[3,512,128]{2,1,0:T(8,128)}, f32[3,512,128]{2,1,0:T(8,128)S(1)}, u32[]{:S(2)}, u32[]{:S(2)}) collective-permute-start(f32[3,512,128]{2,1,0:T(8,128)} %bitcast.40), channel_id=1, source_target_pairs={{0,8},{8,16},{16,24},{24,32},{32,40},{40,48},{48,56},{56,64},{64,7... | collective-permute-start | bytes 2359304 | tf_op jit(solution)/shard_map/ppermute | solution.py:432
  15.0 10.7 %copy-start.2 = (s32[512,2]{0,1:T(2,128)S(1)}, s32[512,2]{0,1:T(2,128)}, u32[]{:S(2)}) copy-start(s32[512,2]{0,1:T(2,128)} %param.16) | copy-start | bytes 12292
  23.1 11.6 %copy-start = (f32[1,3,65536]{2,0,1:T(1,128)S(1)}, f32[1,3,65536]{2,0,1:T(1,128)}, u32[]{:S(2)}) copy-start(f32[1,3,65536]{2,0,1:T(1,128)} %param.10) | copy-start | bytes 2359300
  71.2 31.4 %copy-start.1 = (f32[1,3,65536]{2,0,1:T(1,128)S(1)}, f32[1,3,65536]{2,0,1:T(1,128)}, u32[]{:S(2)}) copy-start(f32[1,3,65536]{2,0,1:T(1,128)} %param.11) | copy-start | bytes 2359300

commit v3 on v1

--- a/solution.py
+++ b/solution.py
@@ -12,7 +12,7 @@
 GROUPS = 16
 GROUP_ROWS = 32
 CELLS = 32
-TILES_AT_ONCE = 8
+TILES_AT_ONCE = 16
 time_step = 0.1
 f32 = jnp.float32
 bf16 = jnp.bfloat16
@@ -153,7 +153,45 @@
     return high, middle, rest - middle
 
 
-def force_kernel(pairs, position, charges, lower, upper, lower_q, upper_q, force, rows_j, rows_i, rows_a, feat_j, feat_i, feat_a, sums):
+def step_kernel(
+    count, last, scalars, pairs, ghosts, partial, position, velocity, charges, lower_q, upper_q, inv_mass, path_weight,
+    new_position, new_velocity, result, *rest,
+):
+    if last:
+        kept_q = ()
+    else:
+        kept_q, rest = rest[:2], rest[2:]
+    (
+        rows_j, rows_i, rows_a, feat_j, feat_i, feat_a, sums, spread_a, spread_b,
+        lower, upper, parts, final, sent, got, sent_last, got_last,
+    ) = rest
+    me = lax.axis_index("dom")
+    half = GHOST_ROWS // 2
+    barrier = pltpu.get_barrier_semaphore()
+    for k in range(1, count):
+        pl.semaphore_signal(
+            barrier, inc=1, device_id={"dom": lax.rem(me + k, count)}, device_id_type=pl.DeviceIdType.MESH
+        )
+    pl.semaphore_wait(barrier, count - 1)
+
+    def send(source, target, k, sent_now, got_now):
+        copy = pltpu.make_async_remote_copy(
+            src_ref=source,
+            dst_ref=target,
+            send_sem=sent_now,
+            recv_sem=got_now,
+            device_id={"dom": lax.rem(me + k, count)},
+            device_id_type=pl.DeviceIdType.MESH,
+        )
+        copy.start()
+        return copy
+
+    ghost_copies = [
+        send(ghosts.at[:, pl.ds(half, half)], lower, 1, sent.at[0], got.at[0]),
+        send(ghosts.at[:, pl.ds(0, half)], upper, count - 1, sent.at[count], got.at[count]),
+    ]
+    term_copies = [send(partial, parts.at[me], k, sent.at[k], got.at[k]) for k in range(1, count)]
+
     zero8 = jnp.zeros((8, LANES), f32)
     one8 = jnp.ones((8, LANES), f32)
     for f in (13, 14, 15):
@@ -207,41 +245,63 @@
 
         return block
 
-    lax.fori_loop(0, 16, ghost_block(lower, lower_q, TILES), 0)
-    lax.fori_loop(0, 16, ghost_block(upper, upper_q, TILES + 128), 0)
+    for copy in ghost_copies:
+        copy.wait()
+    if last:
+        charge_of = (lower_q, upper_q)
+    else:
+        charge_of = (lower.at[3], upper.at[3])
+        kept_q[0][...] = lower[3]
+        kept_q[1][...] = upper[3]
+    lax.fori_loop(0, 16, ghost_block(lower, charge_of[0], TILES), 0)
+    lax.fori_loop(0, 16, ghost_block(upper, charge_of[1], TILES + 128), 0)
 
     def contract(a, b, left, right):
         return lax.dot_general(a, b, (((left,), (right,)), ((), ())), preferred_element_type=f32)
 
-    def tiles(n, carry):
-        found = []
-        for u in range(TILES_AT_ONCE):
-            tile = n * TILES_AT_ONCE + u
-            one, two = pairs[2 * tile], pairs[2 * tile + 1]
-            near = jnp.concatenate([feat_j[one], feat_j[two]], axis=1)
-            spread = contract(jnp.concatenate([near] * 3, axis=0), feat_i[tile], 0, 0)
-            found.append((tile, one, two, spread))
-        done = []
-        for tile, one, two, spread in found:
-            weight = pl.reciprocal(spread * spread, approx=True)
-            high = weight.astype(bf16)
-            low = (weight - high.astype(f32)).astype(bf16)
-            near = jnp.concatenate([feat_a[one], feat_a[two]], axis=1)
-            done.append(
-                (
-                    tile,
-                    contract(
-                        jnp.concatenate([near, near], axis=1), jnp.concatenate([high, low], axis=0), 1, 0
-                    ),
-                )
-            )
-        for tile, value in done:
-            sums[pl.ds(pl.multiple_of(tile * 16, 16), 16), :] = value
+    def listed(tile):
+        tile = jnp.minimum(tile, TILES - 1)
+        return tile, pairs[2 * tile], pairs[2 * tile + 1]
+
+    def spread_of(tile):
+        tile, one, two = listed(tile)
+        near = jnp.concatenate([feat_j[one], feat_j[two]], axis=1)
+        return contract(jnp.concatenate([near] * 3, axis=0), feat_i[tile], 0, 0)
+
+    def force_of(tile, spread):
+        tile, one, two = listed(tile)
+        weight = pl.reciprocal(spread * spread, approx=True)
+        high = weight.astype(bf16)
+        low = (weight - high.astype(f32)).astype(bf16)
+        near = jnp.concatenate([feat_a[one], feat_a[two]], axis=1)
+        return contract(jnp.concatenate([near, near], axis=1), jnp.concatenate([high, low], axis=0), 1, 0)
+
+    many = TILES_AT_ONCE
+    for u in range(many):
+        spread_a[u] = spread_of(u)
+
+    def tiles(m, carry):
+        for now, later, n in ((spread_a, spread_b, 2 * m), (spread_b, spread_a, 2 * m + 1)):
+            done = []
+            for u in range(many):
+                later[u] = spread_of((n + 1) * many + u)
+                done.append(force_of(n * many + u, now[u]))
+            for u in range(many):
+                sums[pl.ds(pl.multiple_of((n * many + u) * 16, 16), 16), :] = done[u]
         return carry
 
-    lax.fori_loop(0, TILES // TILES_AT_ONCE, tiles, 0)
-
-    def combine(b, carry):
+    lax.fori_loop(0, TILES // many // 2, tiles, 0)
+
+    def total_of(terms, own, copies):
+        for copy in copies:
+            copy.wait()
+        terms[me] = own[...]
+        return jnp.sum(terms[...])
+
+    progress = total_of(parts, partial, term_copies)
+    pull = scalars[0] * (progress - scalars[1])
+
+    def combine(b, part):
         base = pl.multiple_of(b * 8, 8)
         here = pl.ds(base, 8)
         total = []
@@ -251,19 +311,47 @@
             value = value + sums[pl.ds(base * 16 + 8 + k, 8, stride=16), :]
             total.append(value)
         q = charges[here, :]
+        weight = path_weight[here, :]
+        rate = time_step * inv_mass[here, :]
         for c in range(3):
-            force[c, here, :] = q * (position[c, here, :] * total[0] - total[c + 1])
-        return carry
-
-    lax.fori_loop(0, TILES // 8, combine, 0)
-
-
-def pair_forces(pairs, position, charges, lower, upper, lower_q, upper_q):
+            old = position[c, here, :]
+            force = q * (old * total[0] - total[c + 1])
+            if c == 2:
+                force = force - pull * weight
+            moved = velocity[c, here, :] + rate * force
+            placed = old + time_step * moved
+            new_velocity[c, here, :] = moved
+            new_position[c, here, :] = placed
+        return part + weight * placed
+
+    ending = lax.fori_loop(0, TILES // 8, combine, jnp.zeros((8, LANES), f32))
+    if last:
+        partial_last = spread_a.at[0, pl.ds(0, 8), :]
+        spread_a[0, pl.ds(0, 8), :] = ending
+        final_copies = [
+            send(partial_last, final.at[me], k, sent_last.at[k], got_last.at[k]) for k in range(1, count)
+        ]
+        off = total_of(final, partial_last, final_copies) - scalars[1]
+        result[...] = jnp.full((8, LANES), 0.5 * scalars[0] * off * off, f32)
+    else:
+        result[...] = ending
+
+
+def step(number, last, scalars, pairs, ghosts, partial, position, velocity, charges, lower_q, upper_q, inv_mass, path_weight):
+    count = lax.axis_size("dom")
+    comps, rows = ghosts.shape[:2]
+    whole = jax.ShapeDtypeStruct((3, TILES, LANES), f32)
+    side_q = jax.ShapeDtypeStruct((rows // 2, LANES), f32)
+    kept = () if last else (side_q, side_q)
+
+    def kernel(*refs):
+        step_kernel(count, last, *refs)
+
     return pl.pallas_call(
-        force_kernel,
-        out_shape=jax.ShapeDtypeStruct((3, TILES, LANES), f32),
-        in_specs=[SMEM] + [VMEM] * 6,
-        out_specs=VMEM,
+        kernel,
+        out_shape=(whole, whole, jax.ShapeDtypeStruct((8, LANES), f32)) + kept,
+        in_specs=[SMEM] * 2 + [VMEM] * 9,
+        out_specs=(VMEM,) * (3 + len(kept)),
         scratch_shapes=[
             pltpu.VMEM((8 * 16, LANES), f32),
             pltpu.VMEM((8 * 48, LANES), f32),
@@ -272,75 +360,41 @@
             pltpu.VMEM((TILES, 48, LANES), bf16),
             pltpu.VMEM((TILES + 256, 16, LANES), bf16),
             pltpu.VMEM((TILES * 16, LANES), f32),
+            pltpu.VMEM((TILES_AT_ONCE, 2 * LANES, LANES), f32),
+            pltpu.VMEM((TILES_AT_ONCE, 2 * LANES, LANES), f32),
+            pltpu.VMEM((comps, rows // 2, LANES), f32),
+            pltpu.VMEM((comps, rows // 2, LANES), f32),
+            pltpu.VMEM((count, 8, LANES), f32),
+            pltpu.VMEM((count, 8, LANES), f32),
+            pltpu.SemaphoreType.DMA((count + 1,)),
+            pltpu.SemaphoreType.DMA((count + 1,)),
+            pltpu.SemaphoreType.DMA((count,)),
+            pltpu.SemaphoreType.DMA((count,)),
         ],
-        compiler_params=params(),
-        name="pair_forces",
-    )(pairs, position, charges, lower, upper, lower_q, upper_q)
-
-
-def advance(scalars, position, velocity, force, inv_mass, path_weight, new_position, new_velocity):
-    weight = path_weight[...]
-    rate = time_step * inv_mass[...]
-    pull = scalars[0] * (scalars[1] - scalars[2])
-    for c in range(3):
-        total = force[c]
-        if c == 2:
-            total = total - pull * weight
-        moved = velocity[c] + rate * total
-        new_velocity[c] = moved
-        new_position[c] = position[c] + time_step * moved
-    return jnp.sum((weight * new_position[2]).reshape(64, 8, LANES), axis=0)
-
-
-def middle_kernel(
-    scalars, position, velocity, force, inv_mass, path_weight, source, place, span, cell_rows,
-    new_position, new_velocity, ghosts, partial, listed,
-):
-    partial[...] = advance(scalars, position, velocity, force, inv_mass, path_weight, new_position, new_velocity)
-
+        compiler_params=pltpu.CompilerParams(
+            vmem_limit_bytes=58 * 1024 * 1024, collective_id=number, has_side_effects=True
+        ),
+        name="step",
+    )(scalars, pairs, ghosts, partial, position, velocity, charges, lower_q, upper_q, inv_mass, path_weight)
+
+
+def second_gather_kernel(position, source, place, span, cell_rows, ghosts, listed):
     def read_row(c, r):
-        return new_position[c, pl.ds(r, 1), :]
+        return position[c, pl.ds(r, 1), :]
 
     gather_stages(3, read_row, source, place, span, cell_rows, listed, ghosts)
 
 
-def last_kernel(scalars, position, velocity, force, inv_mass, path_weight, new_position, new_velocity, partial):
-    partial[...] = advance(scalars, position, velocity, force, inv_mass, path_weight, new_position, new_velocity)
-
-
-def middle_update(scalars, position, velocity, force, inv_mass, path_weight, plan):
-    whole = jax.ShapeDtypeStruct((3, TILES, LANES), f32)
+def second_gather(position, plan):
     return pl.pallas_call(
-        middle_kernel,
-        out_shape=(
-            whole,
-            whole,
-            jax.ShapeDtypeStruct((3, GHOST_ROWS, LANES), f32),
-            jax.ShapeDtypeStruct((8, LANES), f32),
-        ),
-        in_specs=[SMEM] + [VMEM] * 7 + [SMEM] * 2,
-        out_specs=(VMEM,) * 4,
+        second_gather_kernel,
+        out_shape=jax.ShapeDtypeStruct((3, GHOST_ROWS, LANES), f32),
+        in_specs=[VMEM] * 3 + [SMEM] * 2,
+        out_specs=VMEM,
         scratch_shapes=[pltpu.VMEM((3, GHOST_ROWS, LANES), f32)],
         compiler_params=params(),
-        name="middle_update",
-    )(scalars, position, velocity, force, inv_mass, path_weight, *plan)
-
-
-def last_update(scalars, position, velocity, force, inv_mass, path_weight):
-    whole = jax.ShapeDtypeStruct((3, TILES, LANES), f32)
-    return pl.pallas_call(
-        last_kernel,
-        out_shape=(whole, whole, jax.ShapeDtypeStruct((8, LANES), f32)),
-        in_specs=[SMEM] + [VMEM] * 5,
-        out_specs=(VMEM,) * 3,
-        compiler_params=params(),
-        name="last_update",
-    )(scalars, position, velocity, force, inv_mass, path_weight)
-
-
-def passed_along(shard, axis, by):
-    count = lax.axis_size(axis)
-    return lax.ppermute(shard, axis, [(i, (i + by) % count) for i in range(count)])
+        name="second_gather",
+    )(position, *plan)
 
 
 def shifted(shard, axis, by):
@@ -372,27 +426,21 @@
     center = bias_center[0]
     spring = bias_spring[0]
 
-    half = GHOST_ROWS // 2
+    scalars = jnp.stack([spring, center])
     ghosts, partial = first_gather(position, charges, path_weight, plan)
-    lower = passed_along(ghosts[:, half:], "dom", 1)
-    upper = passed_along(ghosts[:, :half], "dom", -1)
-    lower_q, upper_q = lower[3], upper[3]
+    lower_q = upper_q = jnp.zeros((GHOST_ROWS // 2, LANES), f32)
     for step_index in range(STEPS):
-        progress = lax.psum(jnp.sum(partial), "dom")
-        force = pair_forces(pairs, position, charges, lower, upper, lower_q, upper_q)
-        scalars = jnp.stack([spring, progress, center])
-        if step_index < STEPS - 1:
-            position, velocity, ghosts, partial = middle_update(
-                scalars, position, velocity, force, inv_mass, path_weight, plan
-            )
-            lower = passed_along(ghosts[:, half:], "dom", 1)
-            upper = passed_along(ghosts[:, :half], "dom", -1)
-        else:
-            position, velocity, partial = last_update(scalars, position, velocity, force, inv_mass, path_weight)
-    progress = lax.psum(jnp.sum(partial), "dom")
-    energy = 0.5 * spring * (progress - center) ** 2
+        last = step_index == STEPS - 1
+        position, velocity, partial, *kept_q = step(
+            step_index, last, scalars, pairs, ghosts, partial, position, velocity,
+            charges, lower_q, upper_q, inv_mass, path_weight,
+        )
+        if not last:
+            lower_q, upper_q = kept_q
+            ghosts = second_gather(position, plan)
+    energy = partial[0, :1]
     atoms = TILES * LANES
-    return position.reshape(1, 3, atoms), velocity.reshape(1, 3, atoms), energy[None]
+    return position.reshape(1, 3, atoms), velocity.reshape(1, 3, atoms), energy
 
 
 def solution(mesh):

time: 248 us -> 164 us (0.66)
  blocking collectives: 66.4 us -> 0 us
  starting transfers between devices: 24.3 us -> 11.2 us
  other arithmetic: 25.7 us -> 22.4 us
    psum x3 -> x0, blocking collectives: 66.4 us -> none  [body(): progress = lax.psum(jnp.sum(partial), 'dom')]
    ppermute x4 -> x0, starting transfers between devices: 11.4 us -> none  [passed_along(): lax.ppermute(shard, axis, [(i, (i + by) % count) for i in range(count)])]
    unnamed x21 -> x15, local copies, waits for them, and re-layouts: 0.99 us -> 3.89 us
    pallas_call x4 -> x3, Pallas kernels: 103 us -> 99.9 us  [the longest x2 84.2 us: step(): pl.pallas_call(kernel, out_shape=(whole, whole, jax.ShapeDtypeStruct((8,...]
    reduce_sum x3 -> x0, other arithmetic: 2.49 us -> none  [body(): progress = lax.psum(jnp.sum(partial), 'dom')]
  transfers between devices with their start and end apart: 8 -> 4, of which waited for: 0 -> 0; matrix products, arithmetic and copies ran while one was open for 11% -> 15% of each run, Pallas kernels for 7% -> 12%
where the time goes in v3:
time: 164 us; the launch traced here: 163 us
  Pallas kernels  119 us (73%)
  other arithmetic  22.4 us (14%)
  starting transfers between devices  11.2 us (7%)
  local copies, waits for them, and re-layouts  7.51 us (5%)
  between operations  2.76 us (2%)
    pallas_call x2, Pallas kernels, step(): pl.pallas_call(kernel, out_shape=(whole, whole, jax.ShapeDtypeStruct((8,...  84.2 us
    pallas_call x1, Pallas kernels, first_gather(): pl.pallas_call(first_gather_kernel, out_shape=(jax.ShapeDtypeStruct((4, G...  18.9 us
    pallas_call x1, Pallas kernels, second_gather(): pl.pallas_call(second_gather_kernel, out_shape=jax.ShapeDtypeStruct((3, G...  15.7 us
    ppermute x4, starting transfers between devices, shifted(): return lax.ppermute(shard, axis, pairs)  11.2 us
    sort x1, other arithmetic, plan_halo(): key, = lax.sort((key,), num_keys=1, is_stable=False)  7.31 us
    sort x1, other arithmetic, plan_halo(): back, = lax.sort((back,), num_keys=1, is_stable=False)  7.31 us
    unnamed x15, local copies, waits for them, and re-layouts  3.89 us
  transfers between devices with their start and end apart: 4, of which 0 were waited for; matrix products, arithmetic and copies ran while one was open for 15% of the time, Pallas kernels for 12%

profile of v3, /device:TPU:96, one launch (start us, length us, event | category | flops | bytes accessed | tf_op | source)
XLA Modules:
  0.0 162.6 jit_solution(2384350234099410780)
XLA Ops:
  0.6 2.8 %collective-permute-start.1 = (f32[3,512,128]{2,1,0:T(8,128)}, f32[3,512,128]{2,1,0:T(8,128)S(1)}, u32[]{:S(2)}, u32[]{:S(2)}) collective-permute-start(f32[3,512,128]{2,1,0:T(8,128)} %bitcast.34), channel_id=1, source_target_pairs={{8,0},{16,8},{24,16},{32,24},{40,32},{48,40},{56,48},{64,56},{72,6... | collective-permute-start | bytes 2359304 | tf_op jit(solution)/shard_map/ppermute | solution.py:403
  3.4 1.9 %collective-permute-start = (f32[3,512,128]{2,1,0:T(8,128)}, f32[3,512,128]{2,1,0:T(8,128)}, u32[]{:S(2)}, u32[]{:S(2)}) collective-permute-start(f32[3,512,128]{2,1,0:T(8,128)} %bitcast.35), channel_id=1, source_target_pairs={{0,8},{8,16},{16,24},{24,32},{32,40},{40,48},{48,56},{56,64},{64,7... | collective-permute-start | bytes 2359304 | tf_op jit(solution)/shard_map/ppermute | solution.py:403
  5.3 4.5 %collective-permute-start.3 = (f32[3,512,128]{2,1,0:T(8,128)}, f32[3,512,128]{2,1,0:T(8,128)S(1)}, u32[]{:S(2)}, u32[]{:S(2)}) collective-permute-start(f32[3,512,128]{2,1,0:T(8,128)} %bitcast.37), channel_id=1, source_target_pairs={{8,0},{16,8},{24,16},{32,24},{40,32},{48,40},{56,48},{64,56},{72,6... | collective-permute-start | bytes 2359304 | tf_op jit(solution)/shard_map/ppermute | solution.py:403
  9.9 1.9 %collective-permute-start.2 = (f32[3,512,128]{2,1,0:T(8,128)}, f32[3,512,128]{2,1,0:T(8,128)S(1)}, u32[]{:S(2)}, u32[]{:S(2)}) collective-permute-start(f32[3,512,128]{2,1,0:T(8,128)} %bitcast.38), channel_id=1, source_target_pairs={{0,8},{8,16},{16,24},{24,32},{32,40},{40,48},{48,56},{56,64},{64,7... | collective-permute-start | bytes 2359304 | tf_op jit(solution)/shard_map/ppermute | solution.py:403
  11.8 1.0 broadcast_shift-right-arithmetic_fusion.1
  15.0 7.3 %sort.14 = s32[32768]{0:T(1024)S(1)} sort(s32[32768]{0:T(1024)S(1)} %or_or_fusion), dimensions={0}, to_apply=%region_0.0 | sort | flops 491520 | bytes 262144 | tf_op jit(solution)/shard_map/sort | solution.py:32
  22.3 0.7 broadcast_shift-right-arithmetic_fusion
  23.1 0.8 slice_reduce_fusion.1
  23.9 0.6 pad_maximum_fusion.refs_0_
  25.1 0.8 copy.21
  25.9 0.8 reshape.87.refs_1_
  26.7 7.3 %sort.15 = s32[32768]{0:T(1024)S(1)} sort(s32[32768]{0:T(1024)S(1)} %get-tuple-element.41), dimensions={0}, to_apply=%region_1.0 | sort | flops 491520 | bytes 262144 | tf_op jit(solution)/shard_map/sort | solution.py:36
  34.6 0.6 pad_add_fusion.cell_rows
  35.2 0.7 and_bitcast_fusion.place
  35.9 2.1 %select_select_fusion.1.position.refs_4_ = f32[3,512,128]{2,1,0:T(8,128)} fusion(f32[3,512,128]{2,1,0:T(8,128)} %collective-permute-done, f32[3,512,128]{2,1,0:T(8,128)S(1)} %collective-permute-done.1, f32[3,512,128]{2,1,0:T(8,128)S(1)} %bitcast.36, pred[]{:T(512)S(6)} %eq.22, pred[]{:T(512)S(6)} %eq.10), kind=kLoop, calls=%fused_computation.5 | loop fusion | flops 393216 | bytes 3145730 | tf_op jit(solution)/shard_map/jit(_where)/select_n | solution.py:417
  38.0 18.9 %first_gather.1 = (f32[4,256,128]{2,1,0:T(8,128)}, f32[8,128]{1,0:T(8,128)}) custom-call(f32[3,512,128]{2,1,0:T(8,128)} %select_select_fusion.1.position.refs_4_, f32[512,128]{1,0:T(8,128)} %bitcast.24, f32[512,128]{1,0:T(8,128)} %bitcast.27, s32[256,128]{1,0:T(8,128)} %get-tuple-element.42.source, s32[256,128]{1,0:T(8,128)} %and_bitcast_fusion.place, ...), custom_call_target="tpu_custom_call" | custom-call | tf_op jit(solution)/shard_map/first_gather/pallas_call | solution.py:135
  56.9 1.0 select_select_fusion.refs_5_
  57.9 0.6 broadcast_in_dim.2.refs_7_.refs_8_
  58.5 40.4 %step.2 = (f32[3,512,128]{2,1,0:T(8,128)}, f32[3,512,128]{2,1,0:T(8,128)}, f32[8,128]{1,0:T(8,128)}, f32[128,128]{1,0:T(8,128)}, f32[128,128]{1,0:T(8,128)}) custom-call(f32[2]{0:T(128)} %pad_maximum_fusion.refs_0_, s32[1024]{0:T(1024)} %reshape.87.refs_1_, f32[4,256,128]{2,1,0:T(8,128)} %get-tuple-element.13.refs_2_, f32[8,128]{1,0:T(8,128)} %get-tuple-element.14.refs_3_, ...), custom_call_target="tpu_custom_call" | custom-call | tf_op jit(solution)/shard_map/step/pallas_call | solution.py:350
  98.9 15.7 %second_gather.1.refs_2_ = f32[3,256,128]{2,1,0:T(8,128)} custom-call(f32[3,512,128]{2,1,0:T(8,128)} %get-tuple-element.15.position.refs_4_, s32[256,128]{1,0:T(8,128)} %get-tuple-element.42.source, s32[256,128]{1,0:T(8,128)} %and_bitcast_fusion.place, s32[2,32]{1,0:T(2,128)} %pad_add_fusion.1.span, s32[2,512]{1,0:T(2,128)} %pad_add_fusion.cell_rows), custom_call_target="tpu_custom_call" | custom-call | tf_op jit(solution)/shard_map/second_gather/pallas_call | solution.py:389
  114.5 43.9 %step.3 = (f32[3,512,128]{2,1,0:T(8,128)}, f32[3,512,128]{2,1,0:T(8,128)}, f32[8,128]{1,0:T(8,128)}) custom-call(f32[2]{0:T(128)} %pad_maximum_fusion.refs_0_, s32[1024]{0:T(1024)} %reshape.87.refs_1_, f32[3,256,128]{2,1,0:T(8,128)} %second_gather.1.refs_2_, f32[8,128]{1,0:T(8,128)} %get-tuple-element.16.refs_3_, ...), custom_call_target="tpu_custom_call" | custom-call | tf_op jit(solution)/shard_map/step/pallas_call | solution.py:350
  158.4 1.2 slice.11
  159.6 2.1 %copy.31 = f32[1,3,65536]{2,0,1:T(1,128)} copy(f32[1,3,65536]{2,0,1:T(1,128)} %bitcast.33) | data formatting | bytes 1572864
  161.7 0.9 copy.32
  (25 shorter events, 1.5 us)
Async XLA Ops:
  0.6 35.2 %collective-permute-start.1 = (f32[3,512,128]{2,1,0:T(8,128)}, f32[3,512,128]{2,1,0:T(8,128)S(1)}, u32[]{:S(2)}, u32[]{:S(2)}) collective-permute-start(f32[3,512,128]{2,1,0:T(8,128)} %bitcast.34), channel_id=1, source_target_pairs={{8,0},{16,8},{24,16},{32,24},{40,32},{48,40},{56,48},{64,56},{72,6... | collective-permute-start | bytes 2359304 | tf_op jit(solution)/shard_map/ppermute | solution.py:403
  3.4 32.5 %collective-permute-start = (f32[3,512,128]{2,1,0:T(8,128)}, f32[3,512,128]{2,1,0:T(8,128)}, u32[]{:S(2)}, u32[]{:S(2)}) collective-permute-start(f32[3,512,128]{2,1,0:T(8,128)} %bitcast.35), channel_id=1, source_target_pairs={{0,8},{8,16},{16,24},{24,32},{32,40},{40,48},{48,56},{56,64},{64,7... | collective-permute-start | bytes 2359304 | tf_op jit(solution)/shard_map/ppermute | solution.py:403
  5.3 51.5 %collective-permute-start.3 = (f32[3,512,128]{2,1,0:T(8,128)}, f32[3,512,128]{2,1,0:T(8,128)S(1)}, u32[]{:S(2)}, u32[]{:S(2)}) collective-permute-start(f32[3,512,128]{2,1,0:T(8,128)} %bitcast.37), channel_id=1, source_target_pairs={{8,0},{16,8},{24,16},{32,24},{40,32},{48,40},{56,48},{64,56},{72,6... | collective-permute-start | bytes 2359304 | tf_op jit(solution)/shard_map/ppermute | solution.py:403
  9.9 47.0 %collective-permute-start.2 = (f32[3,512,128]{2,1,0:T(8,128)}, f32[3,512,128]{2,1,0:T(8,128)S(1)}, u32[]{:S(2)}, u32[]{:S(2)}) collective-permute-start(f32[3,512,128]{2,1,0:T(8,128)} %bitcast.38), channel_id=1, source_target_pairs={{0,8},{8,16},{16,24},{24,32},{32,40},{40,48},{48,56},{56,64},{64,7... | collective-permute-start | bytes 2359304 | tf_op jit(solution)/shard_map/ppermute | solution.py:403
  23.0 12.8 %copy-start.1 = (f32[1,3,65536]{2,0,1:T(1,128)S(1)}, f32[1,3,65536]{2,0,1:T(1,128)}, u32[]{:S(2)}) copy-start(f32[1,3,65536]{2,0,1:T(1,128)} %param.10) | copy-start | bytes 2359300
  23.8 10.2 %copy-start.3 = (s32[32]{0:T(128)S(1)}, s32[32]{0:T(128)}, u32[]{:S(2)}) copy-start(s32[32]{0:T(128)} %get-tuple-element.35) | copy-start | bytes 388
  23.8 10.2 %copy-start.4 = (s32[32]{0:T(128)S(1)}, s32[32]{0:T(128)}, u32[]{:S(2)}) copy-start(s32[32]{0:T(128)} %get-tuple-element.36) | copy-start | bytes 388
  38.0 18.9 %copy-start.2 = (f32[1,3,65536]{2,0,1:T(1,128)S(1)}, f32[1,3,65536]{2,0,1:T(1,128)}, u32[]{:S(2)}) copy-start(f32[1,3,65536]{2,0,1:T(1,128)} %param.11) | copy-start | bytes 2359300
  159.6 2.1 %copy-start = (f32[3,512,128]{2,1,0:T(8,128)S(1)}, f32[3,512,128]{2,1,0:T(8,128)}, u32[]{:S(2)}) copy-start(f32[3,512,128]{2,1,0:T(8,128)} %get-tuple-element.21) | copy-start | bytes 2359300

commit v4 on v3

--- a/solution.py
+++ b/solution.py
@@ -12,6 +12,7 @@
 GROUPS = 16
 GROUP_ROWS = 32
 CELLS = 32
+CAPACITY = 4096
 TILES_AT_ONCE = 16
 time_step = 0.1
 f32 = jnp.float32
@@ -24,126 +25,220 @@
     return pltpu.CompilerParams(vmem_limit_bytes=58 * 1024 * 1024)
 
 
-def plan_halo(halo_index):
-    index = halo_index.reshape(-1)
-    count = index.shape[0]
-    slot = lax.iota(jnp.int32, count)
-    key = ((index >> 12) << 27) | (slot << 12) | (index & 4095)
-    (key,) = lax.sort((key,), num_keys=1, is_stable=False)
-    group = key >> 27
-    source = (group << 12) | (key & 4095)
-    back = (((key >> 12) & (count - 1)) << 15) | slot
-    (back,) = lax.sort((back,), num_keys=1, is_stable=False)
-    place = back & (count - 1)
-    block_group = (index >> 12).reshape(CELLS, count // CELLS)
-    counts = jnp.sum(
-        (block_group[None] == lax.iota(jnp.int32, GROUPS)[:, None, None]).astype(jnp.int32), axis=2
-    ).reshape(-1)
-    cells = GROUPS * CELLS
-    before = (lax.iota(jnp.int32, cells)[:, None] > lax.iota(jnp.int32, cells)[None, :]).astype(jnp.int32)
-    starts = jnp.sum(before * counts[None, :], axis=1)
-    first_row = jnp.minimum(starts >> 7, GHOST_ROWS - 1)
-    last_row = jnp.maximum(starts + counts - 1, starts) >> 7
-    last_row = jnp.minimum(last_row, GHOST_ROWS - 1)
-    ranges = group.reshape(GHOST_ROWS // 8, 1024)
-    return (
-        source.reshape(GHOST_ROWS, LANES),
-        place.reshape(GHOST_ROWS, LANES),
-        jnp.stack([ranges[:, 0], ranges[:, -1]]),
-        jnp.stack([first_row, last_row]),
-    )
-
-
-def gather_stages(comps, read_row, source, place, span, cell_rows, listed, out):
-    def list_block(v, carry):
-        base = pl.multiple_of(v * 8, 8)
-        src = source[pl.ds(base, 8), :]
-        lane = src & 127
-        row = src >> 7
-
-        def one_group(group, accs):
-            first = pl.multiple_of(group * GROUP_ROWS, GROUP_ROWS)
-            accs = list(accs)
+def start_kernel(
+    count, position, halo, below, above, source, place, cells, sent, got,
+):
+    me = lax.axis_index("rep")
+    ahead, behind = lax.rem(me + 1, count), lax.rem(me + count - 1, count)
+    barrier = pltpu.get_barrier_semaphore()
+    for other in (ahead, behind):
+        pl.semaphore_signal(barrier, inc=1, device_id={"rep": other}, device_id_type=pl.DeviceIdType.MESH)
+    pl.semaphore_wait(barrier, 2)
+    copies = []
+    for n, (other, target) in enumerate(((ahead, below), (behind, above))):
+        copy = pltpu.make_async_remote_copy(
+            src_ref=position,
+            dst_ref=target,
+            send_sem=sent.at[n],
+            recv_sem=got.at[n],
+            device_id={"rep": other},
+            device_id_type=pl.DeviceIdType.MESH,
+        )
+        copy.start()
+        copies.append(copy)
+
+    shape = (GHOST_ROWS, LANES)
+    row = lax.broadcasted_iota(jnp.int32, shape, 0)
+    lane = lax.broadcasted_iota(jnp.int32, shape, 1)
+    wide = (LANES, 2 * LANES)
+    across = lax.broadcasted_iota(jnp.int32, wide, 1)
+    ahead_lane = (lax.broadcasted_iota(jnp.int32, wide, 0) < across) | (across >= LANES)
+    ahead_lane = jnp.where(ahead_lane, 1.0, 0.0).astype(bf16)
+    square = (GHOST_ROWS, GHOST_ROWS)
+    ahead_row = lax.broadcasted_iota(jnp.int32, square, 1) < lax.broadcasted_iota(jnp.int32, square, 0)
+    ahead_row = jnp.where(ahead_row, 1.0, 0.0).astype(bf16)
+    place[...] = jnp.zeros(shape, jnp.int32)
+
+    def one_group(group, carry):
+        index = halo[...]
+        member = (index >> 12) == group
+        flag = jnp.where(member, 1.0, 0.0).astype(bf16)
+        within = jnp.dot(flag, ahead_lane, preferred_element_type=f32)
+        in_row = within[:, LANES:]
+        earlier = jnp.dot(ahead_row, in_row.astype(bf16), preferred_element_type=f32)
+        rank = (within[:, :LANES] + earlier).astype(jnp.int32)
+        place[...] = jnp.where(member, rank + group * CAPACITY, place[...])
+        marks = jnp.where(lane * 8 == row, earlier, 0.0)
+        marks = marks + jnp.where((lane == CELLS) & (row == GHOST_ROWS - 1), earlier + in_row, 0.0)
+        marks = jnp.sum(marks.reshape(GHOST_ROWS // 8, 8, LANES), axis=0)
+        cells[pl.ds(pl.multiple_of(group * 8, 8), 8), :] = jnp.broadcast_to(
+            jnp.sum(marks, axis=0, keepdims=True), (8, LANES)
+        ).astype(jnp.int32)
+        shift = row * LANES + lane - rank
+        items = jnp.where(member, (1 << 28) | (shift << 12) | (index & 4095), 0)
+        for bit in range(15):
+            step_by = 1 << bit
+            if step_by < LANES:
+                following = pltpu.roll(items, items.shape[0] - 1, 0)
+                mixed = jnp.where(lane < step_by, following, items)
+                moved = pltpu.roll(mixed, LANES - step_by, 1)
+                held = items
+            else:
+                rows = step_by // LANES
+                if rows < 32:
+                    if rows < 8:
+                        moved = pltpu.roll(items, items.shape[0] - rows, 0)
+                    else:
+                        moved = jnp.concatenate([items[rows:], items[:rows]], axis=0)
+                    held = items
+                else:
+                    blocks = items.reshape(items.shape[0] // 64, 2, 32, LANES)
+                    held = blocks[:, 0].reshape(-1, LANES)
+                    moved = blocks[:, 1].reshape(-1, LANES)
+            mask = 1 << (12 + bit)
+            items = jnp.where((moved & mask) != 0, moved, jnp.where((held & mask) != 0, 0, held))
+        source[pl.ds(pl.multiple_of(group * 32, 32), 32), :] = items & 4095
+        return carry
+
+    lax.fori_loop(0, GROUPS, one_group, 0)
+    for copy in copies:
+        copy.wait()
+
+
+def start(position, halo, number):
+    count = lax.axis_size("rep")
+    whole = jax.ShapeDtypeStruct(position.shape, f32)
+
+    def kernel(*refs):
+        start_kernel(count, *refs)
+
+    anywhere = pl.BlockSpec(memory_space=pl.ANY)
+    return pl.pallas_call(
+        kernel,
+        out_shape=(
+            whole,
+            whole,
+            jax.ShapeDtypeStruct((GROUPS * 32, LANES), jnp.int32),
+            jax.ShapeDtypeStruct((GHOST_ROWS, LANES), jnp.int32),
+            jax.ShapeDtypeStruct((GROUPS * 8, LANES), jnp.int32),
+        ),
+        in_specs=[anywhere, VMEM],
+        out_specs=(anywhere, anywhere, VMEM, VMEM, VMEM),
+        scratch_shapes=[pltpu.SemaphoreType.DMA((2,)), pltpu.SemaphoreType.DMA((2,))],
+        compiler_params=pltpu.CompilerParams(
+            vmem_limit_bytes=32 * 1024 * 1024, collective_id=number, has_side_effects=True
+        ),
+        name="start",
+    )(position, halo)
+
+
+def gather_stages(comps, read_row, source, place, cells, listed, out):
+    zeros = (jnp.zeros((8, LANES), f32),) * comps
+
+    def one_group(group, carry):
+        first = pl.multiple_of(group * GROUP_ROWS, GROUP_ROWS)
+
+        def list_block(v, carry):
+            here = pl.ds(pl.multiple_of(first + v * 8, 8), 8)
+            src = source[here, :]
+            lane = src & 127
+            row = src >> 7
+            accs = list(zeros)
             for u in range(GROUP_ROWS):
-                here = row == first + u
+                mine = row == u
                 for c in range(comps):
                     line = jnp.broadcast_to(read_row(c, first + u), (8, LANES))
-                    accs[c] = jnp.where(here, jnp.take_along_axis(line, lane, axis=1), accs[c])
-            return tuple(accs)
-
-        zero = jnp.zeros((8, LANES), f32)
-        accs = lax.fori_loop(span[0, v], span[1, v] + 1, one_group, (zero,) * comps)
-        for c in range(comps):
-            listed[c, pl.ds(base, 8), :] = accs[c]
-        return carry
-
-    lax.fori_loop(0, GHOST_ROWS // 8, list_block, 0)
+                    accs[c] = jnp.where(mine, jnp.take_along_axis(line, lane, axis=1), accs[c])
+            for c in range(comps):
+                listed[c, here, :] = accs[c]
+            return carry
+
+        return lax.fori_loop(0, (cells[group * 8, CELLS] + 1023) >> 10, list_block, carry)
+
+    lax.fori_loop(0, GROUPS, one_group, 0)
 
     def slot_block(t, carry):
-        base = pl.multiple_of(t * 8, 8)
-        at = place[pl.ds(base, 8), :]
+        here = pl.ds(pl.multiple_of(t * 8, 8), 8)
+        at = place[here, :]
         lane = at & 127
         row = at >> 7
 
         def visit(r, accs):
-            here = row == r
+            mine = row == r
             return tuple(
                 jnp.where(
-                    here,
+                    mine,
                     jnp.take_along_axis(jnp.broadcast_to(listed[c, pl.ds(r, 1), :], (8, LANES)), lane, axis=1),
                     accs[c],
                 )
                 for c in range(comps)
             )
 
-        accs = (jnp.zeros((8, LANES), f32),) * comps
+        def rows_of(g):
+            begin, end = cells[g * 8, t], cells[g * 8, t + 1]
+            return g * 32 + jnp.minimum(begin >> 7, 31), g * 32 + (jnp.maximum(end - 1, begin) >> 7)
+
+        accs = zeros
         widest = 0
         for g in range(GROUPS):
-            first = cell_rows[0, g * CELLS + t]
-            last = cell_rows[1, g * CELLS + t]
+            first, last = rows_of(g)
+            last = jnp.minimum(last, g * 32 + 31)
             accs = visit(first, accs)
             accs = visit(last, accs)
             widest = jnp.maximum(widest, last - first)
         for c in range(comps):
-            out[c, pl.ds(base, 8), :] = accs[c]
+            out[c, here, :] = accs[c]
 
         @pl.when(widest > 1)
         def _():
             def rest(g, accs):
-                return lax.fori_loop(cell_rows[0, g * CELLS + t], cell_rows[1, g * CELLS + t] + 1, visit, accs)
-
-            more = lax.fori_loop(0, GROUPS, rest, tuple(out[c, pl.ds(base, 8), :] for c in range(comps)))
+                first, last = rows_of(g)
+                return lax.fori_loop(first, jnp.minimum(last, g * 32 + 31) + 1, visit, accs)
+
+            more = lax.fori_loop(0, GROUPS, rest, tuple(out[c, here, :] for c in range(comps)))
             for c in range(comps):
-                out[c, pl.ds(base, 8), :] = more[c]
+                out[c, here, :] = more[c]
 
         return carry
 
     lax.fori_loop(0, GHOST_ROWS // 8, slot_block, 0)
 
 
-def first_gather_kernel(position, charges, path_weight, source, place, span, cell_rows, ghosts, partial, listed):
+def pick(partner, window, own, below, above):
+    wanted = jnp.full(own.shape, partner, jnp.int32)
+    return jnp.where(wanted == window - 1, below, jnp.where(wanted == window + 1, above, own))
+
+
+def first_gather_kernel(
+    partner, cells, own, below, above, charges, path_weight, source, place, position, ghosts, partial, listed
+):
+    window = lax.axis_index("rep")
+    for c in range(3):
+        position[c] = pick(partner[0], window, own[c], below[c], above[c])
+
     def read_row(c, r):
         if c == 3:
             return charges[pl.ds(r, 1), :]
         return position[c, pl.ds(r, 1), :]
 
     partial[...] = jnp.sum((path_weight[...] * position[2]).reshape(64, 8, LANES), axis=0)
-    gather_stages(4, read_row, source, place, span, cell_rows, listed, ghosts)
-
-
-def first_gather(position, charges, path_weight, plan):
+    gather_stages(4, read_row, source, place, cells, listed, ghosts)
+
+
+def first_gather(partner, own, below, above, charges, path_weight, source, place, cells):
     return pl.pallas_call(
         first_gather_kernel,
         out_shape=(
+            jax.ShapeDtypeStruct((3, TILES, LANES), f32),
             jax.ShapeDtypeStruct((4, GHOST_ROWS, LANES), f32),
             jax.ShapeDtypeStruct((8, LANES), f32),
         ),
-        in_specs=[VMEM] * 5 + [SMEM] * 2,
-        out_specs=(VMEM, VMEM),
-        scratch_shapes=[pltpu.VMEM((4, GHOST_ROWS, LANES), f32)],
+        in_specs=[SMEM] * 2 + [VMEM] * 7,
+        out_specs=(VMEM,) * 3,
+        scratch_shapes=[pltpu.VMEM((4, GROUPS * 32, LANES), f32)],
         compiler_params=params(),
         name="first_gather",
-    )(position, charges, path_weight, *plan)
+    )(partner, cells, own, below, above, charges, path_weight, source, place)
 
 
 def parts3(value):
@@ -154,13 +249,14 @@
 
 
 def step_kernel(
-    count, last, scalars, pairs, ghosts, partial, position, velocity, charges, lower_q, upper_q, inv_mass, path_weight,
+    count, windows, last, scalars, partner, pairs, ghosts, partial, position, velocity, charges, lower_q, upper_q, inv_mass, path_weight,
     new_position, new_velocity, result, *rest,
 ):
     if last:
         kept_q = ()
     else:
         kept_q, rest = rest[:2], rest[2:]
+        rest, velocity_below, velocity_above, sent_v, got_v = rest[:-4], *rest[-4:]
     (
         rows_j, rows_i, rows_a, feat_j, feat_i, feat_a, sums, spread_a, spread_b,
         lower, upper, parts, final, sent, got, sent_last, got_last,
@@ -172,7 +268,14 @@
         pl.semaphore_signal(
             barrier, inc=1, device_id={"dom": lax.rem(me + k, count)}, device_id_type=pl.DeviceIdType.MESH
         )
-    pl.semaphore_wait(barrier, count - 1)
+    if last:
+        pl.semaphore_wait(barrier, count - 1)
+    else:
+        window = lax.axis_index("rep")
+        ahead, behind = lax.rem(window + 1, windows), lax.rem(window + windows - 1, windows)
+        for other in (ahead, behind):
+            pl.semaphore_signal(barrier, inc=1, device_id={"rep": other}, device_id_type=pl.DeviceIdType.MESH)
+        pl.semaphore_wait(barrier, count + 1)
 
     def send(source, target, k, sent_now, got_now):
         copy = pltpu.make_async_remote_copy(
@@ -191,6 +294,19 @@
         send(ghosts.at[:, pl.ds(0, half)], upper, count - 1, sent.at[count], got.at[count]),
     ]
     term_copies = [send(partial, parts.at[me], k, sent.at[k], got.at[k]) for k in range(1, count)]
+    velocity_copies = []
+    if not last:
+        for n, (other, target) in enumerate(((ahead, velocity_below), (behind, velocity_above))):
+            copy = pltpu.make_async_remote_copy(
+                src_ref=velocity,
+                dst_ref=target,
+                send_sem=sent_v.at[n],
+                recv_sem=got_v.at[n],
+                device_id={"rep": other},
+                device_id_type=pl.DeviceIdType.MESH,
+            )
+            copy.start()
+            velocity_copies.append(copy)
 
     zero8 = jnp.zeros((8, LANES), f32)
     one8 = jnp.ones((8, LANES), f32)
@@ -300,6 +416,14 @@
 
     progress = total_of(parts, partial, term_copies)
     pull = scalars[0] * (progress - scalars[1])
+    for copy in velocity_copies:
+        copy.wait()
+
+    def velocity_at(c, here):
+        own = velocity[c, here, :]
+        if last:
+            return own
+        return pick(partner[0], window, own, velocity_below[c, here, :], velocity_above[c, here, :])
 
     def combine(b, part):
         base = pl.multiple_of(b * 8, 8)
@@ -318,7 +442,7 @@
             force = q * (old * total[0] - total[c + 1])
             if c == 2:
                 force = force - pull * weight
-            moved = velocity[c, here, :] + rate * force
+            moved = velocity_at(c, here) + rate * force
             placed = old + time_step * moved
             new_velocity[c, here, :] = moved
             new_position[c, here, :] = placed
@@ -337,20 +461,26 @@
         result[...] = ending
 
 
-def step(number, last, scalars, pairs, ghosts, partial, position, velocity, charges, lower_q, upper_q, inv_mass, path_weight):
-    count = lax.axis_size("dom")
+def step(number, last, scalars, partner, pairs, ghosts, partial, position, velocity, charges, lower_q, upper_q, inv_mass, path_weight):
+    count, windows = lax.axis_size("dom"), lax.axis_size("rep")
     comps, rows = ghosts.shape[:2]
     whole = jax.ShapeDtypeStruct((3, TILES, LANES), f32)
     side_q = jax.ShapeDtypeStruct((rows // 2, LANES), f32)
     kept = () if last else (side_q, side_q)
+    carried = () if last else (
+        pltpu.VMEM(velocity.shape, f32),
+        pltpu.VMEM(velocity.shape, f32),
+        pltpu.SemaphoreType.DMA((2,)),
+        pltpu.SemaphoreType.DMA((2,)),
+    )
 
     def kernel(*refs):
-        step_kernel(count, last, *refs)
+        step_kernel(count, windows, last, *refs)
 
     return pl.pallas_call(
         kernel,
         out_shape=(whole, whole, jax.ShapeDtypeStruct((8, LANES), f32)) + kept,
-        in_specs=[SMEM] * 2 + [VMEM] * 9,
+        in_specs=[SMEM] * 3 + [VMEM] * 9,
         out_specs=(VMEM,) * (3 + len(kept)),
         scratch_shapes=[
             pltpu.VMEM((8 * 16, LANES), f32),
@@ -370,37 +500,32 @@
             pltpu.SemaphoreType.DMA((count + 1,)),
             pltpu.SemaphoreType.DMA((count,)),
             pltpu.SemaphoreType.DMA((count,)),
+            *carried,
         ],
         compiler_params=pltpu.CompilerParams(
             vmem_limit_bytes=58 * 1024 * 1024, collective_id=number, has_side_effects=True
         ),
         name="step",
-    )(scalars, pairs, ghosts, partial, position, velocity, charges, lower_q, upper_q, inv_mass, path_weight)
-
-
-def second_gather_kernel(position, source, place, span, cell_rows, ghosts, listed):
+    )(scalars, partner, pairs, ghosts, partial, position, velocity, charges, lower_q, upper_q, inv_mass, path_weight)
+
+
+def second_gather_kernel(cells, position, source, place, ghosts, listed):
     def read_row(c, r):
         return position[c, pl.ds(r, 1), :]
 
-    gather_stages(3, read_row, source, place, span, cell_rows, listed, ghosts)
-
-
-def second_gather(position, plan):
+    gather_stages(3, read_row, source, place, cells, listed, ghosts)
+
+
+def second_gather(position, source, place, cells):
     return pl.pallas_call(
         second_gather_kernel,
         out_shape=jax.ShapeDtypeStruct((3, GHOST_ROWS, LANES), f32),
-        in_specs=[VMEM] * 3 + [SMEM] * 2,
+        in_specs=[SMEM] + [VMEM] * 3,
         out_specs=VMEM,
-        scratch_shapes=[pltpu.VMEM((3, GHOST_ROWS, LANES), f32)],
+        scratch_shapes=[pltpu.VMEM((3, GROUPS * 32, LANES), f32)],
         compiler_params=params(),
         name="second_gather",
-    )(position, *plan)
-
-
-def shifted(shard, axis, by):
-    count = lax.axis_size(axis)
-    pairs = [(i, i + by) for i in range(count) if 0 <= i + by < count]
-    return lax.ppermute(shard, axis, pairs)
+    )(cells, position, source, place)
 
 
 def body(positions, velocities, charges, inv_mass, path_weight, halo_index, tile_pairs, partner, bias_center, bias_spring):
@@ -410,34 +535,22 @@
     inv_mass = inv_mass.reshape(TILES, LANES)
     path_weight = path_weight.reshape(TILES, LANES)
     pairs = tile_pairs.reshape(-1)
-    partner_now = partner[0]
-    window = lax.axis_index("rep")
-
-    def choose(own, below, above):
-        return jnp.where(partner_now == window - 1, below, jnp.where(partner_now == window + 1, above, own))
-
-    position_below = shifted(position, "rep", 1)
-    position_above = shifted(position, "rep", -1)
-    velocity_below = shifted(velocity, "rep", 1)
-    velocity_above = shifted(velocity, "rep", -1)
-    plan = plan_halo(halo_index)
-    position = choose(position, position_below, position_above)
-    velocity = choose(velocity, velocity_below, velocity_above)
-    center = bias_center[0]
-    spring = bias_spring[0]
-
-    scalars = jnp.stack([spring, center])
-    ghosts, partial = first_gather(position, charges, path_weight, plan)
+    halo = halo_index.reshape(GHOST_ROWS, LANES)
+    scalars = jnp.stack([bias_spring[0], bias_center[0]])
+    below, above, source, place, cells = start(position, halo, STEPS)
+    position, ghosts, partial = first_gather(
+        partner, position, below, above, charges, path_weight, source, place, cells
+    )
     lower_q = upper_q = jnp.zeros((GHOST_ROWS // 2, LANES), f32)
     for step_index in range(STEPS):
         last = step_index == STEPS - 1
         position, velocity, partial, *kept_q = step(
-            step_index, last, scalars, pairs, ghosts, partial, position, velocity,
+            step_index, last, scalars, partner, pairs, ghosts, partial, position, velocity,
             charges, lower_q, upper_q, inv_mass, path_weight,
         )
         if not last:
             lower_q, upper_q = kept_q
-            ghosts = second_gather(position, plan)
+            ghosts = second_gather(position, source, place, cells)
     energy = partial[0, :1]
     atoms = TILES * LANES
     return position.reshape(1, 3, atoms), velocity.reshape(1, 3, atoms), energy

time: 164 us -> 155 us (0.945)
  other arithmetic: 22.4 us -> 0.59 us
  Pallas kernels: 119 us -> 139 us
  starting transfers between devices: 11.2 us -> 0 us
  local copies, waits for them, and re-layouts: 7.51 us -> 11.2 us
    pallas_call x1 -> x2, Pallas kernels: 18.9 us -> 38.6 us  [the longest x1 19.9 us: start(): pl.pallas_call(kernel, out_shape=(whole, whole, jax.ShapeDtypeStruct((GRO...]
    sort x2 -> x0, other arithmetic: 14.6 us -> none  [the longest x1 7.31 us: plan_halo(): key, = lax.sort((key,), num_keys=1, is_stable=False)]
    ppermute x4 -> x0, starting transfers between devices: 11.2 us -> none  [shifted(): return lax.ppermute(shard, axis, pairs)]
    unnamed x15 -> x17, local copies, waits for them, and re-layouts: 3.89 us -> 7.58 us
    select_n x2 -> x0, other arithmetic: 3.12 us -> none  [choose(): jnp.where(partner_now == window - 1, below, jnp.where(partner_now == wind...]
    shift_right_arithmetic x2 -> x0, other arithmetic: 1.73 us -> none  [the longest x1 1.04 us: plan_halo(): key = index >> 12 << 27 | slot << 12 | index & 4095]
  transfers between devices with their start and end apart: 4 -> 0, of which waited for: 0 -> 0; matrix products, arithmetic and copies ran while one was open for 15% -> 0% of each run, Pallas kernels for 12% -> 0%
where the time goes in v4:
time: 155 us; the launch traced here: 153 us
  Pallas kernels  139 us (90%)
  local copies, waits for them, and re-layouts  11.2 us (7%)
  between operations  2.7 us (2%)
    pallas_call x2, Pallas kernels, step(): pl.pallas_call(kernel, out_shape=(whole, whole, jax.ShapeDtypeStruct((8,...  84.4 us
    pallas_call x1, Pallas kernels, start(): pl.pallas_call(kernel, out_shape=(whole, whole, jax.ShapeDtypeStruct((GRO...  19.9 us
    pallas_call x1, Pallas kernels, first_gather(): pl.pallas_call(first_gather_kernel, out_shape=(jax.ShapeDtypeStruct((3, T...  18.7 us
    pallas_call x1, Pallas kernels, second_gather(): pl.pallas_call(second_gather_kernel, out_shape=jax.ShapeDtypeStruct((3, G...  15.7 us
    unnamed x17, local copies, waits for them, and re-layouts  7.58 us

profile of v4, /device:TPU:96, one launch (start us, length us, event | category | flops | bytes accessed | tf_op | source)
XLA Modules:
  0.0 153.2 jit_solution(12607654096095896322)
XLA Ops:
  0.6 0.0 copy-start
  2.7 0.6 pad_maximum_fusion.refs_0_
  3.2 1.0 reshape.28.refs_1_
  4.3 0.8 copy.15
  5.1 0.8 reshape.27.refs_2_
  5.9 0.0 copy-done
  5.9 19.9 %start.1 = (f32[3,512,128]{2,1,0:T(8,128)S(1)}, f32[3,512,128]{2,1,0:T(8,128)S(1)}, s32[512,128]{1,0:T(8,128)S(1)}, s32[256,128]{1,0:T(8,128)S(1)}, s32[128,128]{1,0:T(8,128)S(1)}) custom-call(f32[3,512,128]{2,1,0:T(8,128)S(1)} %bitcast.9, s32[256,128]{1,0:T(8,128)S(1)} %reshape.28.refs_1_), custom_call_target="tpu_custom_call" | custom-call | tf_op jit(solution)/shard_map/start/pallas_call | solution.py:116
  25.7 0.0 copy-start.1
  25.7 0.7 copy-done.1
  26.4 0.0 copy-start.2
  26.4 0.9 copy-done.2
  27.3 0.0 copy-start.3
  27.3 0.9 copy-done.3
  28.2 0.7 copy-done.4
  28.9 0.6 copy-done.5
  29.5 18.7 %first_gather.1 = (f32[3,512,128]{2,1,0:T(8,128)}, f32[4,256,128]{2,1,0:T(8,128)}, f32[8,128]{1,0:T(8,128)}) custom-call(s32[1]{0:T(128)S(6)} %copy.20.partner.refs_1_, s32[128,128]{1,0:T(8,128)} %copy-done.5, f32[3,512,128]{2,1,0:T(8,128)} %bitcast.8, f32[3,512,128]{2,1,0:T(8,128)} %copy-done.2, f32[3,512,128]{2,1,0:T(8,128)} %copy-done.3, ...), custom_call_target="tpu_custom_call" | custom-call | tf_op jit(solution)/shard_map/first_gather/pallas_call | solution.py:229
  48.2 0.6 broadcast_in_dim.3.refs_8_.refs_9_
  48.8 41.6 %step.2 = (f32[3,512,128]{2,1,0:T(8,128)}, f32[3,512,128]{2,1,0:T(8,128)}, f32[8,128]{1,0:T(8,128)}, f32[128,128]{1,0:T(8,128)}, f32[128,128]{1,0:T(8,128)}) custom-call(f32[2]{0:T(128)} %pad_maximum_fusion.refs_0_, s32[1]{0:T(128)S(6)} %copy.20.partner.refs_1_, s32[1024]{0:T(1024)} %reshape.27.refs_2_, f32[4,256,128]{2,1,0:T(8,128)} %get-tuple-element.24.refs_3_, ...), custom_call_target="tpu_custom_call" | custom-call | tf_op jit(solution)/shard_map/step/pallas_call | solution.py:480
  90.4 15.7 %second_gather.1.refs_3_ = f32[3,256,128]{2,1,0:T(8,128)} custom-call(s32[128,128]{1,0:T(8,128)} %copy-done.5, f32[3,512,128]{2,1,0:T(8,128)} %get-tuple-element.27.position.refs_5_, s32[512,128]{1,0:T(8,128)} %copy-done.1, s32[256,128]{1,0:T(8,128)} %copy-done.4), custom_call_target="tpu_custom_call" | custom-call | tf_op jit(solution)/shard_map/second_gather/pallas_call | solution.py:520
  106.2 42.8 %step.3 = (f32[3,512,128]{2,1,0:T(8,128)}, f32[3,512,128]{2,1,0:T(8,128)}, f32[8,128]{1,0:T(8,128)}) custom-call(f32[2]{0:T(128)} %pad_maximum_fusion.refs_0_, s32[1]{0:T(128)S(6)} %copy.20.partner.refs_1_, s32[1024]{0:T(1024)} %reshape.27.refs_2_, f32[3,256,128]{2,1,0:T(8,128)} %second_gather.1.refs_3_, f32[8,128]{1,0:T(8,128)} %get-tuple-element.28.refs_4_, ...), custom_call_target="tpu_custom_call" | custom-call | tf_op jit(solution)/shard_map/step/pallas_call | solution.py:480
  149.0 1.2 slice.3
  150.2 2.1 %copy.23 = f32[1,3,65536]{2,0,1:T(1,128)} copy(f32[1,3,65536]{2,0,1:T(1,128)} %bitcast.19) | data formatting | bytes 1572864
  152.3 0.0 copy-done.6
  152.3 0.9 copy.24
  (3 shorter events, 0.0 us)
Async XLA Ops:
  0.6 5.2 %copy-start = (f32[1,3,65536]{2,0,1:T(1,128)S(1)}, f32[1,3,65536]{2,0,1:T(1,128)}, u32[]{:S(2)}) copy-start(f32[1,3,65536]{2,0,1:T(1,128)} %param.10) | copy-start | bytes 2359300
  25.7 0.7 copy-start.1
  26.4 0.9 copy-start.2
  27.3 0.9 copy-start.3
  28.2 0.7 copy-start.4
  28.9 0.6 copy-start.5
  150.2 2.1 %copy-start.6 = (f32[3,512,128]{2,1,0:T(8,128)S(1)}, f32[3,512,128]{2,1,0:T(8,128)}, u32[]{:S(2)}) copy-start(f32[3,512,128]{2,1,0:T(8,128)} %get-tuple-element.33) | copy-start | bytes 2359300

commit v5 on v4

--- a/solution.py
+++ b/solution.py
@@ -25,28 +25,7 @@
     return pltpu.CompilerParams(vmem_limit_bytes=58 * 1024 * 1024)
 
 
-def start_kernel(
-    count, position, halo, below, above, source, place, cells, sent, got,
-):
-    me = lax.axis_index("rep")
-    ahead, behind = lax.rem(me + 1, count), lax.rem(me + count - 1, count)
-    barrier = pltpu.get_barrier_semaphore()
-    for other in (ahead, behind):
-        pl.semaphore_signal(barrier, inc=1, device_id={"rep": other}, device_id_type=pl.DeviceIdType.MESH)
-    pl.semaphore_wait(barrier, 2)
-    copies = []
-    for n, (other, target) in enumerate(((ahead, below), (behind, above))):
-        copy = pltpu.make_async_remote_copy(
-            src_ref=position,
-            dst_ref=target,
-            send_sem=sent.at[n],
-            recv_sem=got.at[n],
-            device_id={"rep": other},
-            device_id_type=pl.DeviceIdType.MESH,
-        )
-        copy.start()
-        copies.append(copy)
-
+def plan_kernel(halo, charges, source, place, cells, ghost_q, counts, listed, raw, arrived):
     shape = (GHOST_ROWS, LANES)
     row = lax.broadcasted_iota(jnp.int32, shape, 0)
     lane = lax.broadcasted_iota(jnp.int32, shape, 1)
@@ -101,61 +80,74 @@
         return carry
 
     lax.fori_loop(0, GROUPS, one_group, 0)
-    for copy in copies:
-        copy.wait()
-
-
-def start(position, halo, number):
-    count = lax.axis_size("rep")
-    whole = jax.ShapeDtypeStruct(position.shape, f32)
-
-    def kernel(*refs):
-        start_kernel(count, *refs)
-
-    anywhere = pl.BlockSpec(memory_space=pl.ANY)
+    copy = pltpu.make_async_copy(cells, counts, arrived)
+    copy.start()
+    copy.wait()
+
+    def read_rows(c, rows):
+        return charges[rows, :]
+
+    gather_stages(1, read_rows, source, place, counts, listed, raw)
+    unmix(1, raw, lambda c, rows, value: ghost_q.__setitem__((rows, slice(None)), value))
+
+
+def plan(halo, charges):
+    table = (GROUPS * 8, LANES)
     return pl.pallas_call(
-        kernel,
+        plan_kernel,
         out_shape=(
-            whole,
-            whole,
             jax.ShapeDtypeStruct((GROUPS * 32, LANES), jnp.int32),
             jax.ShapeDtypeStruct((GHOST_ROWS, LANES), jnp.int32),
-            jax.ShapeDtypeStruct((GROUPS * 8, LANES), jnp.int32),
+            jax.ShapeDtypeStruct(table, jnp.int32),
+            jax.ShapeDtypeStruct((GHOST_ROWS, LANES), f32),
         ),
-        in_specs=[anywhere, VMEM],
-        out_specs=(anywhere, anywhere, VMEM, VMEM, VMEM),
-        scratch_shapes=[pltpu.SemaphoreType.DMA((2,)), pltpu.SemaphoreType.DMA((2,))],
-        compiler_params=pltpu.CompilerParams(
-            vmem_limit_bytes=32 * 1024 * 1024, collective_id=number, has_side_effects=True
-        ),
-        name="start",
-    )(position, halo)
-
-
-def gather_stages(comps, read_row, source, place, cells, listed, out):
+        in_specs=[VMEM] * 2,
+        out_specs=(VMEM,) * 4,
+        scratch_shapes=[
+            pltpu.SMEM(table, jnp.int32),
+            pltpu.VMEM((1, GROUPS * 32, LANES), f32),
+            pltpu.VMEM((1, GHOST_ROWS, LANES), f32),
+            pltpu.SemaphoreType.DMA,
+        ],
+        compiler_params=params(),
+        name="plan",
+    )(halo, charges)
+
+
+def unmix(comps, raw, store):
+    for c in range(comps):
+        for side in range(2):
+            for b in range(GHOST_ROWS // 16):
+                store(c, pl.ds(side * (GHOST_ROWS // 2) + b * 8, 8), raw[c, pl.ds(b * 16 + side, 8, stride=2), :])
+
+
+def gather_stages(comps, read_rows, source, place, cells, listed, out):
     zeros = (jnp.zeros((8, LANES), f32),) * comps
 
-    def one_group(group, carry):
-        first = pl.multiple_of(group * GROUP_ROWS, GROUP_ROWS)
-
-        def list_block(v, carry):
-            here = pl.ds(pl.multiple_of(first + v * 8, 8), 8)
-            src = source[here, :]
-            lane = src & 127
-            row = src >> 7
-            accs = list(zeros)
+    for half in range(GROUPS // 8):
+        first = half * 8 * GROUP_ROWS
+        most = cells[half * 64, CELLS]
+        for k in range(1, 8):
+            most = jnp.maximum(most, cells[half * 64 + k * 8, CELLS])
+
+        def list_rows(pair, carry, first=first):
+            spots = [pl.ds(first + 2 * pair + k, 8, stride=32) for k in range(2)]
+            src = [source[spot, :] for spot in spots]
+            lane = [item & 127 for item in src]
+            row = [item >> 7 for item in src]
+            accs = [list(zeros), list(zeros)]
             for u in range(GROUP_ROWS):
-                mine = row == u
+                mine = [item == u for item in row]
                 for c in range(comps):
-                    line = jnp.broadcast_to(read_row(c, first + u), (8, LANES))
-                    accs[c] = jnp.where(mine, jnp.take_along_axis(line, lane, axis=1), accs[c])
-            for c in range(comps):
-                listed[c, here, :] = accs[c]
+                    lines = read_rows(c, pl.ds(first + u, 8, stride=GROUP_ROWS))
+                    for k in range(2):
+                        accs[k][c] = jnp.where(mine[k], jnp.take_along_axis(lines, lane[k], axis=1), accs[k][c])
+            for k in range(2):
+                for c in range(comps):
+                    listed[c, spots[k], :] = accs[k][c]
             return carry
 
-        return lax.fori_loop(0, (cells[group * 8, CELLS] + 1023) >> 10, list_block, carry)
-
-    lax.fori_loop(0, GROUPS, one_group, 0)
+        lax.fori_loop(0, (most + 255) >> 8, list_rows, 0)
 
     def slot_block(t, carry):
         here = pl.ds(pl.multiple_of(t * 8, 8), 8)
@@ -210,22 +202,31 @@
 
 
 def first_gather_kernel(
-    partner, cells, own, below, above, charges, path_weight, source, place, position, ghosts, partial, listed
+    partner, cells, own, below, above, ghost_q, path_weight, source, place, position, ghosts, partial, listed, raw
 ):
     window = lax.axis_index("rep")
     for c in range(3):
         position[c] = pick(partner[0], window, own[c], below[c], above[c])
-
-    def read_row(c, r):
-        if c == 3:
-            return charges[pl.ds(r, 1), :]
-        return position[c, pl.ds(r, 1), :]
-
     partial[...] = jnp.sum((path_weight[...] * position[2]).reshape(64, 8, LANES), axis=0)
-    gather_stages(4, read_row, source, place, cells, listed, ghosts)
-
-
-def first_gather(partner, own, below, above, charges, path_weight, source, place, cells):
+    ghosts[3] = ghost_q[...]
+    gather_positions(position, source, place, cells, ghosts, listed, raw)
+
+
+def gather_positions(position, source, place, cells, ghosts, listed, raw):
+    def read_rows(c, rows):
+        return position[c, rows, :]
+
+    def store(c, rows, value):
+        ghosts[c, rows, :] = value
+
+    gather_stages(3, read_rows, source, place, cells, listed, raw)
+    unmix(3, raw, store)
+
+
+GATHER_SCRATCH = [pltpu.VMEM((3, GROUPS * 32, LANES), f32), pltpu.VMEM((3, GHOST_ROWS, LANES), f32)]
+
+
+def first_gather(partner, cells, own, below, above, ghost_q, path_weight, source, place):
     return pl.pallas_call(
         first_gather_kernel,
         out_shape=(
@@ -235,10 +236,10 @@
         ),
         in_specs=[SMEM] * 2 + [VMEM] * 7,
         out_specs=(VMEM,) * 3,
-        scratch_shapes=[pltpu.VMEM((4, GROUPS * 32, LANES), f32)],
+        scratch_shapes=GATHER_SCRATCH,
         compiler_params=params(),
         name="first_gather",
-    )(partner, cells, own, below, above, charges, path_weight, source, place)
+    )(partner, cells, own, below, above, ghost_q, path_weight, source, place)
 
 
 def parts3(value):
@@ -249,9 +250,12 @@
 
 
 def step_kernel(
-    count, windows, last, scalars, partner, pairs, ghosts, partial, position, velocity, charges, lower_q, upper_q, inv_mass, path_weight,
-    new_position, new_velocity, result, *rest,
+    count, windows, last, spring, center, partner, pairs, ghosts, partial, position, velocity, charges, inv_mass,
+    path_weight, *rest,
 ):
+    if last:
+        lower_q, upper_q, *rest = rest
+    new_position, new_velocity, result, *rest = rest
     if last:
         kept_q = ()
     else:
@@ -377,7 +381,7 @@
 
     def listed(tile):
         tile = jnp.minimum(tile, TILES - 1)
-        return tile, pairs[2 * tile], pairs[2 * tile + 1]
+        return tile, pairs[0, tile], pairs[1, tile]
 
     def spread_of(tile):
         tile, one, two = listed(tile)
@@ -415,7 +419,7 @@
         return jnp.sum(terms[...])
 
     progress = total_of(parts, partial, term_copies)
-    pull = scalars[0] * (progress - scalars[1])
+    pull = spring[0] * (progress - center[0])
     for copy in velocity_copies:
         copy.wait()
 
@@ -455,13 +459,15 @@
         final_copies = [
             send(partial_last, final.at[me], k, sent_last.at[k], got_last.at[k]) for k in range(1, count)
         ]
-        off = total_of(final, partial_last, final_copies) - scalars[1]
-        result[...] = jnp.full((8, LANES), 0.5 * scalars[0] * off * off, f32)
+        off = total_of(final, partial_last, final_copies) - center[0]
+        result[0] = 0.5 * spring[0] * off * off
     else:
         result[...] = ending
 
 
-def step(number, last, scalars, partner, pairs, ghosts, partial, position, velocity, charges, lower_q, upper_q, inv_mass, path_weight):
+def step(
+    number, last, spring, center, partner, pairs, ghosts, partial, position, velocity, charges, inv_mass, path_weight, *kept_q
+):
     count, windows = lax.axis_size("dom"), lax.axis_size("rep")
     comps, rows = ghosts.shape[:2]
     whole = jax.ShapeDtypeStruct((3, TILES, LANES), f32)
@@ -479,9 +485,9 @@
 
     return pl.pallas_call(
         kernel,
-        out_shape=(whole, whole, jax.ShapeDtypeStruct((8, LANES), f32)) + kept,
-        in_specs=[SMEM] * 3 + [VMEM] * 9,
-        out_specs=(VMEM,) * (3 + len(kept)),
+        out_shape=(whole, whole, jax.ShapeDtypeStruct((1,) if last else (8, LANES), f32)) + kept,
+        in_specs=[SMEM] * 4 + [VMEM] * (7 + len(kept_q)),
+        out_specs=(VMEM, VMEM, SMEM if last else VMEM) + (VMEM,) * len(kept),
         scratch_shapes=[
             pltpu.VMEM((8 * 16, LANES), f32),
             pltpu.VMEM((8 * 48, LANES), f32),
@@ -506,26 +512,32 @@
             vmem_limit_bytes=58 * 1024 * 1024, collective_id=number, has_side_effects=True
         ),
         name="step",
-    )(scalars, partner, pairs, ghosts, partial, position, velocity, charges, lower_q, upper_q, inv_mass, path_weight)
-
-
-def second_gather_kernel(cells, position, source, place, ghosts, listed):
-    def read_row(c, r):
-        return position[c, pl.ds(r, 1), :]
-
-    gather_stages(3, read_row, source, place, cells, listed, ghosts)
-
-
-def second_gather(position, source, place, cells):
+    )(
+        spring, center, partner, pairs, ghosts, partial, position, velocity, charges, inv_mass, path_weight, *kept_q
+    )
+
+
+def second_gather_kernel(cells, *refs):
+    position, source, place, ghosts, listed, raw = refs
+    gather_positions(position, source, place, cells, ghosts, listed, raw)
+
+
+def second_gather(cells, position, source, place):
     return pl.pallas_call(
         second_gather_kernel,
         out_shape=jax.ShapeDtypeStruct((3, GHOST_ROWS, LANES), f32),
         in_specs=[SMEM] + [VMEM] * 3,
         out_specs=VMEM,
-        scratch_shapes=[pltpu.VMEM((3, GROUPS * 32, LANES), f32)],
+        scratch_shapes=GATHER_SCRATCH,
         compiler_params=params(),
         name="second_gather",
     )(cells, position, source, place)
+
+
+def shifted(shard, axis, by):
+    count = lax.axis_size(axis)
+    pairs = [(i, i + by) for i in range(count) if 0 <= i + by < count]
+    return lax.ppermute(shard, axis, pairs)
 
 
 def body(positions, velocities, charges, inv_mass, path_weight, halo_index, tile_pairs, partner, bias_center, bias_spring):
@@ -534,26 +546,25 @@
     charges = charges.reshape(TILES, LANES)
     inv_mass = inv_mass.reshape(TILES, LANES)
     path_weight = path_weight.reshape(TILES, LANES)
-    pairs = tile_pairs.reshape(-1)
-    halo = halo_index.reshape(GHOST_ROWS, LANES)
-    scalars = jnp.stack([bias_spring[0], bias_center[0]])
-    below, above, source, place, cells = start(position, halo, STEPS)
+    pairs = tile_pairs.T
+    halo = halo_index.reshape(2, GHOST_ROWS // 2, LANES).transpose(1, 0, 2).reshape(GHOST_ROWS, LANES)
+    below = shifted(position, "rep", 1)
+    above = shifted(position, "rep", -1)
+    source, place, cells, ghost_q = plan(halo, charges)
     position, ghosts, partial = first_gather(
-        partner, position, below, above, charges, path_weight, source, place, cells
+        partner, cells, position, below, above, ghost_q, path_weight, source, place
     )
-    lower_q = upper_q = jnp.zeros((GHOST_ROWS // 2, LANES), f32)
+    kept_q = ()
     for step_index in range(STEPS):
         last = step_index == STEPS - 1
         position, velocity, partial, *kept_q = step(
-            step_index, last, scalars, partner, pairs, ghosts, partial, position, velocity,
-            charges, lower_q, upper_q, inv_mass, path_weight,
+            step_index, last, bias_spring, bias_center, partner, pairs, ghosts, partial, position, velocity,
+            charges, inv_mass, path_weight, *kept_q,
         )
         if not last:
-            lower_q, upper_q = kept_q
-            ghosts = second_gather(position, source, place, cells)
-    energy = partial[0, :1]
+            ghosts = second_gather(cells, position, source, place)
     atoms = TILES * LANES
-    return position.reshape(1, 3, atoms), velocity.reshape(1, 3, atoms), energy
+    return position.reshape(1, 3, atoms), velocity.reshape(1, 3, atoms), partial
 
 
 def solution(mesh):

time: 155 us -> 157 us (1.013)
  local copies, waits for them, and re-layouts: 11.2 us -> 4.13 us
  starting transfers between devices: 0 us -> 4.69 us
  Pallas kernels: 139 us -> 143 us
  between operations: 2.7 us -> 4.42 us
    pallas_call x3, Pallas kernels: 104 us -> 115 us  [the longest x2 87.5 us: step(): pl.pallas_call(kernel, out_shape=(whole, whole, jax.ShapeDtypeStruct((1,)...]
    ppermute x0 -> x2, starting transfers between devices: none -> 4.69 us  [shifted(): return lax.ppermute(shard, axis, pairs)]
    pallas_call x1, Pallas kernels: 18.7 us -> 14.4 us  [first_gather(): pl.pallas_call(first_gather_kernel, out_shape=(jax.ShapeDtypeStruct((3, T...]
    unnamed x17 -> x8, local copies, waits for them, and re-layouts: 7.58 us -> 4.13 us
    pallas_call x1, Pallas kernels: 15.7 us -> 13.9 us  [second_gather(): pl.pallas_call(second_gather_kernel, out_shape=jax.ShapeDtypeStruct((3, G...]
    reshape x2 -> x0, local copies, waits for them, and re-layouts: 1.78 us -> none  [the longest x1 1.02 us: body(): halo = halo_index.reshape(GHOST_ROWS, LANES)]
  transfers between devices with their start and end apart: 0 -> 2, of which waited for: 0 -> 0; matrix products, arithmetic and copies ran while one was open for 0% -> 0% of each run, Pallas kernels for 0% -> 18%
where the time goes in v5:
time: 157 us; the launch traced here: 156 us
  Pallas kernels  143 us (91%)
  starting transfers between devices  4.69 us (3%)
  between operations  4.42 us (3%)
  local copies, waits for them, and re-layouts  4.13 us (3%)
    pallas_call x2, Pallas kernels, step(): pl.pallas_call(kernel, out_shape=(whole, whole, jax.ShapeDtypeStruct((1,)...  87.5 us
    pallas_call x1, Pallas kernels, plan(): pl.pallas_call(plan_kernel, out_shape=(jax.ShapeDtypeStruct((GROUPS * 32,...  27.4 us
    pallas_call x1, Pallas kernels, first_gather(): pl.pallas_call(first_gather_kernel, out_shape=(jax.ShapeDtypeStruct((3, T...  14.4 us
    pallas_call x1, Pallas kernels, second_gather(): pl.pallas_call(second_gather_kernel, out_shape=jax.ShapeDtypeStruct((3, G...  13.9 us
    ppermute x2, starting transfers between devices, shifted(): return lax.ppermute(shard, axis, pairs)  4.69 us
    unnamed x8, local copies, waits for them, and re-layouts  4.13 us
  transfers between devices with their start and end apart: 2, of which 0 were waited for; matrix products, arithmetic and copies ran while one was open for 0% of the time, Pallas kernels for 18%

profile of v5, /device:TPU:96, one launch (start us, length us, event | category | flops | bytes accessed | tf_op | source)
XLA Modules:
  0.0 156.4 jit_solution(1566313669507017761)
XLA Ops:
  0.6 2.8 %collective-permute-start.1 = (f32[3,512,128]{2,1,0:T(8,128)}, f32[3,512,128]{2,1,0:T(8,128)S(1)}, u32[]{:S(2)}, u32[]{:S(2)}) collective-permute-start(f32[3,512,128]{2,1,0:T(8,128)} %bitcast.23), channel_id=1, source_target_pairs={{8,0},{16,8},{24,16},{32,24},{40,32},{48,40},{56,48},{64,56},{72,6... | collective-permute-start | bytes 2359304 | tf_op jit(solution)/shard_map/ppermute | solution.py:540
  3.4 1.9 %collective-permute-start = (f32[3,512,128]{2,1,0:T(8,128)}, f32[3,512,128]{2,1,0:T(8,128)S(1)}, u32[]{:S(2)}, u32[]{:S(2)}) collective-permute-start(f32[3,512,128]{2,1,0:T(8,128)} %bitcast.24), channel_id=1, source_target_pairs={{0,8},{8,16},{16,24},{24,32},{32,40},{40,48},{48,56},{56,64},{64,7... | collective-permute-start | bytes 2359304 | tf_op jit(solution)/shard_map/ppermute | solution.py:540
  7.3 27.4 %plan.1 = (s32[512,128]{1,0:T(8,128)}, s32[256,128]{1,0:T(8,128)}, s32[128,128]{1,0:T(8,128)}, f32[256,128]{1,0:T(8,128)}) custom-call(s32[256,128]{1,0:T(8,128)} %bitcast.27, f32[512,128]{1,0:T(8,128)} %bitcast.13), custom_call_target="tpu_custom_call" | custom-call | tf_op jit(solution)/shard_map/plan/pallas_call | solution.py:96
  34.7 0.0 collective-permute-done.1.above
  34.7 0.0 copy-start.1
  34.7 0.0 collective-permute-done.below
  34.7 0.0 copy-start.2
  34.7 0.8 copy-done.1
  35.6 0.3 copy-done.2
  35.8 14.4 %first_gather.1 = (f32[3,512,128]{2,1,0:T(8,128)}, f32[4,256,128]{2,1,0:T(8,128)}, f32[8,128]{1,0:T(8,128)}) custom-call(s32[1]{0:T(128)S(6)} %copy.22.partner.refs_2_, s32[128,128]{1,0:T(8,128)} %get-tuple-element.18.cells, f32[3,512,128]{2,1,0:T(8,128)} %bitcast.25, f32[3,512,128]{2,1,0:T(8,128)} %copy-done.2, f32[3,512,128]{2,1,0:T(8,128)} %copy-done.1, ...), custom_call_target="tpu_custom_call" | custom-call | tf_op jit(solution)/shard_map/first_gather/pallas_call | solution.py:230
  50.2 42.6 %step.2 = (f32[3,512,128]{2,1,0:T(8,128)}, f32[3,512,128]{2,1,0:T(8,128)}, f32[8,128]{1,0:T(8,128)}, f32[128,128]{1,0:T(8,128)}, f32[128,128]{1,0:T(8,128)}) custom-call(f32[1]{0:T(128)S(6)} %copy.24.refs_0_, f32[1]{0:T(128)S(6)} %copy.23.refs_1_, s32[1]{0:T(128)S(6)} %copy.22.partner.refs_2_, s32[2,512]{1,0:T(2,128)} %bitcast.28, ...), custom_call_target="tpu_custom_call" | custom-call | tf_op jit(solution)/shard_map/step/pallas_call | solution.py:486
  92.8 13.9 %second_gather.1.refs_4_ = f32[3,256,128]{2,1,0:T(8,128)} custom-call(s32[128,128]{1,0:T(8,128)} %get-tuple-element.18.cells, f32[3,512,128]{2,1,0:T(8,128)} %get-tuple-element.25.refs_0_.refs_6_, s32[512,128]{1,0:T(8,128)} %get-tuple-element.20.source.refs_1_, s32[256,128]{1,0:T(8,128)} %get-tuple-element.21.place.refs_2_), custom_call_target="tpu_custom_call" | custom-call | tf_op jit(solution)/shard_map/second_gather/pallas_call | solution.py:526
  106.7 44.9 %step.3 = (f32[3,512,128]{2,1,0:T(8,128)}, f32[3,512,128]{2,1,0:T(8,128)}, f32[1]{0:T(128)}) custom-call(f32[1]{0:T(128)S(6)} %copy.24.refs_0_, f32[1]{0:T(128)S(6)} %copy.23.refs_1_, s32[1]{0:T(128)S(6)} %copy.22.partner.refs_2_, s32[2,512]{1,0:T(2,128)} %bitcast.29, f32[3,256,128]{2,1,0:T(8,128)} %second_gather.1.refs_4_, ...), custom_call_target="tpu_custom_call" | custom-call | tf_op jit(solution)/shard_map/step/pallas_call | solution.py:486
  151.6 0.0 copy-start
  151.6 2.1 %copy.25 = f32[1,3,65536]{2,0,1:T(1,128)} copy(f32[1,3,65536]{2,0,1:T(1,128)} %bitcast.22) | data formatting | bytes 1572864
  153.8 0.0 copy-done
  153.8 0.9 copy.26
Async XLA Ops:
  0.6 34.1 %collective-permute-start.1 = (f32[3,512,128]{2,1,0:T(8,128)}, f32[3,512,128]{2,1,0:T(8,128)S(1)}, u32[]{:S(2)}, u32[]{:S(2)}) collective-permute-start(f32[3,512,128]{2,1,0:T(8,128)} %bitcast.23), channel_id=1, source_target_pairs={{8,0},{16,8},{24,16},{32,24},{40,32},{48,40},{56,48},{64,56},{72,6... | collective-permute-start | bytes 2359304 | tf_op jit(solution)/shard_map/ppermute | solution.py:540
  3.4 31.3 %collective-permute-start = (f32[3,512,128]{2,1,0:T(8,128)}, f32[3,512,128]{2,1,0:T(8,128)S(1)}, u32[]{:S(2)}, u32[]{:S(2)}) collective-permute-start(f32[3,512,128]{2,1,0:T(8,128)} %bitcast.24), channel_id=1, source_target_pairs={{0,8},{8,16},{16,24},{24,32},{32,40},{40,48},{48,56},{56,64},{64,7... | collective-permute-start | bytes 2359304 | tf_op jit(solution)/shard_map/ppermute | solution.py:540
  34.7 0.9 copy-start.1
  34.7 1.1 copy-start.2
  151.6 2.1 %copy-start = (f32[3,512,128]{2,1,0:T(8,128)S(1)}, f32[3,512,128]{2,1,0:T(8,128)}, u32[]{:S(2)}) copy-start(f32[3,512,128]{2,1,0:T(8,128)} %get-tuple-element.31) | copy-start | bytes 2359300

commit v6 on v5

--- a/solution.py
+++ b/solution.py
@@ -25,7 +25,7 @@
     return pltpu.CompilerParams(vmem_limit_bytes=58 * 1024 * 1024)
 
 
-def plan_kernel(halo, charges, source, place, cells, ghost_q, counts, listed, raw, arrived):
+def plan_kernel(halo, source, place, cells):
     shape = (GHOST_ROWS, LANES)
     row = lax.broadcasted_iota(jnp.int32, shape, 0)
     lane = lax.broadcasted_iota(jnp.int32, shape, 1)
@@ -80,38 +80,21 @@
         return carry
 
     lax.fori_loop(0, GROUPS, one_group, 0)
-    copy = pltpu.make_async_copy(cells, counts, arrived)
-    copy.start()
-    copy.wait()
-
-    def read_rows(c, rows):
-        return charges[rows, :]
-
-    gather_stages(1, read_rows, source, place, counts, listed, raw)
-    unmix(1, raw, lambda c, rows, value: ghost_q.__setitem__((rows, slice(None)), value))
-
-
-def plan(halo, charges):
-    table = (GROUPS * 8, LANES)
+
+
+def plan(halo):
     return pl.pallas_call(
         plan_kernel,
         out_shape=(
             jax.ShapeDtypeStruct((GROUPS * 32, LANES), jnp.int32),
             jax.ShapeDtypeStruct((GHOST_ROWS, LANES), jnp.int32),
-            jax.ShapeDtypeStruct(table, jnp.int32),
-            jax.ShapeDtypeStruct((GHOST_ROWS, LANES), f32),
+            jax.ShapeDtypeStruct((GROUPS * 8, LANES), jnp.int32),
         ),
-        in_specs=[VMEM] * 2,
-        out_specs=(VMEM,) * 4,
-        scratch_shapes=[
-            pltpu.SMEM(table, jnp.int32),
-            pltpu.VMEM((1, GROUPS * 32, LANES), f32),
-            pltpu.VMEM((1, GHOST_ROWS, LANES), f32),
-            pltpu.SemaphoreType.DMA,
-        ],
+        in_specs=[VMEM],
+        out_specs=(VMEM,) * 3,
         compiler_params=params(),
         name="plan",
-    )(halo, charges)
+    )(halo)
 
 
 def unmix(comps, raw, store):
@@ -202,31 +185,31 @@
 
 
 def first_gather_kernel(
-    partner, cells, own, below, above, ghost_q, path_weight, source, place, position, ghosts, partial, listed, raw
+    partner, cells, own, below, above, charges, path_weight, source, place, position, ghosts, partial, listed, raw
 ):
     window = lax.axis_index("rep")
     for c in range(3):
         position[c] = pick(partner[0], window, own[c], below[c], above[c])
     partial[...] = jnp.sum((path_weight[...] * position[2]).reshape(64, 8, LANES), axis=0)
-    ghosts[3] = ghost_q[...]
-    gather_positions(position, source, place, cells, ghosts, listed, raw)
-
-
-def gather_positions(position, source, place, cells, ghosts, listed, raw):
+    gather_positions(4, (position, charges), source, place, cells, ghosts, listed, raw)
+
+
+def gather_positions(comps, tables, source, place, cells, ghosts, listed, raw):
     def read_rows(c, rows):
-        return position[c, rows, :]
+        return tables[1][rows, :] if c == 3 else tables[0][c, rows, :]
 
     def store(c, rows, value):
         ghosts[c, rows, :] = value
 
-    gather_stages(3, read_rows, source, place, cells, listed, raw)
-    unmix(3, raw, store)
-
-
-GATHER_SCRATCH = [pltpu.VMEM((3, GROUPS * 32, LANES), f32), pltpu.VMEM((3, GHOST_ROWS, LANES), f32)]
-
-
-def first_gather(partner, cells, own, below, above, ghost_q, path_weight, source, place):
+    gather_stages(comps, read_rows, source, place, cells, listed, raw)
+    unmix(comps, raw, store)
+
+
+def gather_scratch(comps):
+    return [pltpu.VMEM((comps, GROUPS * 32, LANES), f32), pltpu.VMEM((comps, GHOST_ROWS, LANES), f32)]
+
+
+def first_gather(partner, cells, own, below, above, charges, path_weight, source, place):
     return pl.pallas_call(
         first_gather_kernel,
         out_shape=(
@@ -236,10 +219,10 @@
         ),
         in_specs=[SMEM] * 2 + [VMEM] * 7,
         out_specs=(VMEM,) * 3,
-        scratch_shapes=GATHER_SCRATCH,
+        scratch_shapes=gather_scratch(4),
         compiler_params=params(),
         name="first_gather",
-    )(partner, cells, own, below, above, ghost_q, path_weight, source, place)
+    )(partner, cells, own, below, above, charges, path_weight, source, place)
 
 
 def parts3(value):
@@ -272,45 +255,11 @@
         pl.semaphore_signal(
             barrier, inc=1, device_id={"dom": lax.rem(me + k, count)}, device_id_type=pl.DeviceIdType.MESH
         )
-    if last:
-        pl.semaphore_wait(barrier, count - 1)
-    else:
+    if not last:
         window = lax.axis_index("rep")
         ahead, behind = lax.rem(window + 1, windows), lax.rem(window + windows - 1, windows)
         for other in (ahead, behind):
             pl.semaphore_signal(barrier, inc=1, device_id={"rep": other}, device_id_type=pl.DeviceIdType.MESH)
-        pl.semaphore_wait(barrier, count + 1)
-
-    def send(source, target, k, sent_now, got_now):
-        copy = pltpu.make_async_remote_copy(
-            src_ref=source,
-            dst_ref=target,
-            send_sem=sent_now,
-            recv_sem=got_now,
-            device_id={"dom": lax.rem(me + k, count)},
-            device_id_type=pl.DeviceIdType.MESH,
-        )
-        copy.start()
-        return copy
-
-    ghost_copies = [
-        send(ghosts.at[:, pl.ds(half, half)], lower, 1, sent.at[0], got.at[0]),
-        send(ghosts.at[:, pl.ds(0, half)], upper, count - 1, sent.at[count], got.at[count]),
-    ]
-    term_copies = [send(partial, parts.at[me], k, sent.at[k], got.at[k]) for k in range(1, count)]
-    velocity_copies = []
-    if not last:
-        for n, (other, target) in enumerate(((ahead, velocity_below), (behind, velocity_above))):
-            copy = pltpu.make_async_remote_copy(
-                src_ref=velocity,
-                dst_ref=target,
-                send_sem=sent_v.at[n],
-                recv_sem=got_v.at[n],
-                device_id={"rep": other},
-                device_id_type=pl.DeviceIdType.MESH,
-            )
-            copy.start()
-            velocity_copies.append(copy)
 
     zero8 = jnp.zeros((8, LANES), f32)
     one8 = jnp.ones((8, LANES), f32)
@@ -354,7 +303,41 @@
         build(base, position[0, here, :], position[1, here, :], position[2, here, :], charges[here, :], True)
         return carry
 
-    lax.fori_loop(0, TILES // 8, own_block, 0)
+    lax.fori_loop(0, TILES // 16, own_block, 0)
+    pl.semaphore_wait(barrier, count - 1 if last else count + 1)
+
+    def send(source, target, k, sent_now, got_now):
+        copy = pltpu.make_async_remote_copy(
+            src_ref=source,
+            dst_ref=target,
+            send_sem=sent_now,
+            recv_sem=got_now,
+            device_id={"dom": lax.rem(me + k, count)},
+            device_id_type=pl.DeviceIdType.MESH,
+        )
+        copy.start()
+        return copy
+
+    ghost_copies = [
+        send(ghosts.at[:, pl.ds(half, half)], lower, 1, sent.at[0], got.at[0]),
+        send(ghosts.at[:, pl.ds(0, half)], upper, count - 1, sent.at[count], got.at[count]),
+    ]
+    term_copies = [send(partial, parts.at[me], k, sent.at[k], got.at[k]) for k in range(1, count)]
+    velocity_copies = []
+    if not last:
+        for n, (other, target) in enumerate(((ahead, velocity_below), (behind, velocity_above))):
+            copy = pltpu.make_async_remote_copy(
+                src_ref=velocity,
+                dst_ref=target,
+                send_sem=sent_v.at[n],
+                recv_sem=got_v.at[n],
+                device_id={"rep": other},
+                device_id_type=pl.DeviceIdType.MESH,
+            )
+            copy.start()
+            velocity_copies.append(copy)
+
+    lax.fori_loop(TILES // 16, TILES // 8, own_block, 0)
 
     def ghost_block(values, charge, offset):
         def block(b, carry):
@@ -519,7 +502,7 @@
 
 def second_gather_kernel(cells, *refs):
     position, source, place, ghosts, listed, raw = refs
-    gather_positions(position, source, place, cells, ghosts, listed, raw)
+    gather_positions(3, (position,), source, place, cells, ghosts, listed, raw)
 
 
 def second_gather(cells, position, source, place):
@@ -528,7 +511,7 @@
         out_shape=jax.ShapeDtypeStruct((3, GHOST_ROWS, LANES), f32),
         in_specs=[SMEM] + [VMEM] * 3,
         out_specs=VMEM,
-        scratch_shapes=GATHER_SCRATCH,
+        scratch_shapes=gather_scratch(3),
         compiler_params=params(),
         name="second_gather",
     )(cells, position, source, place)
@@ -550,9 +533,9 @@
     halo = halo_index.reshape(2, GHOST_ROWS // 2, LANES).transpose(1, 0, 2).reshape(GHOST_ROWS, LANES)
     below = shifted(position, "rep", 1)
     above = shifted(position, "rep", -1)
-    source, place, cells, ghost_q = plan(halo, charges)
+    source, place, cells = plan(halo)
     position, ghosts, partial = first_gather(
-        partner, cells, position, below, above, ghost_q, path_weight, source, place
+        partner, cells, position, below, above, charges, path_weight, source, place
     )
     kept_q = ()
     for step_index in range(STEPS):

time: 157 us -> 151 us (0.962)
  Pallas kernels: 143 us -> 137 us
    pallas_call x1, Pallas kernels: 27.4 us -> 18.6 us  [plan(): pl.pallas_call(plan_kernel, out_shape=(jax.ShapeDtypeStruct((GROUPS * 32,...]
    pallas_call x1, Pallas kernels: 14.4 us -> 17.1 us  [first_gather(): pl.pallas_call(first_gather_kernel, out_shape=(jax.ShapeDtypeStruct((3, T...]
  transfers between devices with their start and end apart: 2 -> 2, of which waited for: 0 -> 0; matrix products, arithmetic and copies ran while one was open for 0% -> 0% of each run, Pallas kernels for 18% -> 12%
where the time goes in v6:
time: 151 us; the launch traced here: 150 us
  Pallas kernels  137 us (91%)
  starting transfers between devices  4.69 us (3%)
  between operations  4.39 us (3%)
  local copies, waits for them, and re-layouts  4.14 us (3%)
    pallas_call x2, Pallas kernels, step(): pl.pallas_call(kernel, out_shape=(whole, whole, jax.ShapeDtypeStruct((1,)...  87.5 us
    pallas_call x1, Pallas kernels, plan(): pl.pallas_call(plan_kernel, out_shape=(jax.ShapeDtypeStruct((GROUPS * 32,...  18.6 us
    pallas_call x1, Pallas kernels, first_gather(): pl.pallas_call(first_gather_kernel, out_shape=(jax.ShapeDtypeStruct((3, T...  17.1 us
    pallas_call x1, Pallas kernels, second_gather(): pl.pallas_call(second_gather_kernel, out_shape=jax.ShapeDtypeStruct((3, G...  13.9 us
    ppermute x2, starting transfers between devices, shifted(): return lax.ppermute(shard, axis, pairs)  4.69 us
    unnamed x8, local copies, waits for them, and re-layouts  4.14 us
  transfers between devices with their start and end apart: 2, of which 0 were waited for; matrix products, arithmetic and copies ran while one was open for 0% of the time, Pallas kernels for 12%

profile of v6, /device:TPU:96, one launch (start us, length us, event | category | flops | bytes accessed | tf_op | source)
XLA Modules:
  0.0 150.3 jit_solution(16061977423027108384)
XLA Ops:
  0.6 2.8 %collective-permute-start.1 = (f32[3,512,128]{2,1,0:T(8,128)}, f32[3,512,128]{2,1,0:T(8,128)S(1)}, u32[]{:S(2)}, u32[]{:S(2)}) collective-permute-start(f32[3,512,128]{2,1,0:T(8,128)} %bitcast.23), channel_id=1, source_target_pairs={{8,0},{16,8},{24,16},{32,24},{40,32},{48,40},{56,48},{64,56},{72,6... | collective-permute-start | bytes 2359304 | tf_op jit(solution)/shard_map/ppermute | solution.py:523
  3.4 1.9 %collective-permute-start = (f32[3,512,128]{2,1,0:T(8,128)}, f32[3,512,128]{2,1,0:T(8,128)S(1)}, u32[]{:S(2)}, u32[]{:S(2)}) collective-permute-start(f32[3,512,128]{2,1,0:T(8,128)} %bitcast.24), channel_id=1, source_target_pairs={{0,8},{8,16},{16,24},{24,32},{32,40},{40,48},{48,56},{56,64},{64,7... | collective-permute-start | bytes 2359304 | tf_op jit(solution)/shard_map/ppermute | solution.py:523
  7.3 18.6 %plan.1 = (s32[512,128]{1,0:T(8,128)}, s32[256,128]{1,0:T(8,128)}, s32[128,128]{1,0:T(8,128)}) custom-call(s32[256,128]{1,0:T(8,128)} %bitcast.27), custom_call_target="tpu_custom_call" | custom-call | tf_op jit(solution)/shard_map/plan/pallas_call | solution.py:86
  25.8 0.0 collective-permute-done.1.above
  25.8 0.0 copy-start.1
  25.8 0.0 collective-permute-done.below
  25.8 0.0 copy-start.2
  25.8 0.9 copy-done.1
  26.7 0.3 copy-done.2
  27.0 17.1 %first_gather.1 = (f32[3,512,128]{2,1,0:T(8,128)}, f32[4,256,128]{2,1,0:T(8,128)}, f32[8,128]{1,0:T(8,128)}) custom-call(s32[1]{0:T(128)S(6)} %copy.22.partner.refs_2_, s32[128,128]{1,0:T(8,128)} %get-tuple-element.17.cells, f32[3,512,128]{2,1,0:T(8,128)} %bitcast.25, f32[3,512,128]{2,1,0:T(8,128)} %copy-done.2, f32[3,512,128]{2,1,0:T(8,128)} %copy-done.1, ...), custom_call_target="tpu_custom_call" | custom-call | tf_op jit(solution)/shard_map/first_gather/pallas_call | solution.py:213
  44.1 43.7 %step.2 = (f32[3,512,128]{2,1,0:T(8,128)}, f32[3,512,128]{2,1,0:T(8,128)}, f32[8,128]{1,0:T(8,128)}, f32[128,128]{1,0:T(8,128)}, f32[128,128]{1,0:T(8,128)}) custom-call(f32[1]{0:T(128)S(6)} %copy.24.refs_0_, f32[1]{0:T(128)S(6)} %copy.23.refs_1_, s32[1]{0:T(128)S(6)} %copy.22.partner.refs_2_, s32[2,512]{1,0:T(2,128)} %bitcast.28, ...), custom_call_target="tpu_custom_call" | custom-call | tf_op jit(solution)/shard_map/step/pallas_call | solution.py:469
  87.8 13.9 %second_gather.1.refs_4_ = f32[3,256,128]{2,1,0:T(8,128)} custom-call(s32[128,128]{1,0:T(8,128)} %get-tuple-element.17.cells, f32[3,512,128]{2,1,0:T(8,128)} %get-tuple-element.23.refs_0_.refs_6_, s32[512,128]{1,0:T(8,128)} %get-tuple-element.18.source.refs_1_, s32[256,128]{1,0:T(8,128)} %get-tuple-element.19.place.refs_2_), custom_call_target="tpu_custom_call" | custom-call | tf_op jit(solution)/shard_map/second_gather/pallas_call | solution.py:509
  101.7 43.8 %step.3 = (f32[3,512,128]{2,1,0:T(8,128)}, f32[3,512,128]{2,1,0:T(8,128)}, f32[1]{0:T(128)}) custom-call(f32[1]{0:T(128)S(6)} %copy.24.refs_0_, f32[1]{0:T(128)S(6)} %copy.23.refs_1_, s32[1]{0:T(128)S(6)} %copy.22.partner.refs_2_, s32[2,512]{1,0:T(2,128)} %bitcast.29, f32[3,256,128]{2,1,0:T(8,128)} %second_gather.1.refs_4_, ...), custom_call_target="tpu_custom_call" | custom-call | tf_op jit(solution)/shard_map/step/pallas_call | solution.py:469
  145.5 0.0 copy-start
  145.5 2.1 %copy.25 = f32[1,3,65536]{2,0,1:T(1,128)} copy(f32[1,3,65536]{2,0,1:T(1,128)} %bitcast.22) | data formatting | bytes 1572864
  147.7 0.0 copy-done
  147.7 0.9 copy.26
Async XLA Ops:
  0.6 25.2 %collective-permute-start.1 = (f32[3,512,128]{2,1,0:T(8,128)}, f32[3,512,128]{2,1,0:T(8,128)S(1)}, u32[]{:S(2)}, u32[]{:S(2)}) collective-permute-start(f32[3,512,128]{2,1,0:T(8,128)} %bitcast.23), channel_id=1, source_target_pairs={{8,0},{16,8},{24,16},{32,24},{40,32},{48,40},{56,48},{64,56},{72,6... | collective-permute-start | bytes 2359304 | tf_op jit(solution)/shard_map/ppermute | solution.py:523
  3.4 22.4 %collective-permute-start = (f32[3,512,128]{2,1,0:T(8,128)}, f32[3,512,128]{2,1,0:T(8,128)S(1)}, u32[]{:S(2)}, u32[]{:S(2)}) collective-permute-start(f32[3,512,128]{2,1,0:T(8,128)} %bitcast.24), channel_id=1, source_target_pairs={{0,8},{8,16},{16,24},{24,32},{32,40},{40,48},{48,56},{56,64},{64,7... | collective-permute-start | bytes 2359304 | tf_op jit(solution)/shard_map/ppermute | solution.py:523
  25.8 0.9 copy-start.1
  25.8 1.1 copy-start.2
  145.5 2.1 %copy-start = (f32[3,512,128]{2,1,0:T(8,128)S(1)}, f32[3,512,128]{2,1,0:T(8,128)}, u32[]{:S(2)}) copy-start(f32[3,512,128]{2,1,0:T(8,128)} %get-tuple-element.29) | copy-start | bytes 2359300

commit v7 on v6

--- a/solution.py
+++ b/solution.py
@@ -25,7 +25,7 @@
     return pltpu.CompilerParams(vmem_limit_bytes=58 * 1024 * 1024)
 
 
-def plan_kernel(halo, source, place, cells):
+def plan_kernel(halo, source, place, cells, ranks, counts):
     shape = (GHOST_ROWS, LANES)
     row = lax.broadcasted_iota(jnp.int32, shape, 0)
     lane = lax.broadcasted_iota(jnp.int32, shape, 1)
@@ -36,23 +36,32 @@
     square = (GHOST_ROWS, GHOST_ROWS)
     ahead_row = lax.broadcasted_iota(jnp.int32, square, 1) < lax.broadcasted_iota(jnp.int32, square, 0)
     ahead_row = jnp.where(ahead_row, 1.0, 0.0).astype(bf16)
-    place[...] = jnp.zeros(shape, jnp.int32)
+    counts[...] = jnp.zeros(shape, f32)
+
+    def count_group(group, carry):
+        member = (halo[...] >> 12) == group
+        within = jnp.dot(jnp.where(member, 1.0, 0.0).astype(bf16), ahead_lane, preferred_element_type=f32)
+        ranks[...] = jnp.where(member, within[:, :LANES].astype(jnp.int32), ranks[...])
+        counts[...] = jnp.where(lane == group, within[:, LANES:], counts[...])
+        return carry
+
+    lax.fori_loop(0, GROUPS, count_group, 0)
+    earlier = jnp.dot(ahead_row, counts[...].astype(bf16), preferred_element_type=f32)
+    total = (earlier[GHOST_ROWS - 1 :] + counts[GHOST_ROWS - 1 :, :]).astype(jnp.int32)
+    earlier = earlier.astype(jnp.int32)
+    for b in range(GHOST_ROWS // 8):
+        here = slice(8 * b, 8 * b + 8)
+        group_of = halo[here, :] >> 12
+        rank = ranks[here, :] + jnp.take_along_axis(earlier[here], group_of, axis=1)
+        ranks[here, :] = rank
+        place[here, :] = rank + group_of * CAPACITY
+        cells[b : b + 1, :] = earlier[8 * b : 8 * b + 1]
+    cells[CELLS : CELLS + 8, :] = jnp.broadcast_to(total, (8, LANES))
 
     def one_group(group, carry):
         index = halo[...]
         member = (index >> 12) == group
-        flag = jnp.where(member, 1.0, 0.0).astype(bf16)
-        within = jnp.dot(flag, ahead_lane, preferred_element_type=f32)
-        in_row = within[:, LANES:]
-        earlier = jnp.dot(ahead_row, in_row.astype(bf16), preferred_element_type=f32)
-        rank = (within[:, :LANES] + earlier).astype(jnp.int32)
-        place[...] = jnp.where(member, rank + group * CAPACITY, place[...])
-        marks = jnp.where(lane * 8 == row, earlier, 0.0)
-        marks = marks + jnp.where((lane == CELLS) & (row == GHOST_ROWS - 1), earlier + in_row, 0.0)
-        marks = jnp.sum(marks.reshape(GHOST_ROWS // 8, 8, LANES), axis=0)
-        cells[pl.ds(pl.multiple_of(group * 8, 8), 8), :] = jnp.broadcast_to(
-            jnp.sum(marks, axis=0, keepdims=True), (8, LANES)
-        ).astype(jnp.int32)
+        rank = ranks[...]
         shift = row * LANES + lane - rank
         items = jnp.where(member, (1 << 28) | (shift << 12) | (index & 4095), 0)
         for bit in range(15):
@@ -88,10 +97,11 @@
         out_shape=(
             jax.ShapeDtypeStruct((GROUPS * 32, LANES), jnp.int32),
             jax.ShapeDtypeStruct((GHOST_ROWS, LANES), jnp.int32),
-            jax.ShapeDtypeStruct((GROUPS * 8, LANES), jnp.int32),
+            jax.ShapeDtypeStruct((CELLS + 8, LANES), jnp.int32),
         ),
         in_specs=[VMEM],
         out_specs=(VMEM,) * 3,
+        scratch_shapes=[pltpu.VMEM((GHOST_ROWS, LANES), jnp.int32), pltpu.VMEM((GHOST_ROWS, LANES), f32)],
         compiler_params=params(),
         name="plan",
     )(halo)
@@ -109,9 +119,9 @@
 
     for half in range(GROUPS // 8):
         first = half * 8 * GROUP_ROWS
-        most = cells[half * 64, CELLS]
+        most = cells[CELLS, half * 8]
         for k in range(1, 8):
-            most = jnp.maximum(most, cells[half * 64 + k * 8, CELLS])
+            most = jnp.maximum(most, cells[CELLS, half * 8 + k])
 
         def list_rows(pair, carry, first=first):
             spots = [pl.ds(first + 2 * pair + k, 8, stride=32) for k in range(2)]
@@ -150,7 +160,7 @@
             )
 
         def rows_of(g):
-            begin, end = cells[g * 8, t], cells[g * 8, t + 1]
+            begin, end = cells[t, g], cells[t + 1, g]
             return g * 32 + jnp.minimum(begin >> 7, 31), g * 32 + (jnp.maximum(end - 1, begin) >> 7)
 
         accs = zeros
@@ -233,8 +243,8 @@
 
 
 def step_kernel(
-    count, windows, last, spring, center, partner, pairs, ghosts, partial, position, velocity, charges, inv_mass,
-    path_weight, *rest,
+    count, windows, last, spring, center, partner, pairs, ghosts, velocity_in, mass_in, weight_in, partial, position,
+    charges, *rest,
 ):
     if last:
         lower_q, upper_q, *rest = rest
@@ -243,11 +253,17 @@
         kept_q = ()
     else:
         kept_q, rest = rest[:2], rest[2:]
-        rest, velocity_below, velocity_above, sent_v, got_v = rest[:-4], *rest[-4:]
+        rest, (velocity_below, velocity_above, sent_v, got_v) = rest[:-4], rest[-4:]
     (
         rows_j, rows_i, rows_a, feat_j, feat_i, feat_a, sums, spread_a, spread_b,
-        lower, upper, parts, final, sent, got, sent_last, got_last,
+        lower, upper, parts, final, sent, got, sent_last, got_last, velocity, inv_mass, path_weight, filled,
     ) = rest
+    late_copies = [
+        pltpu.make_async_copy(source, target, filled.at[n])
+        for n, (source, target) in enumerate(((velocity_in, velocity), (mass_in, inv_mass), (weight_in, path_weight)))
+    ]
+    for copy in late_copies:
+        copy.start()
     me = lax.axis_index("dom")
     half = GHOST_ROWS // 2
     barrier = pltpu.get_barrier_semaphore()
@@ -323,11 +339,24 @@
         send(ghosts.at[:, pl.ds(0, half)], upper, count - 1, sent.at[count], got.at[count]),
     ]
     term_copies = [send(partial, parts.at[me], k, sent.at[k], got.at[k]) for k in range(1, count)]
+    lax.fori_loop(TILES // 16, TILES // 8, own_block, 0)
+
+    def ghost_block(values, charge, offset):
+        def block(b, carry):
+            base = pl.multiple_of(b * 8, 8)
+            here = pl.ds(base, 8)
+            build(offset + base, values[0, here, :], values[1, here, :], values[2, here, :], charge[here, :], False)
+            return carry
+
+        return block
+
+    for copy in ghost_copies:
+        copy.wait()
     velocity_copies = []
     if not last:
         for n, (other, target) in enumerate(((ahead, velocity_below), (behind, velocity_above))):
             copy = pltpu.make_async_remote_copy(
-                src_ref=velocity,
+                src_ref=velocity_in,
                 dst_ref=target,
                 send_sem=sent_v.at[n],
                 recv_sem=got_v.at[n],
@@ -337,19 +366,6 @@
             copy.start()
             velocity_copies.append(copy)
 
-    lax.fori_loop(TILES // 16, TILES // 8, own_block, 0)
-
-    def ghost_block(values, charge, offset):
-        def block(b, carry):
-            base = pl.multiple_of(b * 8, 8)
-            here = pl.ds(base, 8)
-            build(offset + base, values[0, here, :], values[1, here, :], values[2, here, :], charge[here, :], False)
-            return carry
-
-        return block
-
-    for copy in ghost_copies:
-        copy.wait()
     if last:
         charge_of = (lower_q, upper_q)
     else:
@@ -403,7 +419,7 @@
 
     progress = total_of(parts, partial, term_copies)
     pull = spring[0] * (progress - center[0])
-    for copy in velocity_copies:
+    for copy in late_copies + velocity_copies:
         copy.wait()
 
     def velocity_at(c, here):
@@ -469,7 +485,7 @@
     return pl.pallas_call(
         kernel,
         out_shape=(whole, whole, jax.ShapeDtypeStruct((1,) if last else (8, LANES), f32)) + kept,
-        in_specs=[SMEM] * 4 + [VMEM] * (7 + len(kept_q)),
+        in_specs=[SMEM] * 4 + [pl.BlockSpec(memory_space=pl.ANY)] * 4 + [VMEM] * (3 + len(kept_q)),
         out_specs=(VMEM, VMEM, SMEM if last else VMEM) + (VMEM,) * len(kept),
         scratch_shapes=[
             pltpu.VMEM((8 * 16, LANES), f32),
@@ -489,6 +505,10 @@
             pltpu.SemaphoreType.DMA((count + 1,)),
             pltpu.SemaphoreType.DMA((count,)),
             pltpu.SemaphoreType.DMA((count,)),
+            pltpu.VMEM(velocity.shape, f32),
+            pltpu.VMEM(inv_mass.shape, f32),
+            pltpu.VMEM(path_weight.shape, f32),
+            pltpu.SemaphoreType.DMA((3,)),
             *carried,
         ],
         compiler_params=pltpu.CompilerParams(
@@ -496,7 +516,7 @@
         ),
         name="step",
     )(
-        spring, center, partner, pairs, ghosts, partial, position, velocity, charges, inv_mass, path_weight, *kept_q
+        spring, center, partner, pairs, ghosts, velocity, inv_mass, path_weight, partial, position, charges, *kept_q
     )
 
 

time: 151 us -> 147 us (0.974)
  Pallas kernels: 137 us -> 134 us
    pallas_call x1, Pallas kernels: 18.6 us -> 16.2 us  [plan(): pl.pallas_call(plan_kernel, out_shape=(jax.ShapeDtypeStruct((GROUPS * 32,...]
  transfers between devices with their start and end apart: 2 -> 2, of which waited for: 0 -> 0; matrix products, arithmetic and copies ran while one was open for 0% -> 0% of each run, Pallas kernels for 12% -> 11%
where the time goes in v7:
time: 147 us
  Pallas kernels  134 us (91%)
  starting transfers between devices  4.69 us (3%)
  between operations  4.32 us (3%)
  local copies, waits for them, and re-layouts  4.14 us (3%)
    pallas_call x2, Pallas kernels, step(): pl.pallas_call(kernel, out_shape=(whole, whole, jax.ShapeDtypeStruct((1,)...  86.9 us
    pallas_call x1, Pallas kernels, first_gather(): pl.pallas_call(first_gather_kernel, out_shape=(jax.ShapeDtypeStruct((3, T...  17.1 us
    pallas_call x1, Pallas kernels, plan(): pl.pallas_call(plan_kernel, out_shape=(jax.ShapeDtypeStruct((GROUPS * 32,...  16.2 us
    pallas_call x1, Pallas kernels, second_gather(): pl.pallas_call(second_gather_kernel, out_shape=jax.ShapeDtypeStruct((3, G...  13.2 us
    ppermute x2, starting transfers between devices, shifted(): return lax.ppermute(shard, axis, pairs)  4.69 us
    unnamed x8, local copies, waits for them, and re-layouts  4.14 us
  transfers between devices with their start and end apart: 2, of which 0 were waited for; matrix products, arithmetic and copies ran while one was open for 0% of the time, Pallas kernels for 11%

profile of v7, /device:TPU:96, one launch (start us, length us, event | category | flops | bytes accessed | tf_op | source)
XLA Modules:
  0.0 146.7 jit_solution(11912973529913929313)
XLA Ops:
  0.6 2.8 %collective-permute-start.1 = (f32[3,512,128]{2,1,0:T(8,128)}, f32[3,512,128]{2,1,0:T(8,128)S(1)}, u32[]{:S(2)}, u32[]{:S(2)}) collective-permute-start(f32[3,512,128]{2,1,0:T(8,128)} %bitcast.23), channel_id=1, source_target_pairs={{8,0},{16,8},{24,16},{32,24},{40,32},{48,40},{56,48},{64,56},{72,6... | collective-permute-start | bytes 2359304 | tf_op jit(solution)/shard_map/ppermute | solution.py:543
  3.4 1.9 %collective-permute-start = (f32[3,512,128]{2,1,0:T(8,128)}, f32[3,512,128]{2,1,0:T(8,128)S(1)}, u32[]{:S(2)}, u32[]{:S(2)}) collective-permute-start(f32[3,512,128]{2,1,0:T(8,128)} %bitcast.24), channel_id=1, source_target_pairs={{0,8},{8,16},{16,24},{24,32},{32,40},{40,48},{48,56},{56,64},{64,7... | collective-permute-start | bytes 2359304 | tf_op jit(solution)/shard_map/ppermute | solution.py:543
  7.3 16.2 %plan.1 = (s32[512,128]{1,0:T(8,128)}, s32[256,128]{1,0:T(8,128)}, s32[40,128]{1,0:T(8,128)}) custom-call(s32[256,128]{1,0:T(8,128)} %bitcast.27), custom_call_target="tpu_custom_call" | custom-call | tf_op jit(solution)/shard_map/plan/pallas_call | solution.py:95
  23.5 0.0 collective-permute-done.1.above
  23.5 0.0 copy-start.1
  23.5 0.0 collective-permute-done.below
  23.5 0.0 copy-start.2
  23.5 0.9 copy-done.1
  24.4 0.3 copy-done.2
  24.7 17.1 %first_gather.1 = (f32[3,512,128]{2,1,0:T(8,128)}, f32[4,256,128]{2,1,0:T(8,128)}, f32[8,128]{1,0:T(8,128)}) custom-call(s32[1]{0:T(128)S(6)} %copy.22.partner.refs_2_, s32[40,128]{1,0:T(8,128)} %get-tuple-element.17.cells, f32[3,512,128]{2,1,0:T(8,128)} %bitcast.25, f32[3,512,128]{2,1,0:T(8,128)} %copy-done.2, f32[3,512,128]{2,1,0:T(8,128)} %copy-done.1, ...), custom_call_target="tpu_custom_call" | custom-call | tf_op jit(solution)/shard_map/first_gather/pallas_call | solution.py:223
  41.8 43.3 %step.2 = (f32[3,512,128]{2,1,0:T(8,128)}, f32[3,512,128]{2,1,0:T(8,128)}, f32[8,128]{1,0:T(8,128)}, f32[128,128]{1,0:T(8,128)}, f32[128,128]{1,0:T(8,128)}) custom-call(f32[1]{0:T(128)S(6)} %copy.24.refs_0_, f32[1]{0:T(128)S(6)} %copy.23.refs_1_, s32[1]{0:T(128)S(6)} %copy.22.partner.refs_2_, s32[2,512]{1,0:T(2,128)} %bitcast.28, ...), custom_call_target="tpu_custom_call" | custom-call | tf_op jit(solution)/shard_map/step/pallas_call | solution.py:485
  85.1 13.2 %second_gather.1.refs_4_ = f32[3,256,128]{2,1,0:T(8,128)} custom-call(s32[40,128]{1,0:T(8,128)} %get-tuple-element.17.cells, f32[3,512,128]{2,1,0:T(8,128)} %get-tuple-element.23.refs_0_.refs_9_, s32[512,128]{1,0:T(8,128)} %get-tuple-element.18.source.refs_1_, s32[256,128]{1,0:T(8,128)} %get-tuple-element.19.place.refs_2_), custom_call_target="tpu_custom_call" | custom-call | tf_op jit(solution)/shard_map/second_gather/pallas_call | solution.py:529
  98.3 43.6 %step.3 = (f32[3,512,128]{2,1,0:T(8,128)}, f32[3,512,128]{2,1,0:T(8,128)}, f32[1]{0:T(128)}) custom-call(f32[1]{0:T(128)S(6)} %copy.24.refs_0_, f32[1]{0:T(128)S(6)} %copy.23.refs_1_, s32[1]{0:T(128)S(6)} %copy.22.partner.refs_2_, s32[2,512]{1,0:T(2,128)} %bitcast.29, f32[3,256,128]{2,1,0:T(8,128)} %second_gather.1.refs_4_, ...), custom_call_target="tpu_custom_call" | custom-call | tf_op jit(solution)/shard_map/step/pallas_call | solution.py:485
  141.9 0.0 copy-start
  141.9 2.1 %copy.25 = f32[1,3,65536]{2,0,1:T(1,128)} copy(f32[1,3,65536]{2,0,1:T(1,128)} %bitcast.22) | data formatting | bytes 1572864
  144.1 0.0 copy-done
  144.1 0.9 copy.26
Async XLA Ops:
  0.6 22.9 %collective-permute-start.1 = (f32[3,512,128]{2,1,0:T(8,128)}, f32[3,512,128]{2,1,0:T(8,128)S(1)}, u32[]{:S(2)}, u32[]{:S(2)}) collective-permute-start(f32[3,512,128]{2,1,0:T(8,128)} %bitcast.23), channel_id=1, source_target_pairs={{8,0},{16,8},{24,16},{32,24},{40,32},{48,40},{56,48},{64,56},{72,6... | collective-permute-start | bytes 2359304 | tf_op jit(solution)/shard_map/ppermute | solution.py:543
  3.4 20.1 %collective-permute-start = (f32[3,512,128]{2,1,0:T(8,128)}, f32[3,512,128]{2,1,0:T(8,128)S(1)}, u32[]{:S(2)}, u32[]{:S(2)}) collective-permute-start(f32[3,512,128]{2,1,0:T(8,128)} %bitcast.24), channel_id=1, source_target_pairs={{0,8},{8,16},{16,24},{24,32},{32,40},{40,48},{48,56},{56,64},{64,7... | collective-permute-start | bytes 2359304 | tf_op jit(solution)/shard_map/ppermute | solution.py:543
  23.5 0.9 copy-start.1
  23.5 1.1 copy-start.2
  141.9 2.1 %copy-start = (f32[3,512,128]{2,1,0:T(8,128)S(1)}, f32[3,512,128]{2,1,0:T(8,128)}, u32[]{:S(2)}) copy-start(f32[3,512,128]{2,1,0:T(8,128)} %get-tuple-element.29) | copy-start | bytes 2359300

commit v8 on v7

--- a/solution.py
+++ b/solution.py
@@ -22,7 +22,7 @@
 
 
 def params():
-    return pltpu.CompilerParams(vmem_limit_bytes=58 * 1024 * 1024)
+    return pltpu.CompilerParams(vmem_limit_bytes=20 * 1024 * 1024)
 
 
 def plan_kernel(halo, source, place, cells, ranks, counts):
@@ -45,7 +45,7 @@
         counts[...] = jnp.where(lane == group, within[:, LANES:], counts[...])
         return carry
 
-    lax.fori_loop(0, GROUPS, count_group, 0)
+    lax.fori_loop(0, GROUPS, count_group, 0, unroll=4)
     earlier = jnp.dot(ahead_row, counts[...].astype(bf16), preferred_element_type=f32)
     total = (earlier[GHOST_ROWS - 1 :] + counts[GHOST_ROWS - 1 :, :]).astype(jnp.int32)
     earlier = earlier.astype(jnp.int32)
@@ -88,7 +88,11 @@
         source[pl.ds(pl.multiple_of(group * 32, 32), 32), :] = items & 4095
         return carry
 
-    lax.fori_loop(0, GROUPS, one_group, 0)
+    def two_groups(pair, carry):
+        one_group(2 * pair, carry)
+        return one_group(2 * pair + 1, carry)
+
+    lax.fori_loop(0, GROUPS // 2, two_groups, 0)
 
 
 def plan(halo):
@@ -142,7 +146,7 @@
 
         lax.fori_loop(0, (most + 255) >> 8, list_rows, 0)
 
-    def slot_block(t, carry):
+    def slot_block(t):
         here = pl.ds(pl.multiple_of(t * 8, 8), 8)
         at = place[here, :]
         lane = at & 127
@@ -163,19 +167,20 @@
             begin, end = cells[t, g], cells[t + 1, g]
             return g * 32 + jnp.minimum(begin >> 7, 31), g * 32 + (jnp.maximum(end - 1, begin) >> 7)
 
-        accs = zeros
-        widest = 0
-        for g in range(GROUPS):
-            first, last = rows_of(g)
-            last = jnp.minimum(last, g * 32 + 31)
-            accs = visit(first, accs)
-            accs = visit(last, accs)
-            widest = jnp.maximum(widest, last - first)
-        for c in range(comps):
-            out[c, here, :] = accs[c]
-
-        @pl.when(widest > 1)
-        def _():
+        def narrow():
+            accs = zeros
+            widest = 0
+            for g in range(GROUPS):
+                first, last = rows_of(g)
+                last = jnp.minimum(last, g * 32 + 31)
+                accs = visit(first, accs)
+                accs = visit(last, accs)
+                widest = jnp.maximum(widest, last - first)
+            for c in range(comps):
+                out[c, here, :] = accs[c]
+            return widest
+
+        def wide():
             def rest(g, accs):
                 first, last = rows_of(g)
                 return lax.fori_loop(first, jnp.minimum(last, g * 32 + 31) + 1, visit, accs)
@@ -184,9 +189,20 @@
             for c in range(comps):
                 out[c, here, :] = more[c]
 
+        return narrow, wide
+
+    def slot_blocks(n, carry):
+        blocks = [slot_block(2 * n + k) for k in range(2)]
+        widest = [narrow() for narrow, _ in blocks]
+
+        @pl.when(jnp.maximum(*widest) > 1)
+        def _():
+            for _, wide in blocks:
+                wide()
+
         return carry
 
-    lax.fori_loop(0, GHOST_ROWS // 8, slot_block, 0)
+    lax.fori_loop(0, GHOST_ROWS // 16, slot_blocks, 0)
 
 
 def pick(partner, window, own, below, above):
@@ -512,7 +528,7 @@
             *carried,
         ],
         compiler_params=pltpu.CompilerParams(
-            vmem_limit_bytes=58 * 1024 * 1024, collective_id=number, has_side_effects=True
+            vmem_limit_bytes=40 * 1024 * 1024, collective_id=number, has_side_effects=True
         ),
         name="step",
     )(

time: 147 us -> 136 us (0.925)
  Pallas kernels: 134 us -> 117 us
  waiting for transfers between devices: 0.01 us -> 3.62 us
  local copies, waits for them, and re-layouts: 4.14 us -> 6.35 us
    pallas_call x2, Pallas kernels: 86.9 us -> 80.6 us  [step(): pl.pallas_call(kernel, out_shape=(whole, whole, jax.ShapeDtypeStruct((1,)...]
    pallas_call x1, Pallas kernels: 16.2 us -> 10.7 us  [plan(): pl.pallas_call(plan_kernel, out_shape=(jax.ShapeDtypeStruct((GROUPS * 32,...]
    ppermute x2, waiting for transfers between devices: 0.01 us -> 3.62 us  [shifted(): return lax.ppermute(shard, axis, pairs)]
    pallas_call x1, Pallas kernels: 17.1 us -> 14.4 us  [first_gather(): pl.pallas_call(first_gather_kernel, out_shape=(jax.ShapeDtypeStruct((3, T...]
    unnamed x8 -> x20, local copies, waits for them, and re-layouts: 4.14 us -> 6.35 us
    pallas_call x1, Pallas kernels: 13.2 us -> 11 us  [second_gather(): pl.pallas_call(second_gather_kernel, out_shape=jax.ShapeDtypeStruct((3, G...]
  transfers between devices with their start and end apart: 2 -> 2, of which waited for: 0 -> 2; matrix products, arithmetic and copies ran while one was open for 0% -> 0% of each run, Pallas kernels for 11% -> 8%
where the time goes in v8:
time: 136 us
  Pallas kernels  117 us (86%)
  local copies, waits for them, and re-layouts  6.35 us (5%)
  starting transfers between devices  4.69 us (3%)
  between operations  4.44 us (3%)
  waiting for transfers between devices  3.62 us (3%)
    pallas_call x2, Pallas kernels, step(): pl.pallas_call(kernel, out_shape=(whole, whole, jax.ShapeDtypeStruct((1,)...  80.6 us
    pallas_call x1, Pallas kernels, first_gather(): pl.pallas_call(first_gather_kernel, out_shape=(jax.ShapeDtypeStruct((3, T...  14.4 us
    pallas_call x1, Pallas kernels, second_gather(): pl.pallas_call(second_gather_kernel, out_shape=jax.ShapeDtypeStruct((3, G...  11 us
    pallas_call x1, Pallas kernels, plan(): pl.pallas_call(plan_kernel, out_shape=(jax.ShapeDtypeStruct((GROUPS * 32,...  10.7 us
    unnamed x20, local copies, waits for them, and re-layouts  6.35 us
    ppermute x2, starting transfers between devices, shifted(): return lax.ppermute(shard, axis, pairs)  4.69 us
    ppermute x2, waiting for transfers between devices, shifted(): return lax.ppermute(shard, axis, pairs)  3.62 us
  transfers between devices with their start and end apart: 2, of which 2 were waited for; matrix products, arithmetic and copies ran while one was open for 0% of the time, Pallas kernels for 8%

profile of v8, /device:TPU:96, one launch (start us, length us, event | category | flops | bytes accessed | tf_op | source)
XLA Modules:
  0.0 135.9 jit_solution(5172182643289818135)
XLA Ops:
  0.6 2.8 %collective-permute-start.1 = (f32[3,512,128]{2,1,0:T(8,128)}, f32[3,512,128]{2,1,0:T(8,128)S(1)}, u32[]{:S(2)}, u32[]{:S(2)}) collective-permute-start(f32[3,512,128]{2,1,0:T(8,128)} %bitcast.23), channel_id=1, source_target_pairs={{8,0},{16,8},{24,16},{32,24},{40,32},{48,40},{56,48},{64,56},{72,6... | collective-permute-start | bytes 2359304 | tf_op jit(solution)/shard_map/ppermute | solution.py:559
  3.4 1.9 %collective-permute-start = (f32[3,512,128]{2,1,0:T(8,128)}, f32[3,512,128]{2,1,0:T(8,128)S(1)}, u32[]{:S(2)}, u32[]{:S(2)}) collective-permute-start(f32[3,512,128]{2,1,0:T(8,128)} %bitcast.24), channel_id=1, source_target_pairs={{0,8},{8,16},{16,24},{24,32},{32,40},{40,48},{48,56},{56,64},{64,7... | collective-permute-start | bytes 2359304 | tf_op jit(solution)/shard_map/ppermute | solution.py:559
  7.3 0.0 copy-start.7
  7.3 0.9 copy-done.7
  8.2 10.7 %plan.1 = (s32[512,128]{1,0:T(8,128)S(1)}, s32[256,128]{1,0:T(8,128)S(1)}, s32[40,128]{1,0:T(8,128)S(1)}) custom-call(s32[256,128]{1,0:T(8,128)S(1)} %bitcast.27), custom_call_target="tpu_custom_call" | custom-call | tf_op jit(solution)/shard_map/plan/pallas_call | solution.py:99
  18.9 0.6 collective-permute-done.1.above
  19.5 3.1 %collective-permute-done.below = f32[3,512,128]{2,1,0:T(8,128)S(1)} collective-permute-done((f32[3,512,128]{2,1,0:T(8,128)}, f32[3,512,128]{2,1,0:T(8,128)S(1)}, u32[]{:S(2)}, u32[]{:S(2)}) %collective-permute-start) | collective-permute-done | bytes 786464 | tf_op jit(solution)/shard_map/ppermute | solution.py:559
  22.6 0.0 copy-start
  22.6 0.9 copy-done
  23.5 0.9 copy-done.2
  24.5 0.0 copy-start.5
  24.5 1.1 copy-done.5
  25.6 14.4 %first_gather.1 = (f32[3,512,128]{2,1,0:T(8,128)S(1)}, f32[4,256,128]{2,1,0:T(8,128)S(1)}, f32[8,128]{1,0:T(8,128)S(1)}) custom-call(s32[1]{0:T(128)S(6)} %copy.22.partner.refs_2_, s32[40,128]{1,0:T(8,128)S(1)} %get-tuple-element.17.cells, f32[3,512,128]{2,1,0:T(8,128)S(1)} %bitcast.25, f32[3,512,128]{2,1,0:T(8,128)S(1)} %collective-permute-done.below, ...), custom_call_target="tpu_custom_call" | custom-call | tf_op jit(solution)/shard_map/first_gather/pallas_call | solution.py:239
  40.0 0.0 copy-start.8
  40.0 0.0 copy-done.1
  40.0 0.0 copy-done.3
  40.0 0.0 copy-done.4
  40.0 0.0 copy-done.6
  40.0 0.6 copy-done.8
  40.7 39.7 %step.2 = (f32[3,512,128]{2,1,0:T(8,128)S(1)}, f32[3,512,128]{2,1,0:T(8,128)S(1)}, f32[8,128]{1,0:T(8,128)S(1)}, f32[128,128]{1,0:T(8,128)S(1)}, f32[128,128]{1,0:T(8,128)S(1)}) custom-call(f32[1]{0:T(128)S(6)} %copy.24.refs_0_, f32[1]{0:T(128)S(6)} %copy.23.refs_1_, s32[1]{0:T(128)S(6)} %copy.22.partner.refs_2_, s32[2,512]{1,0:T(2,128)S(1)} %bitcast.28, ...), custom_call_target="tpu_custom_call" | custom-call | tf_op jit(solution)/shard_map/step/pallas_call | solution.py:501
  80.3 11.0 %second_gather.1.refs_4_ = f32[3,256,128]{2,1,0:T(8,128)S(1)} custom-call(s32[40,128]{1,0:T(8,128)S(1)} %get-tuple-element.17.cells, f32[3,512,128]{2,1,0:T(8,128)S(1)} %get-tuple-element.23.refs_0_.refs_9_, s32[512,128]{1,0:T(8,128)S(1)} %get-tuple-element.18.source.refs_1_, s32[256,128]{1,0:T(8,128)S(1)} %get-tuple-element.19.place.refs_2_), custom_call_target="tpu_custom_call" | custom-call | tf_op jit(solution)/shard_map/second_gather/pallas_call | solution.py:545
  91.4 41.0 %step.3 = (f32[3,512,128]{2,1,0:T(8,128)S(1)}, f32[3,512,128]{2,1,0:T(8,128)S(1)}, f32[1]{0:T(128)}) custom-call(f32[1]{0:T(128)S(6)} %copy.24.refs_0_, f32[1]{0:T(128)S(6)} %copy.23.refs_1_, s32[1]{0:T(128)S(6)} %copy.22.partner.refs_2_, s32[2,512]{1,0:T(2,128)S(1)} %bitcast.29, f32[3,256,128]{2,1,0:T(8,128)S(1)} %second_gather.1.refs_4_, ...), custom_call_target="tpu_custom_call" | custom-call | tf_op jit(solution)/shard_map/step/pallas_call | solution.py:501
  132.4 0.9 copy.25
  133.2 0.9 copy.26
  (5 shorter events, 0.0 us)
Async XLA Ops:
  0.6 18.9 %collective-permute-start.1 = (f32[3,512,128]{2,1,0:T(8,128)}, f32[3,512,128]{2,1,0:T(8,128)S(1)}, u32[]{:S(2)}, u32[]{:S(2)}) collective-permute-start(f32[3,512,128]{2,1,0:T(8,128)} %bitcast.23), channel_id=1, source_target_pairs={{8,0},{16,8},{24,16},{32,24},{40,32},{48,40},{56,48},{64,56},{72,6... | collective-permute-start | bytes 2359304 | tf_op jit(solution)/shard_map/ppermute | solution.py:559
  3.4 19.2 %collective-permute-start = (f32[3,512,128]{2,1,0:T(8,128)}, f32[3,512,128]{2,1,0:T(8,128)S(1)}, u32[]{:S(2)}, u32[]{:S(2)}) collective-permute-start(f32[3,512,128]{2,1,0:T(8,128)} %bitcast.24), channel_id=1, source_target_pairs={{0,8},{8,16},{16,24},{24,32},{32,40},{40,48},{48,56},{56,64},{64,7... | collective-permute-start | bytes 2359304 | tf_op jit(solution)/shard_map/ppermute | solution.py:559
  7.3 0.9 copy-start.7
  22.6 1.0 copy-start
  23.5 0.9 copy-start.2
  24.5 1.1 copy-start.5
  25.6 14.4 %copy-start.1 = (f32[65536]{0:T(1024)S(1)}, f32[65536]{0:T(1024)}, u32[]{:S(2)}) copy-start(f32[65536]{0:T(1024)} %param.12) | copy-start | bytes 786436
  25.6 14.4 %copy-start.3 = (f32[65536]{0:T(1024)S(1)}, f32[65536]{0:T(1024)}, u32[]{:S(2)}) copy-start(f32[65536]{0:T(1024)} %param.14) | copy-start | bytes 786436
  25.6 14.4 %copy-start.4 = (f32[65536]{0:T(1024)S(1)}, f32[65536]{0:T(1024)}, u32[]{:S(2)}) copy-start(f32[65536]{0:T(1024)} %param.13) | copy-start | bytes 786436
  25.6 14.4 %copy-start.6 = (f32[1,3,65536]{2,0,1:T(1,128)S(1)}, f32[1,3,65536]{2,0,1:T(1,128)}, u32[]{:S(2)}) copy-start(f32[1,3,65536]{2,0,1:T(1,128)} %param.11) | copy-start | bytes 2359300
  40.0 0.7 copy-start.8

commit v9 on v8

--- a/solution.py
+++ b/solution.py
@@ -107,6 +107,7 @@
         out_specs=(VMEM,) * 3,
         scratch_shapes=[pltpu.VMEM((GHOST_ROWS, LANES), jnp.int32), pltpu.VMEM((GHOST_ROWS, LANES), f32)],
         compiler_params=params(),
+        cost_estimate=pl.CostEstimate(flops=10_000_000_000, bytes_accessed=40_000_000, transcendentals=0),
         name="plan",
     )(halo)
 
@@ -247,6 +248,7 @@
         out_specs=(VMEM,) * 3,
         scratch_shapes=gather_scratch(4),
         compiler_params=params(),
+        cost_estimate=pl.CostEstimate(flops=10_000_000_000, bytes_accessed=40_000_000, transcendentals=0),
         name="first_gather",
     )(partner, cells, own, below, above, charges, path_weight, source, place)
 
@@ -444,36 +446,43 @@
             return own
         return pick(partner[0], window, own, velocity_below[c, here, :], velocity_above[c, here, :])
 
-    def combine(b, part):
-        base = pl.multiple_of(b * 8, 8)
-        here = pl.ds(base, 8)
-        total = []
-        for k in range(4):
-            value = sums[pl.ds(base * 16 + k, 8, stride=16), :]
-            value = value + sums[pl.ds(base * 16 + 4 + k, 8, stride=16), :]
-            value = value + sums[pl.ds(base * 16 + 8 + k, 8, stride=16), :]
-            total.append(value)
-        q = charges[here, :]
-        weight = path_weight[here, :]
-        rate = time_step * inv_mass[here, :]
-        for c in range(3):
-            old = position[c, here, :]
-            force = q * (old * total[0] - total[c + 1])
-            if c == 2:
-                force = force - pull * weight
-            moved = velocity_at(c, here) + rate * force
-            placed = old + time_step * moved
-            new_velocity[c, here, :] = moved
-            new_position[c, here, :] = placed
-        return part + weight * placed
-
-    ending = lax.fori_loop(0, TILES // 8, combine, jnp.zeros((8, LANES), f32))
+    def combine(components):
+        def block(b, part):
+            base = pl.multiple_of(b * 8, 8)
+            here = pl.ds(base, 8)
+
+            def summed(k):
+                value = sums[pl.ds(base * 16 + k, 8, stride=16), :]
+                value = value + sums[pl.ds(base * 16 + 4 + k, 8, stride=16), :]
+                return value + sums[pl.ds(base * 16 + 8 + k, 8, stride=16), :]
+
+            base_sum = summed(0)
+            q = charges[here, :]
+            weight = path_weight[here, :]
+            rate = time_step * inv_mass[here, :]
+            for c in components:
+                old = position[c, here, :]
+                force = q * (old * base_sum - summed(c + 1))
+                if c == 2:
+                    force = force - pull * weight
+                moved = velocity_at(c, here) + rate * force
+                placed = old + time_step * moved
+                new_velocity[c, here, :] = moved
+                new_position[c, here, :] = placed
+                if c == 2:
+                    part = part + weight * placed
+            return part
+
+        return lax.fori_loop(0, TILES // 8, block, jnp.zeros((8, LANES), f32))
+
+    ending = combine((2,) if last else (0, 1, 2))
     if last:
         partial_last = spread_a.at[0, pl.ds(0, 8), :]
         spread_a[0, pl.ds(0, 8), :] = ending
         final_copies = [
             send(partial_last, final.at[me], k, sent_last.at[k], got_last.at[k]) for k in range(1, count)
         ]
+        combine((0, 1))
         off = total_of(final, partial_last, final_copies) - center[0]
         result[0] = 0.5 * spring[0] * off * off
     else:
@@ -549,6 +558,7 @@
         out_specs=VMEM,
         scratch_shapes=gather_scratch(3),
         compiler_params=params(),
+        cost_estimate=pl.CostEstimate(flops=10_000_000_000, bytes_accessed=40_000_000, transcendentals=0),
         name="second_gather",
     )(cells, position, source, place)
 

time: 136 us -> 133 us (0.978)
  local copies, waits for them, and re-layouts: 6.35 us -> 3.34 us
    unnamed x20 -> x16, local copies, waits for them, and re-layouts: 6.35 us -> 3.34 us
where the time goes in v9:
time: 133 us; the launch traced here: 132 us
  Pallas kernels  116 us (87%)
  starting transfers between devices  4.68 us (4%)
  between operations  4.44 us (3%)
  waiting for transfers between devices  3.62 us (3%)
  local copies, waits for them, and re-layouts  3.34 us (3%)
    pallas_call x2, Pallas kernels, step(): pl.pallas_call(kernel, out_shape=(whole, whole, jax.ShapeDtypeStruct((1,)...  80.2 us
    pallas_call x1, Pallas kernels, first_gather(): pl.pallas_call(first_gather_kernel, out_shape=(jax.ShapeDtypeStruct((3, T...  14.3 us
    pallas_call x1, Pallas kernels, second_gather(): pl.pallas_call(second_gather_kernel, out_shape=jax.ShapeDtypeStruct((3, G...  11 us
    pallas_call x1, Pallas kernels, plan(): pl.pallas_call(plan_kernel, out_shape=(jax.ShapeDtypeStruct((GROUPS * 32,...  10.8 us
    ppermute x2, starting transfers between devices, shifted(): return lax.ppermute(shard, axis, pairs)  4.68 us
    ppermute x2, waiting for transfers between devices, shifted(): return lax.ppermute(shard, axis, pairs)  3.62 us
    unnamed x16, local copies, waits for them, and re-layouts  3.34 us
  transfers between devices with their start and end apart: 2, of which 2 were waited for; matrix products, arithmetic and copies ran while one was open for 0% of the time, Pallas kernels for 8%

profile of v9, /device:TPU:96, one launch (start us, length us, event | category | flops | bytes accessed | tf_op | source)
XLA Modules:
  0.0 132.4 jit_solution(11157200227979837732)
XLA Ops:
  0.6 2.8 %collective-permute-start.1 = (f32[3,512,128]{2,1,0:T(8,128)}, f32[3,512,128]{2,1,0:T(8,128)S(1)}, u32[]{:S(2)}, u32[]{:S(2)}) collective-permute-start(f32[3,512,128]{2,1,0:T(8,128)} %bitcast.26), channel_id=1, source_target_pairs={{8,0},{16,8},{24,16},{32,24},{40,32},{48,40},{56,48},{64,56},{72,6... | collective-permute-start | bytes 2359304 | tf_op jit(solution)/shard_map/ppermute | solution.py:569
  3.4 1.9 %collective-permute-start = (f32[3,512,128]{2,1,0:T(8,128)}, f32[3,512,128]{2,1,0:T(8,128)S(1)}, u32[]{:S(2)}, u32[]{:S(2)}) collective-permute-start(f32[3,512,128]{2,1,0:T(8,128)} %bitcast.27), channel_id=1, source_target_pairs={{0,8},{8,16},{16,24},{24,32},{32,40},{40,48},{48,56},{56,64},{64,7... | collective-permute-start | bytes 2359304 | tf_op jit(solution)/shard_map/ppermute | solution.py:569
  7.3 0.0 copy-start.6
  7.3 0.9 copy-done.6
  8.2 0.0 copy-start
  8.2 0.0 copy-start.1
  8.2 10.8 %plan.1 = (s32[512,128]{1,0:T(8,128)S(1)}, s32[256,128]{1,0:T(8,128)S(1)}, s32[40,128]{1,0:T(8,128)S(1)}) custom-call(s32[256,128]{1,0:T(8,128)S(1)} %bitcast.29), custom_call_target="tpu_custom_call" | custom-call | flops 10000000000 | bytes 40000000 | tf_op jit(solution)/shard_map/plan/pallas_call | solution.py:99
  18.9 0.5 collective-permute-done.1.above
  19.5 3.1 %collective-permute-done.below = f32[3,512,128]{2,1,0:T(8,128)S(1)} collective-permute-done((f32[3,512,128]{2,1,0:T(8,128)}, f32[3,512,128]{2,1,0:T(8,128)S(1)}, u32[]{:S(2)}, u32[]{:S(2)}) %collective-permute-start) | collective-permute-done | bytes 786464 | tf_op jit(solution)/shard_map/ppermute | solution.py:569
  22.6 0.0 copy-done
  22.6 0.0 copy-done.1
  22.6 0.0 copy-done.5
  22.6 0.0 copy-start.2
  22.6 0.0 copy-start.3
  22.6 14.3 %first_gather.1 = (f32[3,512,128]{2,1,0:T(8,128)S(1)}, f32[4,256,128]{2,1,0:T(8,128)S(1)}, f32[8,128]{1,0:T(8,128)S(1)}) custom-call(s32[1]{0:T(128)S(6)} %copy.22.partner.refs_2_, s32[40,128]{1,0:T(8,128)S(1)} %get-tuple-element.17.cells, f32[3,512,128]{2,1,0:T(8,128)S(1)} %bitcast.28, f32[3,512,128]{2,1,0:T(8,128)S(1)} %collective-permute-done.below, ...), custom_call_target="tpu_custom_call" | custom-call | flops 10000000000 | bytes 40000000 | tf_op jit(solution)/shard_map/first_gather/pallas_call | solution.py:240
  36.9 0.0 copy-start.4
  36.9 0.0 copy-done.2
  36.9 0.0 copy-done.3
  36.9 0.7 copy-done.4
  37.6 39.7 %step.2 = (f32[3,512,128]{2,1,0:T(8,128)S(1)}, f32[3,512,128]{2,1,0:T(8,128)S(1)}, f32[8,128]{1,0:T(8,128)S(1)}, f32[128,128]{1,0:T(8,128)S(1)}, f32[128,128]{1,0:T(8,128)S(1)}) custom-call(f32[1]{0:T(128)S(6)} %copy.24.refs_0_, f32[1]{0:T(128)S(6)} %copy.23.refs_1_, s32[1]{0:T(128)S(6)} %copy.22.partner.refs_2_, s32[2,512]{1,0:T(2,128)S(1)} %bitcast.24, ...), custom_call_target="tpu_custom_call" | custom-call | tf_op jit(solution)/shard_map/step/pallas_call | solution.py:510
  77.3 11.0 %second_gather.1.refs_4_ = f32[3,256,128]{2,1,0:T(8,128)S(1)} custom-call(s32[40,128]{1,0:T(8,128)S(1)} %get-tuple-element.17.cells, f32[3,512,128]{2,1,0:T(8,128)S(1)} %get-tuple-element.23.refs_0_.refs_9_, s32[512,128]{1,0:T(8,128)S(1)} %get-tuple-element.18.source.refs_1_, s32[256,128]{1,0:T(8,128)S(1)} %get-tuple-element.19.place.refs_2_), custom_call_target="tpu_custom_call" | custom-call | flops 10000000000 | bytes 40000000 | tf_op jit(solution)/shard_map/second_gather/pallas_call | solution.py:554
  88.4 40.5 %step.3 = (f32[3,512,128]{2,1,0:T(8,128)S(1)}, f32[3,512,128]{2,1,0:T(8,128)S(1)}, f32[1]{0:T(128)}) custom-call(f32[1]{0:T(128)S(6)} %copy.24.refs_0_, f32[1]{0:T(128)S(6)} %copy.23.refs_1_, s32[1]{0:T(128)S(6)} %copy.22.partner.refs_2_, s32[2,512]{1,0:T(2,128)S(1)} %bitcast.25, f32[3,256,128]{2,1,0:T(8,128)S(1)} %second_gather.1.refs_4_, ...), custom_call_target="tpu_custom_call" | custom-call | tf_op jit(solution)/shard_map/step/pallas_call | solution.py:510
  128.9 0.9 copy.25
  129.7 0.9 copy.26
  (1 shorter events, 0.0 us)
Async XLA Ops:
  0.6 18.9 %collective-permute-start.1 = (f32[3,512,128]{2,1,0:T(8,128)}, f32[3,512,128]{2,1,0:T(8,128)S(1)}, u32[]{:S(2)}, u32[]{:S(2)}) collective-permute-start(f32[3,512,128]{2,1,0:T(8,128)} %bitcast.26), channel_id=1, source_target_pairs={{8,0},{16,8},{24,16},{32,24},{40,32},{48,40},{56,48},{64,56},{72,6... | collective-permute-start | bytes 2359304 | tf_op jit(solution)/shard_map/ppermute | solution.py:569
  3.4 19.2 %collective-permute-start = (f32[3,512,128]{2,1,0:T(8,128)}, f32[3,512,128]{2,1,0:T(8,128)S(1)}, u32[]{:S(2)}, u32[]{:S(2)}) collective-permute-start(f32[3,512,128]{2,1,0:T(8,128)} %bitcast.27), channel_id=1, source_target_pairs={{0,8},{8,16},{16,24},{24,32},{32,40},{40,48},{48,56},{56,64},{64,7... | collective-permute-start | bytes 2359304 | tf_op jit(solution)/shard_map/ppermute | solution.py:569
  7.3 0.9 copy-start.6
  8.2 14.4 %copy-start = (f32[65536]{0:T(1024)S(1)}, f32[65536]{0:T(1024)}, u32[]{:S(2)}) copy-start(f32[65536]{0:T(1024)} %param.12) | copy-start | bytes 786436
  8.2 14.4 %copy-start.1 = (f32[65536]{0:T(1024)S(1)}, f32[65536]{0:T(1024)}, u32[]{:S(2)}) copy-start(f32[65536]{0:T(1024)} %param.14) | copy-start | bytes 786436
  8.2 14.4 %copy-start.5 = (f32[1,3,65536]{2,0,1:T(1,128)S(1)}, f32[1,3,65536]{2,0,1:T(1,128)}, u32[]{:S(2)}) copy-start(f32[1,3,65536]{2,0,1:T(1,128)} %param.10) | copy-start | bytes 2359300
  22.6 14.3 %copy-start.2 = (f32[65536]{0:T(1024)S(1)}, f32[65536]{0:T(1024)}, u32[]{:S(2)}) copy-start(f32[65536]{0:T(1024)} %param.13) | copy-start | bytes 786436
  22.6 14.3 %copy-start.3 = (f32[1,3,65536]{2,0,1:T(1,128)S(1)}, f32[1,3,65536]{2,0,1:T(1,128)}, u32[]{:S(2)}) copy-start(f32[1,3,65536]{2,0,1:T(1,128)} %param.11) | copy-start | bytes 2359300
  36.9 0.7 copy-start.4

commit v10 on v9

--- a/solution.py
+++ b/solution.py
@@ -13,7 +13,8 @@
 GROUP_ROWS = 32
 CELLS = 32
 CAPACITY = 4096
-TILES_AT_ONCE = 16
+TILES_AT_ONCE = 32
+ROW_SETS = 4
 time_step = 0.1
 f32 = jnp.float32
 bf16 = jnp.bfloat16
@@ -297,47 +298,51 @@
 
     zero8 = jnp.zeros((8, LANES), f32)
     one8 = jnp.ones((8, LANES), f32)
-    for f in (13, 14, 15):
-        rows_j[pl.ds(f, 8, stride=16), :] = zero8
-    rows_j[pl.ds(12, 8, stride=16), :] = one8
-    for f in (12, 13, 14, 15):
-        rows_a[pl.ds(f, 8, stride=16), :] = zero8
+    many_rows = ROW_SETS
     rows_i[...] = jnp.zeros_like(rows_i)
-    for f in (9, 10, 11):
-        rows_i[pl.ds(f, 8, stride=48), :] = one8
-
-    def build(first_tile, x, y, z, q, own):
+    for k in range(many_rows):
+        for f in (13, 14, 15):
+            rows_j[pl.ds(128 * k + f, 8, stride=16), :] = zero8
+        rows_j[pl.ds(128 * k + 12, 8, stride=16), :] = one8
+        for f in (12, 13, 14, 15):
+            rows_a[pl.ds(128 * k + f, 8, stride=16), :] = zero8
+        for f in (9, 10, 11):
+            rows_i[pl.ds(384 * k + f, 8, stride=48), :] = one8
+
+    def build(k_rows, first_tile, x, y, z, q, own):
+        at_j, at_i = 128 * k_rows, 384 * k_rows
         norm = x * x + y * y + z * z
         split = [parts3(value) for value in (x, y, z)]
         for c in range(3):
             for s in range(3):
-                rows_j[pl.ds(3 * s + c, 8, stride=16), :] = split[c][s]
+                rows_j[pl.ds(at_j + 3 * s + c, 8, stride=16), :] = split[c][s]
         for s, value in enumerate(parts3(norm)):
-            rows_j[pl.ds(9 + s, 8, stride=16), :] = value
+            rows_j[pl.ds(at_j + 9 + s, 8, stride=16), :] = value
         for k, value in enumerate((q, q * x, q * y, q * z)):
             for s, piece in enumerate(parts3(value)):
-                rows_a[pl.ds(4 * s + k, 8, stride=16), :] = piece
+                rows_a[pl.ds(at_j + 4 * s + k, 8, stride=16), :] = piece
         for n in range(8):
-            feat_j[first_tile + n] = rows_j[16 * n : 16 * n + 16, :].astype(bf16)
-            feat_a[first_tile + n] = rows_a[16 * n : 16 * n + 16, :].astype(bf16)
+            feat_j[first_tile + n] = rows_j[at_j + 16 * n : at_j + 16 * n + 16, :].astype(bf16)
+            feat_a[first_tile + n] = rows_a[at_j + 16 * n : at_j + 16 * n + 16, :].astype(bf16)
         if own:
             for c in range(3):
                 for s in range(3):
                     value = -2.0 * split[c][s]
                     for j in range(3 - s):
-                        rows_i[pl.ds(16 * s + 3 * j + c, 8, stride=48), :] = value
+                        rows_i[pl.ds(at_i + 16 * s + 3 * j + c, 8, stride=48), :] = value
             for s, value in enumerate(parts3(norm + 1.0)):
-                rows_i[pl.ds(16 * s + 12, 8, stride=48), :] = value
+                rows_i[pl.ds(at_i + 16 * s + 12, 8, stride=48), :] = value
             for n in range(8):
-                feat_i[first_tile + n] = rows_i[48 * n : 48 * n + 48, :].astype(bf16)
-
-    def own_block(b, carry):
-        base = pl.multiple_of(b * 8, 8)
-        here = pl.ds(base, 8)
-        build(base, position[0, here, :], position[1, here, :], position[2, here, :], charges[here, :], True)
+                feat_i[first_tile + n] = rows_i[at_i + 48 * n : at_i + 48 * n + 48, :].astype(bf16)
+
+    def own_block(n, carry):
+        for k in range(many_rows):
+            base = pl.multiple_of((n * many_rows + k) * 8, 8)
+            here = pl.ds(base, 8)
+            build(k, base, position[0, here, :], position[1, here, :], position[2, here, :], charges[here, :], True)
         return carry
 
-    lax.fori_loop(0, TILES // 16, own_block, 0)
+    lax.fori_loop(0, TILES // 16 // many_rows, own_block, 0)
     pl.semaphore_wait(barrier, count - 1 if last else count + 1)
 
     def send(source, target, k, sent_now, got_now):
@@ -357,14 +362,18 @@
         send(ghosts.at[:, pl.ds(0, half)], upper, count - 1, sent.at[count], got.at[count]),
     ]
     term_copies = [send(partial, parts.at[me], k, sent.at[k], got.at[k]) for k in range(1, count)]
-    lax.fori_loop(TILES // 16, TILES // 8, own_block, 0)
+    lax.fori_loop(TILES // 16 // many_rows, TILES // 8 // many_rows, own_block, 0)
 
     def ghost_block(values, charge, offset):
-        def block(b, carry):
+        def block(n, carry):
+            for k in range(many_rows):
+                one_ghost_block(n * many_rows + k, k)
+            return carry
+
+        def one_ghost_block(b, k):
             base = pl.multiple_of(b * 8, 8)
             here = pl.ds(base, 8)
-            build(offset + base, values[0, here, :], values[1, here, :], values[2, here, :], charge[here, :], False)
-            return carry
+            build(k, offset + base, values[0, here, :], values[1, here, :], values[2, here, :], charge[here, :], False)
 
         return block
 
@@ -390,8 +399,8 @@
         charge_of = (lower.at[3], upper.at[3])
         kept_q[0][...] = lower[3]
         kept_q[1][...] = upper[3]
-    lax.fori_loop(0, 16, ghost_block(lower, charge_of[0], TILES), 0)
-    lax.fori_loop(0, 16, ghost_block(upper, charge_of[1], TILES + 128), 0)
+    lax.fori_loop(0, 16 // many_rows, ghost_block(lower, charge_of[0], TILES), 0)
+    lax.fori_loop(0, 16 // many_rows, ghost_block(upper, charge_of[1], TILES + 128), 0)
 
     def contract(a, b, left, right):
         return lax.dot_general(a, b, (((left,), (right,)), ((), ())), preferred_element_type=f32)
@@ -473,7 +482,7 @@
                     part = part + weight * placed
             return part
 
-        return lax.fori_loop(0, TILES // 8, block, jnp.zeros((8, LANES), f32))
+        return lax.fori_loop(0, TILES // 8, block, jnp.zeros((8, LANES), f32), unroll=4)
 
     ending = combine((2,) if last else (0, 1, 2))
     if last:
@@ -513,9 +522,9 @@
         in_specs=[SMEM] * 4 + [pl.BlockSpec(memory_space=pl.ANY)] * 4 + [VMEM] * (3 + len(kept_q)),
         out_specs=(VMEM, VMEM, SMEM if last else VMEM) + (VMEM,) * len(kept),
         scratch_shapes=[
-            pltpu.VMEM((8 * 16, LANES), f32),
-            pltpu.VMEM((8 * 48, LANES), f32),
-            pltpu.VMEM((8 * 16, LANES), f32),
+            pltpu.VMEM((ROW_SETS * 8 * 16, LANES), f32),
+            pltpu.VMEM((ROW_SETS * 8 * 48, LANES), f32),
+            pltpu.VMEM((ROW_SETS * 8 * 16, LANES), f32),
             pltpu.VMEM((TILES + 256, 16, LANES), bf16),
             pltpu.VMEM((TILES, 48, LANES), bf16),
             pltpu.VMEM((TILES + 256, 16, LANES), bf16),

time: 133 us -> 128 us (0.962)
  Pallas kernels: 116 us -> 112 us
    pallas_call x2, Pallas kernels: 80.2 us -> 75.7 us  [step(): pl.pallas_call(kernel, out_shape=(whole, whole, jax.ShapeDtypeStruct((1,)...]
where the time goes in v10:
time: 128 us
  Pallas kernels  112 us (88%)
  starting transfers between devices  4.68 us (4%)
  between operations  4.44 us (3%)
  waiting for transfers between devices  3.62 us (3%)
  local copies, waits for them, and re-layouts  3.34 us (3%)
    pallas_call x2, Pallas kernels, step(): pl.pallas_call(kernel, out_shape=(whole, whole, jax.ShapeDtypeStruct((1,)...  75.7 us
    pallas_call x1, Pallas kernels, first_gather(): pl.pallas_call(first_gather_kernel, out_shape=(jax.ShapeDtypeStruct((3, T...  14.3 us
    pallas_call x1, Pallas kernels, second_gather(): pl.pallas_call(second_gather_kernel, out_shape=jax.ShapeDtypeStruct((3, G...  11.2 us
    pallas_call x1, Pallas kernels, plan(): pl.pallas_call(plan_kernel, out_shape=(jax.ShapeDtypeStruct((GROUPS * 32,...  10.7 us
    ppermute x2, starting transfers between devices, shifted(): return lax.ppermute(shard, axis, pairs)  4.68 us
    ppermute x2, waiting for transfers between devices, shifted(): return lax.ppermute(shard, axis, pairs)  3.62 us
    unnamed x16, local copies, waits for them, and re-layouts  3.34 us
  transfers between devices with their start and end apart: 2, of which 2 were waited for; matrix products, arithmetic and copies ran while one was open for 0% of the time, Pallas kernels for 8%

profile of v10, /device:TPU:96, one launch (start us, length us, event | category | flops | bytes accessed | tf_op | source)
XLA Modules:
  0.0 128.0 jit_solution(7500917564951452428)
XLA Ops:
  0.6 2.8 %collective-permute-start.1 = (f32[3,512,128]{2,1,0:T(8,128)}, f32[3,512,128]{2,1,0:T(8,128)S(1)}, u32[]{:S(2)}, u32[]{:S(2)}) collective-permute-start(f32[3,512,128]{2,1,0:T(8,128)} %bitcast.26), channel_id=1, source_target_pairs={{8,0},{16,8},{24,16},{32,24},{40,32},{48,40},{56,48},{64,56},{72,6... | collective-permute-start | bytes 2359304 | tf_op jit(solution)/shard_map/ppermute | solution.py:578
  3.4 1.9 %collective-permute-start = (f32[3,512,128]{2,1,0:T(8,128)}, f32[3,512,128]{2,1,0:T(8,128)S(1)}, u32[]{:S(2)}, u32[]{:S(2)}) collective-permute-start(f32[3,512,128]{2,1,0:T(8,128)} %bitcast.27), channel_id=1, source_target_pairs={{0,8},{8,16},{16,24},{24,32},{32,40},{40,48},{48,56},{56,64},{64,7... | collective-permute-start | bytes 2359304 | tf_op jit(solution)/shard_map/ppermute | solution.py:578
  7.3 0.0 copy-start.6
  7.3 0.9 copy-done.6
  8.2 0.0 copy-start
  8.2 0.0 copy-start.1
  8.2 10.7 %plan.1 = (s32[512,128]{1,0:T(8,128)S(1)}, s32[256,128]{1,0:T(8,128)S(1)}, s32[40,128]{1,0:T(8,128)S(1)}) custom-call(s32[256,128]{1,0:T(8,128)S(1)} %bitcast.29), custom_call_target="tpu_custom_call" | custom-call | flops 10000000000 | bytes 40000000 | tf_op jit(solution)/shard_map/plan/pallas_call | solution.py:100
  18.9 0.6 collective-permute-done.1.above
  19.5 3.1 %collective-permute-done.below = f32[3,512,128]{2,1,0:T(8,128)S(1)} collective-permute-done((f32[3,512,128]{2,1,0:T(8,128)}, f32[3,512,128]{2,1,0:T(8,128)S(1)}, u32[]{:S(2)}, u32[]{:S(2)}) %collective-permute-start) | collective-permute-done | bytes 786464 | tf_op jit(solution)/shard_map/ppermute | solution.py:578
  22.6 0.0 copy-done
  22.6 0.0 copy-done.1
  22.6 0.0 copy-done.5
  22.6 0.0 copy-start.2
  22.6 0.0 copy-start.3
  22.6 14.3 %first_gather.1 = (f32[3,512,128]{2,1,0:T(8,128)S(1)}, f32[4,256,128]{2,1,0:T(8,128)S(1)}, f32[8,128]{1,0:T(8,128)S(1)}) custom-call(s32[1]{0:T(128)S(6)} %copy.22.partner.refs_2_, s32[40,128]{1,0:T(8,128)S(1)} %get-tuple-element.17.cells, f32[3,512,128]{2,1,0:T(8,128)S(1)} %bitcast.28, f32[3,512,128]{2,1,0:T(8,128)S(1)} %collective-permute-done.below, ...), custom_call_target="tpu_custom_call" | custom-call | flops 10000000000 | bytes 40000000 | tf_op jit(solution)/shard_map/first_gather/pallas_call | solution.py:241
  36.9 0.0 copy-start.4
  36.9 0.0 copy-done.2
  36.9 0.0 copy-done.3
  36.9 0.7 copy-done.4
  37.6 37.4 %step.2 = (f32[3,512,128]{2,1,0:T(8,128)S(1)}, f32[3,512,128]{2,1,0:T(8,128)S(1)}, f32[8,128]{1,0:T(8,128)S(1)}, f32[128,128]{1,0:T(8,128)S(1)}, f32[128,128]{1,0:T(8,128)S(1)}) custom-call(f32[1]{0:T(128)S(6)} %copy.24.refs_0_, f32[1]{0:T(128)S(6)} %copy.23.refs_1_, s32[1]{0:T(128)S(6)} %copy.22.partner.refs_2_, s32[2,512]{1,0:T(2,128)S(1)} %bitcast.24, ...), custom_call_target="tpu_custom_call" | custom-call | tf_op jit(solution)/shard_map/step/pallas_call | solution.py:519
  75.0 11.2 %second_gather.1.refs_4_ = f32[3,256,128]{2,1,0:T(8,128)S(1)} custom-call(s32[40,128]{1,0:T(8,128)S(1)} %get-tuple-element.17.cells, f32[3,512,128]{2,1,0:T(8,128)S(1)} %get-tuple-element.23.refs_0_.refs_9_, s32[512,128]{1,0:T(8,128)S(1)} %get-tuple-element.18.source.refs_1_, s32[256,128]{1,0:T(8,128)S(1)} %get-tuple-element.19.place.refs_2_), custom_call_target="tpu_custom_call" | custom-call | flops 10000000000 | bytes 40000000 | tf_op jit(solution)/shard_map/second_gather/pallas_call | solution.py:563
  86.2 38.2 %step.3 = (f32[3,512,128]{2,1,0:T(8,128)S(1)}, f32[3,512,128]{2,1,0:T(8,128)S(1)}, f32[1]{0:T(128)}) custom-call(f32[1]{0:T(128)S(6)} %copy.24.refs_0_, f32[1]{0:T(128)S(6)} %copy.23.refs_1_, s32[1]{0:T(128)S(6)} %copy.22.partner.refs_2_, s32[2,512]{1,0:T(2,128)S(1)} %bitcast.25, f32[3,256,128]{2,1,0:T(8,128)S(1)} %second_gather.1.refs_4_, ...), custom_call_target="tpu_custom_call" | custom-call | tf_op jit(solution)/shard_map/step/pallas_call | solution.py:519
  124.5 0.9 copy.25
  125.3 0.9 copy.26
  (1 shorter events, 0.0 us)
Async XLA Ops:
  0.6 18.9 %collective-permute-start.1 = (f32[3,512,128]{2,1,0:T(8,128)}, f32[3,512,128]{2,1,0:T(8,128)S(1)}, u32[]{:S(2)}, u32[]{:S(2)}) collective-permute-start(f32[3,512,128]{2,1,0:T(8,128)} %bitcast.26), channel_id=1, source_target_pairs={{8,0},{16,8},{24,16},{32,24},{40,32},{48,40},{56,48},{64,56},{72,6... | collective-permute-start | bytes 2359304 | tf_op jit(solution)/shard_map/ppermute | solution.py:578
  3.4 19.2 %collective-permute-start = (f32[3,512,128]{2,1,0:T(8,128)}, f32[3,512,128]{2,1,0:T(8,128)S(1)}, u32[]{:S(2)}, u32[]{:S(2)}) collective-permute-start(f32[3,512,128]{2,1,0:T(8,128)} %bitcast.27), channel_id=1, source_target_pairs={{0,8},{8,16},{16,24},{24,32},{32,40},{40,48},{48,56},{56,64},{64,7... | collective-permute-start | bytes 2359304 | tf_op jit(solution)/shard_map/ppermute | solution.py:578
  7.3 0.9 copy-start.6
  8.2 14.4 %copy-start = (f32[65536]{0:T(1024)S(1)}, f32[65536]{0:T(1024)}, u32[]{:S(2)}) copy-start(f32[65536]{0:T(1024)} %param.12) | copy-start | bytes 786436
  8.2 14.4 %copy-start.1 = (f32[65536]{0:T(1024)S(1)}, f32[65536]{0:T(1024)}, u32[]{:S(2)}) copy-start(f32[65536]{0:T(1024)} %param.14) | copy-start | bytes 786436
  8.2 14.4 %copy-start.5 = (f32[1,3,65536]{2,0,1:T(1,128)S(1)}, f32[1,3,65536]{2,0,1:T(1,128)}, u32[]{:S(2)}) copy-start(f32[1,3,65536]{2,0,1:T(1,128)} %param.10) | copy-start | bytes 2359300
  22.6 14.3 %copy-start.2 = (f32[65536]{0:T(1024)S(1)}, f32[65536]{0:T(1024)}, u32[]{:S(2)}) copy-start(f32[65536]{0:T(1024)} %param.13) | copy-start | bytes 786436
  22.6 14.3 %copy-start.3 = (f32[1,3,65536]{2,0,1:T(1,128)S(1)}, f32[1,3,65536]{2,0,1:T(1,128)}, u32[]{:S(2)}) copy-start(f32[1,3,65536]{2,0,1:T(1,128)} %param.11) | copy-start | bytes 2359300
  36.9 0.7 copy-start.4
